TPU v7x, 256 devices: a whole 4x4x8 slice. The times are simulated.
256 devices in a mesh: ctx: 16 (over y_hi, x, core), fsdp: 16 (over y_lo, z).
Axes of the slice: x: 4, y: 4 (y_hi: 2, y_lo: 2; y = y_hi * 2 + y_lo), z: 8, core: 2. Of those that a mesh axis runs over, the one named last changes fastest.
Arguments:
- queries: bfloat16 [16, 256, 2048], P('fsdp', 'ctx'), may hold values from -8 to 8
- grad_out: bfloat16 [16, 256, 2048], P('fsdp', 'ctx'), may hold values from -384 to 384
- keys: bfloat16 [16, 4096, 2048], P('fsdp', 'ctx'), may hold values from -8 to 8
- context: bfloat16 [16, 4096, 2048], P('fsdp', 'ctx'), may hold values from -6 to 6
- value_weight: bfloat16 [2048, 2048], P('fsdp'), may hold values from -0.125 to 0.125
- plan: int32 [16, 2, 2], P('fsdp'), may hold values from 0 to 12, as said below
- lengths: int32 [16, 2], P('fsdp'), may hold values from 128 to 3072, as said below
- blocks: int32 [16, 64], P('fsdp', 'ctx'), may hold values from -1 to 47, as said below
Outputs:
- query_grad: bfloat16 [16, 256, 2048], P('fsdp', 'ctx')
- key_grad: bfloat16 [16, 4096, 2048], P('fsdp', 'ctx')
- context_grad: bfloat16 [16, 4096, 2048], P('fsdp', 'ctx')
- weight_grad: float32 [2048, 2048], P(('ctx', 'fsdp'))
Inputs may be any that keep to these rules, and one draw needn't show every extreme that they name: plan[f, 0, e] is the first context index of episode e's group and plan[f, 1, e] its width; the groups of a replica are contiguous, in order, and cover all 16 indices; every width is 4 or more. `lengths`: an episode's length is at most 256 times its group's width; in every replica the episode of the wider group has exactly that length. Each slot of 64 keys holds -1 if it is empty, else the number b of the block of its group's episode that it holds, keys b * 64 to b * 64 + 63 of the episode; the blocks 0 to ceil(length / 64) - 1 of each episode are held exactly once, by slots of its group, and its group's other slots are -1.
All inputs are finite; a program needn't handle non-finite values.
Results may differ from a plain program's by a relative error of at most 0.034.
Values may be sent and summed in bfloat16 or wider, within the bound.
No kernel may reach another device: no remote copies, remote signals or barrier semaphores. Data moves between devices by JAX's collectives and lax.ppermute only.
A program may use at most 128 MiB of HBM per device.

v0:
```python
import functools
import math

import jax
import jax.numpy as jnp
from jax import lax
from jax.sharding import PartitionSpec as P

HD = 128
QC = 128


neg_large = -1e30


def on_device(queries, grad_out, keys, context, value_weight, plan, lengths, blocks):
    ctx_count = lax.axis_size("ctx")
    my_index = lax.axis_index("ctx")
    slot_count = blocks.shape[1]
    kv_rows = keys.shape[1]
    block_len = kv_rows // slot_count
    width_heads = keys.shape[2]
    head_count = width_heads // HD
    query_rows = queries.shape[1] * ctx_count
    episodes = plan.shape[2]
    score_scale = 1.0 / math.sqrt(HD)
    weight = lax.all_gather(value_weight, "fsdp", axis=0, tiled=True)
    values = jnp.dot(context[0], weight, preferred_element_type=jnp.float32).astype(jnp.bfloat16)
    starts = plan[0, 0]
    widths = plan[0, 1]
    numbers = jnp.arange(episodes, dtype=jnp.int32)
    inside = (my_index >= starts) & (my_index < starts + widths)
    episode = jnp.sum(jnp.where(inside, numbers, 0))
    own_length = jnp.sum(jnp.where(numbers == episode, lengths[0], 0))
    query_all, grad_all = (
        lax.all_gather(queries, "ctx", axis=1, tiled=True),
        lax.all_gather(grad_out, "ctx", axis=1, tiled=True),
    )
    q_own = lax.dynamic_slice_in_dim(query_all[0], episode * QC, QC, 0).reshape(QC, head_count, HD)
    g_own = lax.dynamic_slice_in_dim(grad_all[0], episode * QC, QC, 0).reshape(QC, head_count, HD)
    q_pos = own_length - QC + jnp.arange(QC, dtype=jnp.int32)
    key_blocks = keys[0].reshape(slot_count, block_len, head_count, HD)
    value_blocks = values.reshape(slot_count, block_len, head_count, HD)
    k_pos = blocks[0][:, None] * block_len + jnp.arange(block_len, dtype=jnp.int32)[None, :]
    live_key = (blocks[0][:, None] >= 0) & (k_pos < own_length)
    allowed = live_key[:, :, None] & (k_pos[:, :, None] <= q_pos[None, None, :])
    visible = allowed[:, None, :, :]

    def block_terms(slot_id):
        key_rows = key_blocks[slot_id]
        value_rows = value_blocks[slot_id]
        block_scores = (
            jnp.einsum("khd,qhd->hkq", key_rows, q_own, preferred_element_type=jnp.float32)
            * score_scale
        )
        block_prods = jnp.einsum(
            "khd,qhd->hkq", value_rows, g_own, preferred_element_type=jnp.float32
        )
        return (block_scores, block_prods)

    blank_block = jnp.zeros((head_count, block_len, QC), jnp.float32)

    def skipped():
        return (blank_block, blank_block)

    score_list = []
    prod_list = []
    for slot_id in range(slot_count):
        block_scores, block_prods = lax.cond(
            blocks[0, slot_id] >= 0, functools.partial(block_terms, slot_id), skipped
        )
        score_list.append(block_scores)
        prod_list.append(block_prods)
    scores = jnp.stack(score_list)
    prods = jnp.stack(prod_list)
    masked = jnp.where(visible, scores, neg_large)
    local_max = jnp.max(masked, axis=(0, 2))
    column_episode = jnp.arange(query_rows, dtype=jnp.int32) // QC
    own_column = (column_episode == episode)[None, :]

    def spread(piece, filler):
        return jnp.where(own_column, jnp.tile(piece, (1, episodes)), filler)

    def own_rows(whole):
        return lax.dynamic_slice_in_dim(whole, episode * QC, QC, 1)

    row_max = own_rows(lax.pmax(spread(local_max, neg_large), "ctx"))
    unscaled = jnp.where(visible, jnp.exp(scores - row_max[None, :, None, :]), 0.0)
    local_sum = jnp.sum(unscaled, axis=(0, 2))
    local_cross = jnp.sum(unscaled * prods, axis=(0, 2))
    summed, crossed = lax.psum((spread(local_sum, 0.0), spread(local_cross, 0.0)), "ctx")
    row_sum = own_rows(summed)
    row_cross = own_rows(crossed)
    probabilities = unscaled / row_sum[None, :, None, :]
    row_delta = row_cross / row_sum
    dscore = probabilities * (prods - row_delta[None, :, None, :])
    probs_b = probabilities.astype(jnp.bfloat16)
    dscore_b = dscore.astype(jnp.bfloat16)
    value_grad = (
        jnp.einsum("shkq,qhd->skhd", probs_b, g_own, preferred_element_type=jnp.float32)
        .reshape(kv_rows, width_heads)
        .astype(jnp.bfloat16)
    )
    key_grad = (
        (
            score_scale
            * jnp.einsum("shkq,qhd->skhd", dscore_b, q_own, preferred_element_type=jnp.float32)
        )
        .reshape(kv_rows, width_heads)
        .astype(jnp.bfloat16)
    )
    query_part = (
        score_scale
        * jnp.einsum("shkq,skhd->qhd", dscore_b, key_blocks, preferred_element_type=jnp.float32)
    ).reshape(QC, width_heads)
    query_terms = jnp.zeros((query_rows, width_heads), jnp.float32)
    query_terms = lax.dynamic_update_slice_in_dim(query_terms, query_part, episode * QC, 0)
    query_grad = lax.psum_scatter(query_terms[None], "ctx", scatter_dimension=1, tiled=True).astype(
        jnp.bfloat16
    )
    context_grad = lax.dot_general(
        value_grad, weight, (((1,), (1,)), ((), ())), preferred_element_type=jnp.float32
    ).astype(jnp.bfloat16)
    partial_grad = lax.dot_general(
        context[0], value_grad, (((0,), (0,)), ((), ())), preferred_element_type=jnp.float32
    )
    weight_grad = lax.psum_scatter(partial_grad, ("ctx", "fsdp"), scatter_dimension=0, tiled=True)
    return (query_grad, key_grad[None], context_grad[None], weight_grad)


def solution(mesh):
    in_specs = (
        P("fsdp", "ctx", None),
        P("fsdp", "ctx", None),
        P("fsdp", "ctx", None),
        P("fsdp", "ctx", None),
        P("fsdp", None),
        P("fsdp", None, None),
        P("fsdp", None),
        P("fsdp", "ctx"),
    )
    out_specs = (
        P("fsdp", "ctx", None),
        P("fsdp", "ctx", None),
        P("fsdp", "ctx", None),
        P(("ctx", "fsdp"), None),
    )
    return jax.shard_map(
        on_device, mesh=mesh, in_specs=in_specs, out_specs=out_specs, check_vma=False
    )
```

profile of v0, /device:TPU:1, one launch (start us, length us, event | category | flops | bytes accessed | tf_op | source)
XLA Modules:
  0.0 1735.4 jit_solution(15548240276793919064)
XLA Ops:
  9.5 1.5 fusion.23
  15.6 1.5 copy.95
  20.8 44.4 %all-gather.4.cloned.1.call-done = bf16[1,256,2048]{2,1,0:T(8,128)(2,1)} async-done(((bf16[1,16,2048]{2,1,0:T(8,128)(2,1)}), bf16[1,256,2048]{2,1,0:T(8,128)(2,1)}) %all-gather.4.cloned.1.call-update) | async-done | bytes 1048592 | tf_op jit(solution)/shard_map/all_gather | solution.py:36
  65.2 51.7 %all-gather.8.cloned.1.call-done = bf16[1,256,2048]{2,1,0:T(8,128)(2,1)} async-done(((bf16[1,16,2048]{2,1,0:T(8,128)(2,1)}), bf16[1,256,2048]{2,1,0:T(8,128)(2,1)}) %all-gather.8.cloned.1.call-update) | async-done | bytes 1048592 | tf_op jit(solution)/shard_map/all_gather | solution.py:37
  120.2 98.0 %all-gather.6.cloned.1.call-done = bf16[2048,2048]{1,0:T(8,128)(2,1)} async-done(((bf16[128,2048]{1,0:T(8,128)(2,1)}), bf16[2048,2048]{1,0:T(8,128)(2,1)}) %all-gather.6.cloned.1.call-update) | async-done | bytes 8388624 | tf_op jit(solution)/shard_map/all_gather | solution.py:27
  218.1 5.7 fusion.6
  227.2 2.4 conditional.7
  230.5 2.4 conditional.6
  233.8 2.4 conditional.5
  237.1 2.0 constant_dynamic-update-slice_fusion.1
  239.9 1.8 select_reduce_fusion
  241.8 63.9 %pmax.7 = f32[16,256]{1,0:T(8,128)S(1)} all-reduce(f32[16,256]{1,0:T(8,128)S(1)} %bitcast_select_fusion.2), channel_id=1, replica_groups=mesh['ctx'=16,'fsdp'=16] {'ctx'}, use_global_device_ids=true, to_apply=%region_11.12 | all-reduce | flops 4096 | bytes 32768 | tf_op jit(solution)/shard_map/pmax | solution.py:87
  309.0 65.0 %all-reduce = (f32[16,256]{1,0:T(8,128)S(1)}, f32[16,256]{1,0:T(8,128)S(1)}) all-reduce(f32[16,256]{1,0:T(8,128)S(1)} %get-tuple-element.145, f32[16,256]{1,0:T(8,128)S(1)} %get-tuple-element.144), channel_id=1, replica_groups=mesh['ctx'=16,'fsdp'=16] {'ctx'}, use_global_device_ids=true, to_apply=%region_15.16 | all-reduce | flops 8192 | bytes 65536 | tf_op jit(solution)/shard_map/psum | solution.py:91
  373.9 4.0 fusion.20
  377.9 1.5 fusion.10
  379.4 2.5 copy.69
  382.0 1.6 broadcast_in_dim.68
  384.9 1.7 fusion.7
  387.3 8.1 convolution_bitcast_fusion.4
  395.4 17.9 %copy.91 = f32[2048,2048]{1,0:T(8,128)} copy(f32[2048,2048]{0,1:T(8,128)} %convolution_bitcast_fusion.4) | data formatting | bytes 33554432
  416.7 6.8 fusion.4
  423.5 37.1 %reduce-scatter.5.cloned.1.call-done = f32[1,16,2048]{2,1,0:T(8,128)} async-done(((f32[1,256,2048]{2,1,0:T(8,128)}), f32[1,16,2048]{2,1,0:T(8,128)}) %reduce-scatter.5.cloned.1.call-update) | async-done | bytes 131088 | tf_op jit(solution)/shard_map/reduce_scatter | solution.py:118
  460.6 1.5 convert_element_type.76
  462.2 1266.7 %reduce-scatter.7.cloned.1.call-done = f32[8,2048]{1,0:T(8,128)} async-done(((f32[2048,2048]{1,0:T(8,128)}), f32[8,2048]{1,0:T(8,128)}) %reduce-scatter.7.cloned.1.call-update) | async-done | bytes 65552
  (114 shorter events, 33.5 us)
Async XLA Ops:
  7.2 211.0 %copy-start = (bf16[1,256,2048]{2,1,0:T(8,128)(2,1)S(1)}, bf16[1,256,2048]{2,1,0:T(8,128)(2,1)}, u32[]{:S(2)}) copy-start(bf16[1,256,2048]{2,1,0:T(8,128)(2,1)} %param.19) | copy-start | bytes 3145732
  7.2 12.6 copy-start.25
  7.2 9.9 copy-start.26
  7.2 57.9 %all-gather.4.cloned.1.call-start = ((), (), s32[]{:S(2)}) async-start(), calls=%async_computation.2 | async-start | bytes 1114112 | tf_op jit(solution)/shard_map/all_gather | solution.py:36
  7.9 108.9 %all-gather.8.cloned.1.call-start = ((), (), s32[]{:S(2)}) async-start(), calls=%async_computation.4 | async-start | bytes 1114112 | tf_op jit(solution)/shard_map/all_gather | solution.py:37
  8.7 209.4 %all-gather.6.cloned.1.call-start = ((), (), s32[]{:S(2)}) async-start(), calls=%async_computation.3 | async-start | bytes 8912896 | tf_op jit(solution)/shard_map/all_gather | solution.py:27
  9.4 451.2 %reduce-scatter.5.cloned.1.call-start = ((), (), s32[]{:S(2)}) async-start(), calls=%async_computation.5 | async-start | bytes 2228224 | tf_op jit(solution)/shard_map/reduce_scatter | solution.py:118
  223.9 1.0 copy-start.3
  223.9 1.2 copy-start.8
  227.2 1.0 copy-start.10
  228.2 1.0 copy-start.5
  230.5 1.0 copy-start.11
  231.5 1.0 copy-start.6
  234.8 1.0 copy-start.7
  236.2 2.9 copy-start.20
  237.1 68.6 %copy-start.16 = (f32[1,16,64,128]{3,2,1,0:T(8,128)S(1)}, f32[1,16,64,128]{3,2,1,0:T(8,128)}, u32[]{:S(2)}) copy-start(f32[1,16,64,128]{3,2,1,0:T(8,128)} %copy-done.15) | copy-start | bytes 1572868
  241.8 65.3 %copy-start.18 = (f32[1,16,64,128]{3,2,1,0:T(8,128)S(1)}, f32[1,16,64,128]{3,2,1,0:T(8,128)}, u32[]{:S(2)}) copy-start(f32[1,16,64,128]{3,2,1,0:T(8,128)} %copy-done.17) | copy-start | bytes 1572868
  305.7 1.3 copy-start.22
  305.7 1.9 copy-start.2
  307.6 1.3 copy-start.13
  382.0 1.6 copy-start.14
  383.6 1.3 copy-start.9
  384.7 1344.2 %reduce-scatter.7.cloned.1.call-start = ((), (), s32[]{:S(2)}) async-start(), calls=%async_computation.6 | async-start | bytes 16842752
  416.7 1312.2 %copy-start.1 = (bf16[1,256,2048]{2,1,0:T(8,128)(2,1)S(1)}, bf16[1,256,2048]{2,1,0:T(8,128)(2,1)}, u32[]{:S(2)}) copy-start(bf16[1,256,2048]{2,1,0:T(8,128)(2,1)} %param.19) | copy-start | bytes 3145732
  (8 other events, 7.6 us)
Sparse Core Ops, SparseCore 0:
  10.8 54.3 all-gather.3
  67.9 48.9 all-gather.7
  118.7 99.4 all-gather.5
  384.8 75.7 reduce-scatter.4
  463.6 1265.2 reduce-scatter.6
where the time goes:
time: 1770 us; the launch traced here: 1740 us
  waiting for transfers between devices  1500 us (85%)
  blocking collectives  129 us (7%)
  local copies, waits for them, and re-layouts  49.3 us (3%)
  matrix products  26.4 us (1%)
  between operations  18.1 us (1%)
    unnamed x6, waiting for transfers between devices  1270 us
    all_gather x1, waiting for transfers between devices, on_device(): weight = lax.all_gather(value_weight, 'fsdp', axis=0, tiled=True)  98 us
    psum x1, blocking collectives, on_device(): lax.psum((spread(local_sum, 0.0), spread(local_cross, 0.0)), 'ctx')  65 us
    pmax x1, blocking collectives, on_device(): row_max = own_rows(lax.pmax(spread(local_max, neg_large), 'ctx'))  63.9 us
    all_gather x1, waiting for transfers between devices, on_device(): lax.all_gather(grad_out, 'ctx', axis=1, tiled=True)  51.7 us
    all_gather x1, waiting for transfers between devices, on_device(): lax.all_gather(queries, 'ctx', axis=1, tiled=True)  44.4 us
    reduce_scatter x1, waiting for transfers between devices, on_device(): lax.psum_scatter(query_terms[None], 'ctx', scatter_dimension=1, tiled=True)  37.1 us
  transfers between devices with their start and end apart: 5, of which 5 were waited for; matrix products, arithmetic and copies ran while one was open for 3% of the time, Pallas kernels for 0%

commit v1 on v0

v1 whole, which is shorter than its diff:
```python
import functools
import math

import jax
import jax.numpy as jnp
from jax import lax
from jax.experimental import pallas as pl
from jax.experimental.pallas import tpu as pltpu
from jax.sharding import Mesh, PartitionSpec as P

HD = 128
QC = 128
HEADS = 16
BLK = 64
TOK = 256
WIDTH = 2048
SCALE = 1.0 / math.sqrt(HD)
NEG = -1e30
BF = jnp.bfloat16
F32 = jnp.float32
CTX = ("yh", "x", "k")
AXES = ("yh", "x", "k", "yl", "z")
VMEM = pl.BlockSpec(memory_space=pltpu.VMEM)
SMEM = pl.BlockSpec(memory_space=pltpu.SMEM)

I_X, I_K, I_YH, I_EP, I_S0, I_W0, I_S1, I_W1, I_LEN, I_BLK = range(10)


def params(megabytes):
    return pltpu.CompilerParams(vmem_limit_bytes=megabytes << 20)


def cost(flops, size):
    return pl.CostEstimate(flops=flops, bytes_accessed=size, transcendentals=0)


def dot(a, b, ca, cb):
    return lax.dot_general(a, b, (((ca,), (cb,)), ((), ())), preferred_element_type=F32)


def shift(a, axis, by):
    n = lax.axis_size(axis)
    return lax.ppermute(a, axis, [(i, (i + by) % n) for i in range(n)])


def own_rows(qg_ref, which, episode, dst):
    for i in range(8):
        dst[i * 16 : (i + 1) * 16, :] = qg_ref[8 * episode + i, which]


def scores_kernel(info, qg_ref, k_ref, p0, p1, p2, p3, st_ref, q_buf):
    episode = info[I_EP]
    own_rows(qg_ref, 0, episode, q_buf)
    length = info[I_LEN]
    row = lax.broadcasted_iota(jnp.int32, (BLK, QC), 0)
    col = lax.broadcasted_iota(jnp.int32, (BLK, QC), 1)
    limit = jnp.minimum(length - QC + col, length - 1)
    masks = []
    for slot in range(TOK // BLK):
        b = info[I_BLK + slot]
        pos = b * BLK + row
        masks.append((pos <= limit) & (b >= 0))
    visible = jnp.concatenate(masks, axis=0)
    for s, out in enumerate((p0, p1, p2, p3)):
        block = lax.rem(info[I_X] + s, 4)
        for hh in range(4):
            cols = pl.ds(pl.multiple_of(block * 512 + hh * HD, HD), HD)
            sc = dot(k_ref[:, cols], q_buf[:, cols], 1, 1) * SCALE
            masked = jnp.where(visible, sc, NEG)
            top = jnp.max(masked, axis=0, keepdims=True)
            p = jnp.where(visible, jnp.exp(masked - top), 0.0)
            st_ref[0, block, hh : hh + 1, :] = top
            st_ref[1, block, hh : hh + 1, :] = jnp.sum(p, axis=0, keepdims=True)
            out[:, hh * HD : (hh + 1) * HD] = p.astype(BF)


def member(info, ctx_index, e):
    start = info[I_S0 + 2 * e]
    return (ctx_index >= start) & (ctx_index < start + info[I_W0 + 2 * e])


def totals(info, st_ref, e, block):
    top = jnp.full((4, QC), NEG, F32)
    for c in range(16):
        top = jnp.maximum(top, jnp.where(member(info, c, e), st_ref[c, 0, block], NEG))
    total = jnp.zeros((4, QC), F32)
    for c in range(16):
        part = st_ref[c, 1, block] * jnp.exp(st_ref[c, 0, block] - top)
        total = total + jnp.where(member(info, c, e), part, 0.0)
    return top, 1.0 / total


def block_kernel(info, st_ref, qg_ref, *refs):
    p_refs, c_refs = refs[:8], refs[8:16]
    out_ref, g_buf, vg_buf = refs[16:]
    xi = info[I_X]
    cols = pl.ds(pl.multiple_of(xi * 512, 512), 512)
    tops, invs = [], []
    for e in range(2):
        for i in range(8):
            g_buf[e, i * 16 : (i + 1) * 16, :] = qg_ref[8 * e + i, 1, :, cols]
        top, inv = totals(info, st_ref, e, xi)
        tops.append(top)
        invs.append(inv)
    for n in range(8):
        src_x = lax.rem(xi + 4 - n // 2, 4)
        src_k = info[I_K] if n % 2 == 0 else 1 - info[I_K]
        c = info[I_YH] * 8 + src_x * 2 + src_k
        in_one = member(info, c, 1)
        top = jnp.where(in_one, tops[1], tops[0])
        inv = jnp.where(in_one, invs[1], invs[0])
        factor = jnp.exp(st_ref[c, 0, xi] - top) * inv
        e = in_one.astype(jnp.int32)
        for hh in range(4):
            hs = slice(hh * HD, (hh + 1) * HD)
            pr = (p_refs[n][:, hs].astype(F32) * factor[hh : hh + 1, :]).astype(BF)
            vg_buf[n * TOK : (n + 1) * TOK, hs] = dot(pr, g_buf[e, :, hs], 1, 0).astype(BF)
    for tile in range(4):
        acc = jnp.zeros((256, 512), F32)
        for n in range(8):
            acc = acc + dot(
                c_refs[n][:, tile * 256 : (tile + 1) * 256],
                vg_buf[n * TOK : (n + 1) * TOK, :],
                0,
                0,
            )
        for part in range(4):
            r = tile * 256 + part * 64
            yh, xx, yl = r // 512, (r // 128) % 4, (r // 64) % 2
            out_ref[yh * 2 + yl, xx] = acc[part * 64 : (part + 1) * 64].astype(BF)


def values_kernel(
    info, st_ref, qg_ref, ctx_ref, wa, wb, p0, p1, p2, p3,
    prod_ref, probs_ref, cross_ref, cg_ref, g_buf, v_buf, vg_buf,
):
    episode = info[I_EP]
    xi = info[I_X]
    ki = info[I_K]
    own_rows(qg_ref, 1, episode, g_buf)
    col_a = pl.ds(pl.multiple_of(ki * 1024, 1024), 1024)
    col_b = pl.ds(pl.multiple_of((1 - ki) * 1024, 1024), 1024)
    ca, cb = ctx_ref[:, col_a], ctx_ref[:, col_b]
    for t in range(4):
        ts = slice(t * 512, (t + 1) * 512)
        v_buf[:, ts] = (dot(ca, wa[:, ts], 1, 0) + dot(cb, wb[:, ts], 1, 0)).astype(BF)
    me = info[I_YH] * 8 + xi * 2 + ki
    for s, p_ref in enumerate((p0, p1, p2, p3)):
        block = lax.rem(xi + s, 4)
        top, inv = totals(info, st_ref, episode, block)
        factor = jnp.exp(st_ref[me, 0, block] - top) * inv
        for hh in range(4):
            cols = pl.ds(pl.multiple_of(block * 512 + hh * HD, HD), HD)
            pr = p_ref[:, hh * HD : (hh + 1) * HD].astype(F32) * factor[hh : hh + 1, :]
            prod = dot(v_buf[:, cols], g_buf[:, cols], 1, 1)
            prod_ref[:, cols] = prod
            probs_ref[:, cols] = pr
            cross_ref[block, hh : hh + 1, :] = jnp.sum(pr * prod, axis=0, keepdims=True)
            vg_buf[:, cols] = dot(pr.astype(BF), g_buf[:, cols], 1, 0).astype(BF)
    vg = vg_buf[...]
    for w_ref, base in ((wa, ki * 1024), (wb, (1 - ki) * 1024)):
        for t in range(2):
            dst = pl.ds(pl.multiple_of(base + t * 512, 512), 512)
            cg_ref[:, dst] = dot(vg, w_ref[t * 512 : (t + 1) * 512, :], 1, 1).astype(BF)


def grads_kernel(info, cross_ref, qg_ref, k_ref, prod_ref, probs_ref, kg_ref, qp_ref, q_buf):
    episode = info[I_EP]
    own_rows(qg_ref, 0, episode, q_buf)
    for i in range(8):
        qp_ref[1 - episode, i] = jnp.zeros((16, WIDTH), BF)
    for block in range(4):
        delta = jnp.zeros((4, QC), F32)
        for c in range(16):
            delta = delta + jnp.where(member(info, c, episode), cross_ref[c, block], 0.0)
        for hh in range(4):
            hs = slice(block * 512 + hh * HD, block * 512 + (hh + 1) * HD)
            ds = (probs_ref[:, hs] * (prod_ref[:, hs] - delta[hh : hh + 1, :])).astype(BF)
            kg_ref[:, hs] = (SCALE * dot(ds, q_buf[:, hs], 1, 0)).astype(BF)
            part = (SCALE * dot(ds, k_ref[:, hs], 0, 0)).astype(BF)
            for i in range(8):
                qp_ref[episode, i, :, hs] = part[i * 16 : (i + 1) * 16]


def on_device(queries, grad_out, keys, context, value_weight, plan, lengths, blocks):
    yh, xi, ki, yl, zi = (lax.axis_index(a) for a in AXES)
    my_index = yh * 8 + xi * 2 + ki
    keys, context = keys[0], context[0]
    in_one = (my_index >= plan[0, 0, 1]) & (my_index < plan[0, 0, 1] + plan[0, 1, 1])
    episode = in_one.astype(jnp.int32)
    own_length = jnp.where(in_one, lengths[0, 1], lengths[0, 0])
    info = jnp.concatenate([
        jnp.stack([
            xi, ki, yh, episode, plan[0, 0, 0], plan[0, 1, 0], plan[0, 0, 1], plan[0, 1, 1], own_length
        ]).astype(jnp.int32),
        blocks[0],
    ])

    qg = jnp.concatenate([queries, grad_out], axis=0)
    qg_all = lax.all_to_all(jnp.broadcast_to(qg[None], (16,) + qg.shape), CTX, 0, 0)

    w_own = value_weight
    place = lambda y, k: ((y // 2) * 2 + k) * 2 + y % 2
    owners = [(y, k) for y in range(4) for k in range(2) if y % 2 == k]
    around = ("yh", "k", "yl")
    top = lax.ppermute(w_own[:64], around, [(place(y, k), place((y + 1) % 4, k)) for y, k in owners])
    bot = lax.ppermute(w_own[64:], around, [(place(y, k), place((y + 3) % 4, k)) for y, k in owners])
    w_mine = jnp.where(yl == ki, w_own, jnp.concatenate([top, bot], axis=0))
    w_a = lax.all_gather(w_mine, "z", axis=0, tiled=True)
    w_b = shift(w_a, "k", 1)

    cv = context.reshape(TOK, 8, 2, 128)
    c_mine = jnp.where(ki == 0, cv[:, :, 0], cv[:, :, 1]).reshape(TOK, 1024)
    c_oth = jnp.where(ki == 0, cv[:, :, 1], cv[:, :, 0]).reshape(TOK, 1024)
    c_part = shift(c_oth, "k", 1)
    c_m1, c_p1 = shift(c_mine, "x", 1), shift(c_mine, "x", -1)
    d_m1, d_p1 = shift(c_part, "x", 1), shift(c_part, "x", -1)
    c_2 = shift(c_m1, "x", 1)
    d_2 = shift(d_p1, "x", -1)

    sd = jax.ShapeDtypeStruct
    p0, p1, p2, p3, st = pl.pallas_call(
        scores_kernel,
        in_specs=[SMEM, VMEM, VMEM],
        out_specs=[VMEM] * 5,
        out_shape=[sd((TOK, 512), BF)] * 4 + [sd((2, 4, 4, QC), F32)],
        scratch_shapes=[pltpu.VMEM((QC, WIDTH), BF)],
        compiler_params=params(32),
        cost_estimate=cost(134 << 20, 4 << 20),
        name="scores",
    )(info, qg_all, keys)

    p_m1, p_p1, p_2 = shift(p1, "x", 1), shift(p3, "x", -1), shift(p2, "x", 2)
    st_all = lax.all_to_all(jnp.broadcast_to(st[None], (16,) + st.shape), CTX, 0, 0)
    r_0, r_m1, r_p1, r_2 = (shift(a, "k", 1) for a in (p0, p_m1, p_p1, p_2))

    pieces = pl.pallas_call(
        block_kernel,
        in_specs=[SMEM] + [VMEM] * 18,
        out_specs=VMEM,
        out_shape=sd((4, 4, 64, 512), BF),
        scratch_shapes=[pltpu.VMEM((2, QC, 512), BF), pltpu.VMEM((8 * TOK, 512), BF)],
        compiler_params=params(40),
        cost_estimate=cost(2400 << 20, 10 << 20),
        name="block_grad",
    )(
        info, st_all, qg_all,
        p0, r_0, p_m1, r_m1, p_2, r_2, p_p1, r_p1,
        c_mine, c_part, c_m1, d_m1, c_2, d_2, c_p1, d_p1,
    )

    got = lax.all_to_all(pieces, ("yh", "yl"), 0, 0)
    summed = jnp.sum(got.astype(F32), axis=0).reshape(4, 8, 8, 512)
    z_in = summed.transpose(1, 0, 2, 3).astype(BF).reshape(8, 32, 512)
    z_out = lax.all_to_all(z_in, "z", 0, 0)
    x_in = jnp.sum(z_out.astype(F32), axis=0).reshape(4, 8, 512)
    x_out = lax.all_to_all(x_in, "x", 0, 0)
    weight_grad = x_out.transpose(1, 0, 2).reshape(8, WIDTH)

    prods, probs, cross, context_grad = pl.pallas_call(
        values_kernel,
        in_specs=[SMEM] + [VMEM] * 9,
        out_specs=[VMEM] * 4,
        out_shape=[sd((TOK, WIDTH), F32), sd((TOK, WIDTH), F32), sd((4, 4, QC), F32), sd((TOK, WIDTH), BF)],
        scratch_shapes=[pltpu.VMEM((QC, WIDTH), BF), pltpu.VMEM((TOK, WIDTH), BF), pltpu.VMEM((TOK, WIDTH), BF)],
        compiler_params=params(48),
        cost_estimate=cost(4600 << 20, 16 << 20),
        name="values",
    )(info, st_all, qg_all, context, w_a, w_b, p0, p1, p2, p3)

    cross_all = lax.all_to_all(jnp.broadcast_to(cross[None], (16,) + cross.shape), CTX, 0, 0)

    key_grad, q_part = pl.pallas_call(
        grads_kernel,
        in_specs=[SMEM] + [VMEM] * 5,
        out_specs=[VMEM] * 2,
        out_shape=[sd((TOK, WIDTH), BF), sd((2, 8, 16, WIDTH), BF)],
        scratch_shapes=[pltpu.VMEM((QC, WIDTH), BF)],
        compiler_params=params(40),
        cost_estimate=cost(270 << 20, 8 << 20),
        name="grads",
    )(info, cross_all, qg_all, keys, prods, probs)

    q_got = lax.all_to_all(q_part.reshape(16, 16, WIDTH), CTX, 0, 0)
    query_grad = jnp.sum(q_got.astype(F32), axis=0).astype(BF)
    return (query_grad[None], key_grad[None], context_grad[None], weight_grad)


def solution(mesh):
    fine = Mesh(mesh.devices.reshape(2, 4, 2, 2, 8), AXES)
    fsdp = ("yl", "z")
    rows = P(fsdp, CTX, None)
    return jax.shard_map(
        on_device,
        mesh=fine,
        in_specs=(rows, rows, rows, rows, P(fsdp, None), P(fsdp, None, None), P(fsdp, None), P(fsdp, CTX)),
        out_specs=(rows, rows, rows, P(AXES, None)),
        check_vma=False,
    )
```

time: 1770 us -> 278 us (0.16); the launches traced: 1740 us -> 277 us
  waiting for transfers between devices: 1500 us -> 133 us
  blocking collectives: 129 us -> 33.7 us
  starting transfers between devices: 0.37 us -> 40.3 us
  matrix products: 26.4 us -> 0 us
  local copies, waits for them, and re-layouts: 49.3 us -> 27.2 us
  Pallas kernels: 0 us -> 20.1 us
    unnamed x6 -> x1, waiting for transfers between devices: 1270 us -> 0.02 us
    all_gather x3 -> x1, waiting for transfers between devices: 194 us -> 57.2 us  [on_device(): w_a = lax.all_gather(w_mine, 'z', axis=0, tiled=True)]
    psum x1 -> x0, blocking collectives: 65 us -> none  [on_device(): lax.psum((spread(local_sum, 0.0), spread(local_cross, 0.0)), 'ctx')]
    pmax x1 -> x0, blocking collectives: 63.9 us -> none  [on_device(): row_max = own_rows(lax.pmax(spread(local_max, neg_large), 'ctx'))]
    ppermute x0 -> x17, waiting for transfers between devices: none -> 52.4 us  [the longest x15 44.1 us: shift(): return lax.ppermute(a, axis, [(i, (i + by) % n) for i in range(n)])]
    reduce_scatter x1 -> x0, waiting for transfers between devices: 37.1 us -> none  [on_device(): lax.psum_scatter(query_terms[None], 'ctx', scatter_dimension=1, tiled=True)]
    all_to_all x0 -> x2, blocking collectives: none -> 33.7 us  [the longest x1 17.3 us: on_device(): got = lax.all_to_all(pieces, ('yh', 'yl'), 0, 0)]
    dot_general x14 -> x0, matrix products: 26.4 us -> none  [the longest x1 8.14 us: on_device(): lax.dot_general(context[0], value_grad, (((0,), (0,)), ((), ())), preferr...]
  transfers between devices with their start and end apart: 5 -> 23, of which waited for: 5 -> 9; matrix products, arithmetic and copies ran while one was open for 3% -> 6% of each run, Pallas kernels for 0% -> 7%
where the time goes in v1:
time: 278 us; the launch traced here: 277 us
  waiting for transfers between devices  133 us (48%)
  starting transfers between devices  40.3 us (14%)
  blocking collectives  33.7 us (12%)
  local copies, waits for them, and re-layouts  27.2 us (10%)
  Pallas kernels  20.1 us (7%)
  between operations  17.5 us (6%)
  other arithmetic  4.89 us (2%)
    all_gather x1, waiting for transfers between devices, on_device(): w_a = lax.all_gather(w_mine, 'z', axis=0, tiled=True)  57.2 us
    ppermute x15, waiting for transfers between devices, shift(): return lax.ppermute(a, axis, [(i, (i + by) % n) for i in range(n)])  44.1 us
    all_to_all x1, waiting for transfers between devices, on_device(): q_got = lax.all_to_all(q_part.reshape(16, 16, WIDTH), CTX, 0, 0)  17.4 us
    all_to_all x1, blocking collectives, on_device(): got = lax.all_to_all(pieces, ('yh', 'yl'), 0, 0)  17.3 us
    all_to_all x1, blocking collectives, on_device(): lax.all_to_all(jnp.broadcast_to(st[None], (16,) + st.shape), CTX, 0, 0)  16.5 us
    unnamed x47, local copies, waits for them, and re-layouts  14.3 us
    ppermute x15, starting transfers between devices, shift(): return lax.ppermute(a, axis, [(i, (i + by) % n) for i in range(n)])  12.6 us
    pallas_call x1, Pallas kernels, on_device(): pl.pallas_call(values_kernel, in_specs=[SMEM] + [VMEM] * 9, out_specs=[VM...  10.8 us
  transfers between devices with their start and end apart: 23, of which 9 were waited for; matrix products, arithmetic and copies ran while one was open for 6% of the time, Pallas kernels for 7%

profile of v1, /device:TPU:1, one launch (start us, length us, event | category | flops | bytes accessed | tf_op | source)
XLA Modules:
  0.0 276.8 jit_solution(6749354866872717821)
XLA Ops:
  10.9 4.6 %collective-permute-done.1 = bf16[64,2048]{1,0:T(8,128)(2,1)S(1)} collective-permute-done((bf16[64,2048]{1,0:T(8,128)(2,1)S(1)}, bf16[64,2048]{1,0:T(8,128)(2,1)S(1)}, u32[]{:S(2)}, u32[]{:S(2)}) %collective-permute-start.1) | collective-permute-done | bytes 262176 | tf_op jit(solution)/shard_map/ppermute | solution.py:207
  15.5 3.8 %collective-permute-done = bf16[64,2048]{1,0:T(8,128)(2,1)S(1)} collective-permute-done((bf16[64,2048]{1,0:T(8,128)(2,1)S(1)}, bf16[64,2048]{1,0:T(8,128)(2,1)S(1)}, u32[]{:S(2)}, u32[]{:S(2)}) %collective-permute-start) | collective-permute-done | bytes 262176 | tf_op jit(solution)/shard_map/ppermute | solution.py:206
  20.2 57.2 %all-gather.2.cloned.1.call-done.wa = bf16[1024,2048]{1,0:T(8,128)(2,1)} async-done(((bf16[128,2048]{1,0:T(8,128)(2,1)}), bf16[1024,2048]{1,0:T(8,128)(2,1)}) %all-gather.2.cloned.1.call-update) | async-done | bytes 4194320 | tf_op jit(solution)/shard_map/all_gather | solution.py:209
  79.7 7.0 %all-to-all-start = ((bf16[16,2,16,2048]{3,2,1,0:T(8,128)(2,1)}), bf16[16,2,16,2048]{3,2,1,0:T(8,128)(2,1)S(1)}, u32[]{:S(2)}, u32[]{:S(2)}) async-start(bf16[16,2,16,2048]{3,2,1,0:T(8,128)(2,1)} %broadcast_in_dim.12), calls=%async_computation | async-start | bytes 4194304 | tf_op jit(solution)/shard_map/all_to_all | solution.py:200
  88.2 3.4 %fusion = (bf16[256,8,1,128]{3,2,1,0:T(2,128)(2,1)S(1)}, bf16[256,8,1,128]{3,2,1,0:T(2,128)(2,1)S(1)}) fusion(bf16[256,8,2,128]{3,2,1,0:T(2,128)(2,1)} %reshape_squeeze.3), kind=kLoop, calls=%fused_computation.8 | loop fusion | bytes 2097152 | tf_op jit(solution)/shard_map/slice | solution.py:213
  94.7 2.0 collective-permute-start.14
  98.1 27.5 %collective-permute-done.11.refs_10_ = bf16[256,1024]{1,0:T(8,128)(2,1)} collective-permute-done((bf16[256,1024]{1,0:T(8,128)(2,1)}, bf16[256,1024]{1,0:T(8,128)(2,1)}, u32[]{:S(2)}, u32[]{:S(2)}) %collective-permute-start.11) | collective-permute-done | bytes 524320 | tf_op jit(solution)/shard_map/ppermute | solution.py:43
  125.6 2.2 collective-permute-start.13
  132.7 2.6 concatenate.9.info
  135.4 1.7 scores.1
  140.3 7.8 %collective-permute-done.13.refs_12_ = bf16[256,1024]{1,0:T(8,128)(2,1)} collective-permute-done((bf16[256,1024]{1,0:T(8,128)(2,1)}, bf16[256,1024]{1,0:T(8,128)(2,1)}, u32[]{:S(2)}, u32[]{:S(2)}) %collective-permute-start.13) | collective-permute-done | bytes 524320 | tf_op jit(solution)/shard_map/ppermute | solution.py:43
  149.7 3.9 %collective-permute-done.4.refs_2_ = bf16[256,512]{1,0:T(8,128)(2,1)S(1)} collective-permute-done((bf16[256,512]{1,0:T(8,128)(2,1)S(1)}, bf16[256,512]{1,0:T(8,128)(2,1)S(1)}, u32[]{:S(2)}, u32[]{:S(2)}) %collective-permute-start.4) | collective-permute-done | bytes 262176 | tf_op jit(solution)/shard_map/ppermute | solution.py:43
  154.4 4.8 %collective-permute-done.6.refs_4_ = bf16[256,512]{1,0:T(8,128)(2,1)S(1)} collective-permute-done((bf16[256,512]{1,0:T(8,128)(2,1)S(1)}, bf16[256,512]{1,0:T(8,128)(2,1)S(1)}, u32[]{:S(2)}, u32[]{:S(2)}) %collective-permute-start.6) | collective-permute-done | bytes 262176 | tf_op jit(solution)/shard_map/ppermute | solution.py:43
  159.8 16.5 %all_to_all.35.st_ref = f32[16,2,4,4,128]{4,3,2,1,0:T(4,128)S(1)} all-to-all(f32[16,2,4,4,128]{4,3,2,1,0:T(4,128)S(1)} %broadcast_in_dim.13), channel_id=1, replica_groups=mesh['yh'=2,'x'=4,'k'=2,'yl'=2,'z'=8] {'yh','x','k'}, dimensions={0} | all-to-all | bytes 524288 | tf_op jit(solution)/shard_map/all_to_all | solution.py:234
  176.3 5.1 %block_grad.1 = bf16[4,4,64,512]{3,2,1,0:T(8,128)(2,1)S(1)} custom-call(s32[13]{0:T(128)S(1)} %concatenate.9.info, f32[16,2,4,4,128]{4,3,2,1,0:T(4,128)S(1)} %all_to_all.35.st_ref, bf16[16,2,16,2048]{3,2,1,0:T(8,128)(2,1)S(1)} %all-to-all-done.qg_ref, bf16[256,512]{1,0:T(8,128)(2,1)S(1)} %get-tuple-element.16.p0.refs_0_, ...), custom_call_target="tpu_custom_call" | custom-call | flops 2516582400 | bytes 10485760 | tf_op jit(solution)/shard_map/block_grad/pallas_call | solution.py:237
  181.5 17.3 %all_to_all.36 = bf16[4,4,64,512]{3,2,1,0:T(8,128)(2,1)} all-to-all(bf16[4,4,64,512]{3,2,1,0:T(8,128)(2,1)S(1)} %block_grad.1), channel_id=1, replica_groups=mesh['yh'=2,'x'=4,'k'=2,'yl'=2,'z'=8] {'yh','yl'}, dimensions={0} | all-to-all | bytes 2097152 | tf_op jit(solution)/shard_map/all_to_all | solution.py:252
  200.9 4.0 %all-to-all-start.5 = ((bf16[8,32,512]{2,1,0:T(8,128)(2,1)}), bf16[8,32,512]{2,1,0:T(8,128)(2,1)}, u32[]{:S(2)}, u32[]{:S(2)}) async-start(bf16[8,32,512]{2,1,0:T(8,128)(2,1)} %copy_bitcast_fusion.2), calls=%async_computation.5 | async-start | bytes 524288 | tf_op jit(solution)/shard_map/all_to_all | solution.py:255
  210.0 10.8 %values.1 = (f32[256,2048]{1,0:T(8,128)S(1)}, f32[256,2048]{1,0:T(8,128)}, f32[4,4,128]{2,1,0:T(4,128)S(1)}, bf16[256,2048]{1,0:T(8,128)(2,1)}) custom-call(s32[13]{0:T(128)S(1)} %concatenate.9.info, f32[16,2,4,4,128]{4,3,2,1,0:T(4,128)S(1)} %all_to_all.35.st_ref, bf16[16,2,16,2048]{3,2,1,0:T(8,128)(2,1)} %copy-done, bf16[256,2048]{1,0:T(8,128)(2,1)S(1)} %bitcast.45, ...), custom_call_target="tpu_custom_call" | custom-call | flops 4823449600 | bytes 16777216 | tf_op jit(solution)/shard_map/values/pallas_call | solution.py:260
  222.8 5.5 %all-to-all-start.2 = ((f32[16,4,4,128]{3,2,1,0:T(4,128)}), f32[16,4,4,128]{3,2,1,0:T(4,128)S(1)}, u32[]{:S(2)}, u32[]{:S(2)}) async-start(f32[16,4,4,128]{3,2,1,0:T(4,128)} %broadcast_in_dim.14), calls=%async_computation.2 | async-start | bytes 262144 | tf_op jit(solution)/shard_map/all_to_all | solution.py:271
  229.9 6.0 %all-to-all-done.2.cross_ref = f32[16,4,4,128]{3,2,1,0:T(4,128)S(1)} async-done(((f32[16,4,4,128]{3,2,1,0:T(4,128)}), f32[16,4,4,128]{3,2,1,0:T(4,128)S(1)}, u32[]{:S(2)}, u32[]{:S(2)}) %all-to-all-start.2) | async-done | bytes 131104 | tf_op jit(solution)/shard_map/all_to_all | solution.py:271
  235.9 3.3 %all-to-all-start.6 = ((f32[4,8,512]{2,1,0:T(8,128)}), f32[4,8,512]{2,1,0:T(8,128)S(1)}, u32[]{:S(2)}, u32[]{:S(2)}) async-start(f32[4,8,512]{2,1,0:T(8,128)} %bitcast.23), calls=%async_computation.6 | async-start | bytes 131072 | tf_op jit(solution)/shard_map/all_to_all | solution.py:257
  242.4 2.5 grads.1
  245.9 5.3 %all-to-all-start.3 = ((bf16[16,16,2048]{2,1,0:T(8,128)(2,1)}), bf16[16,16,2048]{2,1,0:T(8,128)(2,1)S(1)}, u32[]{:S(2)}, u32[]{:S(2)}) async-start(bf16[16,16,2048]{2,1,0:T(8,128)(2,1)} %bitcast.46), calls=%async_computation.3 | async-start | bytes 2097152 | tf_op jit(solution)/shard_map/all_to_all | solution.py:284
  251.2 17.4 %all-to-all-done.3 = bf16[16,16,2048]{2,1,0:T(8,128)(2,1)S(1)} async-done(((bf16[16,16,2048]{2,1,0:T(8,128)(2,1)}), bf16[16,16,2048]{2,1,0:T(8,128)(2,1)S(1)}, u32[]{:S(2)}, u32[]{:S(2)}) %all-to-all-start.3) | async-done | bytes 1048608 | tf_op jit(solution)/shard_map/all_to_all | solution.py:284
  (92 shorter events, 37.2 us)
Async XLA Ops:
  7.2 71.0 %copy-start.17 = (bf16[1,16,2048]{2,1,0:T(8,128)(2,1)S(1)}, bf16[1,16,2048]{2,1,0:T(8,128)(2,1)}, u32[]{:S(2)}) copy-start(bf16[1,16,2048]{2,1,0:T(8,128)(2,1)} %param.9) | copy-start | bytes 196612
  7.2 70.3 %all-gather.2.cloned.1.call-start = ((), (), s32[]{:S(2)}) async-start(), calls=%async_computation.7 | async-start | bytes 4718592 | tf_op jit(solution)/shard_map/all_gather | solution.py:209
  8.3 7.2 %collective-permute-start.1 = (bf16[64,2048]{1,0:T(8,128)(2,1)S(1)}, bf16[64,2048]{1,0:T(8,128)(2,1)S(1)}, u32[]{:S(2)}, u32[]{:S(2)}) collective-permute-start(bf16[64,2048]{1,0:T(8,128)(2,1)S(1)} %get-tuple-element.31), channel_id=1, source_target_pairs={{0,136},{24,16},{128,8},{152,144},{1,137},{25,17},{129,9},{153,145... | collective-permute-start | bytes 786440 | tf_op jit(solution)/shard_map/ppermute | solution.py:207
  9.6 9.7 %collective-permute-start = (bf16[64,2048]{1,0:T(8,128)(2,1)S(1)}, bf16[64,2048]{1,0:T(8,128)(2,1)S(1)}, u32[]{:S(2)}, u32[]{:S(2)}) collective-permute-start(bf16[64,2048]{1,0:T(8,128)(2,1)S(1)} %get-tuple-element.30), channel_id=1, source_target_pairs={{0,8},{24,144},{128,136},{152,16},{1,9},{25,145},{129,137},{153,17... | collective-permute-start | bytes 786440 | tf_op jit(solution)/shard_map/ppermute | solution.py:206
  77.4 127.5 %collective-permute-start.2 = (bf16[1024,2048]{1,0:T(8,128)(2,1)}, bf16[1024,2048]{1,0:T(8,128)(2,1)}, u32[]{:S(2)}, u32[]{:S(2)}) collective-permute-start(bf16[1024,2048]{1,0:T(8,128)(2,1)} %all-gather.2.cloned.1.call-done.wa), channel_id=1, source_target_pairs={{0,16},{16,0},{1,17},{17,1},{2,18},{18,2},{3,19},{19,3},{4,20},{20... | collective-permute-start | bytes 12582920 | tf_op jit(solution)/shard_map/ppermute | solution.py:43
  79.7 55.6 %all-to-all-start = ((bf16[16,2,16,2048]{3,2,1,0:T(8,128)(2,1)}), bf16[16,2,16,2048]{3,2,1,0:T(8,128)(2,1)S(1)}, u32[]{:S(2)}, u32[]{:S(2)}) async-start(bf16[16,2,16,2048]{3,2,1,0:T(8,128)(2,1)} %broadcast_in_dim.12), calls=%async_computation | async-start | bytes 4194304 | tf_op jit(solution)/shard_map/all_to_all | solution.py:200
  91.9 2.7 collective-permute-start.10
  93.0 32.6 %collective-permute-start.11 = (bf16[256,1024]{1,0:T(8,128)(2,1)}, bf16[256,1024]{1,0:T(8,128)(2,1)}, u32[]{:S(2)}, u32[]{:S(2)}) collective-permute-start(bf16[256,1024]{1,0:T(8,128)(2,1)} %bitcast.42.refs_8_), channel_id=1, source_target_pairs={{0,32},{32,64},{64,96},{96,0},{1,33},{33,65},{65,97},{97,1},{2,34}... | collective-permute-start | bytes 1572872 | tf_op jit(solution)/shard_map/ppermute | solution.py:43
  94.7 33.1 %collective-permute-start.14 = (bf16[256,1024]{1,0:T(8,128)(2,1)}, bf16[256,1024]{1,0:T(8,128)(2,1)}, u32[]{:S(2)}, u32[]{:S(2)}) collective-permute-start(bf16[256,1024]{1,0:T(8,128)(2,1)} %collective-permute-done.10.refs_9_), channel_id=1, source_target_pairs={{0,96},{32,0},{64,32},{96,64},{1,97},{33,1},{65,33},{97,65},{2,98}... | collective-permute-start | bytes 1572872 | tf_op jit(solution)/shard_map/ppermute | solution.py:43
  96.7 40.4 %collective-permute-start.16 = (bf16[256,1024]{1,0:T(8,128)(2,1)}, bf16[256,1024]{1,0:T(8,128)(2,1)}, u32[]{:S(2)}, u32[]{:S(2)}) collective-permute-start(bf16[256,1024]{1,0:T(8,128)(2,1)} %bitcast.42.refs_8_), channel_id=1, source_target_pairs={{0,96},{32,0},{64,32},{96,64},{1,97},{33,1},{65,33},{97,65},{2,98}... | collective-permute-start | bytes 1572872 | tf_op jit(solution)/shard_map/ppermute | solution.py:43
  97.3 41.5 %collective-permute-start.12 = (bf16[256,1024]{1,0:T(8,128)(2,1)}, bf16[256,1024]{1,0:T(8,128)(2,1)}, u32[]{:S(2)}, u32[]{:S(2)}) collective-permute-start(bf16[256,1024]{1,0:T(8,128)(2,1)} %collective-permute-done.10.refs_9_), channel_id=1, source_target_pairs={{0,32},{32,64},{64,96},{96,0},{1,33},{33,65},{65,97},{97,1},{2,34}... | collective-permute-start | bytes 1572872 | tf_op jit(solution)/shard_map/ppermute | solution.py:43
  125.6 22.5 %collective-permute-start.13 = (bf16[256,1024]{1,0:T(8,128)(2,1)}, bf16[256,1024]{1,0:T(8,128)(2,1)}, u32[]{:S(2)}, u32[]{:S(2)}) collective-permute-start(bf16[256,1024]{1,0:T(8,128)(2,1)} %collective-permute-done.11.refs_10_), channel_id=1, source_target_pairs={{0,32},{32,64},{64,96},{96,0},{1,33},{33,65},{65,97},{97,1},{2,34}... | collective-permute-start | bytes 1572872 | tf_op jit(solution)/shard_map/ppermute | solution.py:43
  127.8 21.0 %collective-permute-start.15 = (bf16[256,1024]{1,0:T(8,128)(2,1)}, bf16[256,1024]{1,0:T(8,128)(2,1)}, u32[]{:S(2)}, u32[]{:S(2)}) collective-permute-start(bf16[256,1024]{1,0:T(8,128)(2,1)} %collective-permute-done.14.refs_15_), channel_id=1, source_target_pairs={{0,96},{32,0},{64,32},{96,64},{1,97},{33,1},{65,33},{97,65},{2,98}... | collective-permute-start | bytes 1572872 | tf_op jit(solution)/shard_map/ppermute | solution.py:43
  137.1 16.5 %collective-permute-start.4 = (bf16[256,512]{1,0:T(8,128)(2,1)S(1)}, bf16[256,512]{1,0:T(8,128)(2,1)S(1)}, u32[]{:S(2)}, u32[]{:S(2)}) collective-permute-start(bf16[256,512]{1,0:T(8,128)(2,1)S(1)} %get-tuple-element.17.p1), channel_id=1, source_target_pairs={{0,32},{32,64},{64,96},{96,0},{1,33},{33,65},{65,97},{97,1},{2,34}... | collective-permute-start | bytes 786440 | tf_op jit(solution)/shard_map/ppermute | solution.py:43
  138.9 20.3 %collective-permute-start.6 = (bf16[256,512]{1,0:T(8,128)(2,1)S(1)}, bf16[256,512]{1,0:T(8,128)(2,1)S(1)}, u32[]{:S(2)}, u32[]{:S(2)}) collective-permute-start(bf16[256,512]{1,0:T(8,128)(2,1)S(1)} %get-tuple-element.18.p2), channel_id=1, source_target_pairs={{0,64},{32,96},{64,0},{96,32},{1,65},{33,97},{65,1},{97,33},{2,66}... | collective-permute-start | bytes 786440 | tf_op jit(solution)/shard_map/ppermute | solution.py:43
  148.1 11.7 %collective-permute-start.8 = (bf16[256,512]{1,0:T(8,128)(2,1)S(1)}, bf16[256,512]{1,0:T(8,128)(2,1)S(1)}, u32[]{:S(2)}, u32[]{:S(2)}) collective-permute-start(bf16[256,512]{1,0:T(8,128)(2,1)S(1)} %get-tuple-element.19.p3), channel_id=1, source_target_pairs={{0,96},{32,0},{64,32},{96,64},{1,97},{33,1},{65,33},{97,65},{2,98}... | collective-permute-start | bytes 786440 | tf_op jit(solution)/shard_map/ppermute | solution.py:43
  148.8 27.5 %collective-permute-start.3 = (bf16[256,512]{1,0:T(8,128)(2,1)S(1)}, bf16[256,512]{1,0:T(8,128)(2,1)S(1)}, u32[]{:S(2)}, u32[]{:S(2)}) collective-permute-start(bf16[256,512]{1,0:T(8,128)(2,1)S(1)} %get-tuple-element.16.p0.refs_0_), channel_id=1, source_target_pairs={{0,16},{16,0},{1,17},{17,1},{2,18},{18,2},{3,19},{19,3},{4,20},{20... | collective-permute-start | bytes 786440 | tf_op jit(solution)/shard_map/ppermute | solution.py:43
  153.6 22.7 %collective-permute-start.5 = (bf16[256,512]{1,0:T(8,128)(2,1)S(1)}, bf16[256,512]{1,0:T(8,128)(2,1)S(1)}, u32[]{:S(2)}, u32[]{:S(2)}) collective-permute-start(bf16[256,512]{1,0:T(8,128)(2,1)S(1)} %collective-permute-done.4.refs_2_), channel_id=1, source_target_pairs={{0,16},{16,0},{1,17},{17,1},{2,18},{18,2},{3,19},{19,3},{4,20},{20... | collective-permute-start | bytes 786440 | tf_op jit(solution)/shard_map/ppermute | solution.py:43
  159.2 17.1 %collective-permute-start.7 = (bf16[256,512]{1,0:T(8,128)(2,1)S(1)}, bf16[256,512]{1,0:T(8,128)(2,1)S(1)}, u32[]{:S(2)}, u32[]{:S(2)}) collective-permute-start(bf16[256,512]{1,0:T(8,128)(2,1)S(1)} %collective-permute-done.6.refs_4_), channel_id=1, source_target_pairs={{0,16},{16,0},{1,17},{17,1},{2,18},{18,2},{3,19},{19,3},{4,20},{20... | collective-permute-start | bytes 786440 | tf_op jit(solution)/shard_map/ppermute | solution.py:43
  159.8 16.5 %collective-permute-start.9 = (bf16[256,512]{1,0:T(8,128)(2,1)S(1)}, bf16[256,512]{1,0:T(8,128)(2,1)S(1)}, u32[]{:S(2)}, u32[]{:S(2)}) collective-permute-start(bf16[256,512]{1,0:T(8,128)(2,1)S(1)} %collective-permute-done.8.refs_6_), channel_id=1, source_target_pairs={{0,16},{16,0},{1,17},{17,1},{2,18},{18,2},{3,19},{19,3},{4,20},{20... | collective-permute-start | bytes 786440 | tf_op jit(solution)/shard_map/ppermute | solution.py:43
  200.9 21.2 %all-to-all-start.5 = ((bf16[8,32,512]{2,1,0:T(8,128)(2,1)}), bf16[8,32,512]{2,1,0:T(8,128)(2,1)}, u32[]{:S(2)}, u32[]{:S(2)}) async-start(bf16[8,32,512]{2,1,0:T(8,128)(2,1)} %copy_bitcast_fusion.2), calls=%async_computation.5 | async-start | bytes 524288 | tf_op jit(solution)/shard_map/all_to_all | solution.py:255
  222.8 13.1 %all-to-all-start.2 = ((f32[16,4,4,128]{3,2,1,0:T(4,128)}), f32[16,4,4,128]{3,2,1,0:T(4,128)S(1)}, u32[]{:S(2)}, u32[]{:S(2)}) async-start(f32[16,4,4,128]{3,2,1,0:T(4,128)} %broadcast_in_dim.14), calls=%async_computation.2 | async-start | bytes 262144 | tf_op jit(solution)/shard_map/all_to_all | solution.py:271
  235.9 10.0 %all-to-all-start.6 = ((f32[4,8,512]{2,1,0:T(8,128)}), f32[4,8,512]{2,1,0:T(8,128)S(1)}, u32[]{:S(2)}, u32[]{:S(2)}) async-start(f32[4,8,512]{2,1,0:T(8,128)} %bitcast.23), calls=%async_computation.6 | async-start | bytes 131072 | tf_op jit(solution)/shard_map/all_to_all | solution.py:257
  245.9 22.6 %all-to-all-start.3 = ((bf16[16,16,2048]{2,1,0:T(8,128)(2,1)}), bf16[16,16,2048]{2,1,0:T(8,128)(2,1)S(1)}, u32[]{:S(2)}, u32[]{:S(2)}) async-start(bf16[16,16,2048]{2,1,0:T(8,128)(2,1)} %bitcast.46), calls=%async_computation.3 | async-start | bytes 2097152 | tf_op jit(solution)/shard_map/all_to_all | solution.py:284
  (21 other events, 371.0 us)
Sparse Core Ops, SparseCore 0:
  20.4 57.0 all-gather.1

commit v2 on v0

v2 whole, which is shorter than its diff:
```python
import functools
import math

import jax
import jax.numpy as jnp
from jax import lax
from jax.experimental import pallas as pl
from jax.experimental.pallas import tpu as pltpu
from jax.sharding import Mesh, PartitionSpec as P

HD = 128
QC = 128
HEADS = 16
BLK = 64
TOK = 256
WIDTH = 2048
SCALE = 1.0 / math.sqrt(HD)
NEG = -1e30
BF = jnp.bfloat16
F32 = jnp.float32
CTX = ("yh", "x", "k")
AXES = ("yh", "x", "k", "yl", "z")
VMEM = pl.BlockSpec(memory_space=pltpu.VMEM)
SMEM = pl.BlockSpec(memory_space=pltpu.SMEM)

BLOCK = 512
SOURCE_STEP = (0, 3, 1, 2)

def params(megabytes):
    return pltpu.CompilerParams(vmem_limit_bytes=megabytes << 20)


def cost(flops, size):
    return pl.CostEstimate(flops=flops, bytes_accessed=size, transcendentals=0)


def dot(a, b, ca, cb):
    return lax.dot_general(a, b, (((ca,), (cb,)), ((), ())), preferred_element_type=F32)


def shift(a, axis, by):
    n = lax.axis_size(axis)
    return lax.ppermute(a, axis, [(i, (i + by) % n) for i in range(n)])


class Info:
    def __init__(self, plan, lengths, blocks):
        self.x, self.k, self.yh, self.yl = (lax.axis_index(a) for a in ("x", "k", "yh", "yl"))
        self.start, self.width = plan[0, 0, 1], plan[0, 1, 1]
        self.lengths = [lengths[0, e] for e in range(2)]
        self.blocks = blocks


class Fetched:
    def __init__(self, src, dst, sem):
        self.copy = pltpu.make_async_copy(src, dst, sem)
        self.ref = dst
        self.copy.start()
        self.pending = True

    def __getitem__(self, at):
        self.ready()
        return self.ref[at]

    def ready(self):
        if self.pending:
            self.copy.wait()
            self.pending = False


def call(scalars, kernel, name, outs, args, flops, size, scratch=(), ties=(), picks=None, megabytes=48):
    n_in, n_out, n_tie = len(args), len(outs), len(ties)
    picks = picks or {}

    def body(plan, lengths, blocks, *refs):
        info = Info(plan, lengths, blocks)
        srcs, refs = refs[:n_in], refs[n_in + n_tie :]
        out_refs, refs = refs[:n_out], refs[n_out + n_tie :]
        bufs, sems, rest = refs[:n_in], refs[n_in], refs[n_in + 1 :]
        srcs = [picks[i][0](info, a) if i in picks else a for i, a in enumerate(srcs)]
        ins = [Fetched(a, b, sems.at[i]) for i, (a, b) in enumerate(zip(srcs, bufs))]
        kernel(info, *ins, *out_refs, *rest)
        for a in ins:
            a.ready()

    anywhere = pl.BlockSpec(memory_space=pl.ANY)
    return pl.pallas_call(
        body,
        in_specs=[SMEM] * 3 + [anywhere] * (n_in + n_tie),
        out_specs=[VMEM] * n_out + [anywhere] * n_tie,
        out_shape=[jax.ShapeDtypeStruct(shape, kind) for shape, kind in outs]
        + [jax.ShapeDtypeStruct(a.shape, a.dtype) for a in ties],
        scratch_shapes=[
            pltpu.VMEM(picks[i][1] if i in picks else a.shape, a.dtype) for i, a in enumerate(args)
        ]
        + [pltpu.SemaphoreType.DMA((n_in,))]
        + [pltpu.VMEM(shape, kind) for shape, kind in scratch],
        input_output_aliases={3 + n_in + i: n_out + i for i in range(n_tie)},
        compiler_params=params(megabytes),
        cost_estimate=cost(1, 1),
        name=name,
    )(*scalars, *args, *ties)


def source(info, n):
    sx = lax.rem(info.x + SOURCE_STEP[n], 4)
    c = info.yh * 8 + sx * 2 + info.k
    return sx, (c >= info.start) & (c < info.start + info.width)


def pack_kernel(info, k_ref, q_ref, g_ref, w_ref, out_ref, w_out):
    for b in range(4):
        at = pl.ds(pl.multiple_of(b * BLOCK + info.k * 256, 256), 256)
        w_out[:, b * 256 : (b + 1) * 256] = w_ref[:, at]
    row = lax.broadcasted_iota(jnp.int32, (16, BLOCK), 0)
    held = jnp.zeros((16, BLOCK), F32)
    for slot in range(TOK // BLK):
        held = jnp.where(row == slot, info.blocks[0, slot].astype(F32), held)
    for x in range(4):
        cols = slice(x * BLOCK, (x + 1) * BLOCK)
        out_ref[x, 256:272, :] = q_ref[:, cols]
        out_ref[x, 272:288, :] = g_ref[:, cols]
        out_ref[x, 288:304, :] = held.astype(BF)
        out_ref[x, 0:256, :] = k_ref[:, cols]


def unpack_kernel(info, pay, out_ref):
    for i in range(4):
        out_ref[i] = pay[i]


def gather_rows(info, own, pay_k, pay_y, pay_ky, qg_ref):
    ki, yh = info.k, info.yh
    for pay, base, e, k in (
        (own, 256, yh, ki), (pay_k, 0, yh, 1 - ki), (pay_y, 0, 1 - yh, ki), (pay_ky, 0, 1 - yh, 1 - ki),
    ):
        for which in range(2):
            for i in range(4):
                at = pl.ds(pl.multiple_of((i * 2 + k) * 16, 16), 16)
                lo = base + which * 16
                qg_ref[which, e, at, :] = pay[i, lo : lo + 16, :]


def scores_kernel(info, own, pay_k, pay_y, pay_ky, p_ref, top_ref, ex_ref, qg_ref):
    gather_rows(info, own, pay_k, pay_y, pay_ky, qg_ref)
    row = lax.broadcasted_iota(jnp.int32, (BLK, QC), 0).astype(F32)
    col = lax.broadcasted_iota(jnp.int32, (BLK, QC), 1).astype(F32)
    tops, sums, ones = [], [], []
    for n in range(4):
        sx, in_one = source(info, n)
        e = in_one.astype(jnp.int32)
        length = jnp.where(in_one, info.lengths[1], info.lengths[0]).astype(F32)
        held = own[sx, 288:304, 0:QC].astype(F32)
        masks = []
        for slot in range(TOK // BLK):
            b = held[slot : slot + 1, :]
            masks.append((b >= 0.0) & (b * BLK + row <= length - QC + col))
        visible = jnp.concatenate(masks, axis=0)
        top_rows, sum_rows = [], []
        for hh in range(4):
            hs = slice(hh * HD, (hh + 1) * HD)
            masked = jnp.where(visible, dot(own[sx, 0:256, hs], qg_ref[0, e, :, hs], 1, 1) * SCALE, NEG)
            top = jnp.max(masked, axis=0, keepdims=True)
            p = jnp.where(visible, jnp.exp(masked - top), 0.0)
            p_ref[n, :, hs] = p
            top_rows.append(top)
            sum_rows.append(jnp.sum(p, axis=0, keepdims=True))
        tops.append(jnp.concatenate(top_rows, axis=0))
        sums.append(jnp.concatenate(sum_rows, axis=0))
        ones.append(in_one)
        top_ref[n] = tops[n]
    for e in range(2):
        of_e = [one if e else jnp.logical_not(one) for one in ones]
        top = jnp.full((4, QC), NEG, F32)
        for n in range(4):
            top = jnp.maximum(top, jnp.where(of_e[n], tops[n], NEG))
        total = jnp.zeros((4, QC), F32)
        for n in range(4):
            total = total + jnp.where(of_e[n], sums[n] * jnp.exp(tops[n] - top), 0.0)
        ex_ref[0, e] = top
        ex_ref[1, e] = total


def probs_kernel(
    info, qg_ref, p_ref, top_ref, x0, x1, x2, x3, v0, v1, v2, v3, u1, u2, u3, fac_ref
):
    tops, invs = [], []
    for e in range(2):
        top = jnp.maximum(
            jnp.maximum(x0[0, e], x1[0, e]), jnp.maximum(x2[0, e], x3[0, e])
        )
        total = jnp.zeros((4, QC), F32)
        for x_ref in (x0, x1, x2, x3):
            total = total + x_ref[1, e] * jnp.exp(x_ref[0, e] - top)
        tops.append(top)
        invs.append(1.0 / total)
    for n, home in enumerate(((v0,), (v1, u1), (v2, u2), (v3, u3))):
        _, in_one = source(info, n)
        e = in_one.astype(jnp.int32)
        top = jnp.where(in_one, tops[1], tops[0])
        factor = jnp.exp(top_ref[n] - top) * jnp.where(in_one, invs[1], invs[0])
        fac_ref[n] = factor
        for hh in range(4):
            hs = slice(hh * HD, (hh + 1) * HD)
            pr = (p_ref[n, :, hs] * factor[hh : hh + 1, :]).astype(BF)
            vg = dot(pr, qg_ref[1, e, :, hs], 1, 0).astype(BF)
            for out in home:
                out[:, hs] = vg


def early_kernel(info, v_0, v_1, v_2, c_0, c_1, c_2, out_ref):
    for tile in range(8):
        cols = slice(tile * 256, (tile + 1) * 256)
        acc = jnp.zeros((256, BLOCK), F32)
        for vg, c in ((v_0, c_0), (v_1, c_1), (v_2, c_2)):
            acc = acc + dot(c[:, cols], vg[...], 0, 0)
        for k in range(2):
            out_ref[k, tile * 128 : (tile + 1) * 128, :] = acc[k * 128 : (k + 1) * 128]


def late_rows(half, tile, acc_ref, vg, c):
    cols = [pl.ds(pl.multiple_of((tile * 4 + j * 2 + half) * 128, 128), 128) for j in range(2)]
    left = jnp.concatenate([c[:, at] for at in cols], axis=1)
    return acc_ref[tile * 256 : (tile + 1) * 256, :] + dot(left, vg[...], 0, 0)


def send_kernel(info, acc_ref, vg, c, out_ref):
    for tile in range(4):
        rows = late_rows(1 - info.k, tile, acc_ref, vg, c)
        out_ref[tile * 256 : (tile + 1) * 256, :] = rows.astype(BF)


def keep_kernel(info, acc_ref, vg, c, got_ref, out_ref):
    for tile in range(4):
        acc = late_rows(info.k, tile, acc_ref, vg, c)
        acc = acc + got_ref[tile * 256 : (tile + 1) * 256, :].astype(F32)
        for part in range(4):
            r = tile * 256 + part * 64
            yh, xx, yl = r // 512, (r // 128) % 4, (r // 64) % 2
            out_ref[yh * 2 + yl, xx] = acc[part * 64 : (part + 1) * 64].astype(BF)


def sum_kernel(info, got_ref, out_ref):
    total = jnp.zeros((4, 8, 8, BLOCK), F32)
    for n in range(4):
        total = total + got_ref[n].astype(F32).reshape(4, 8, 8, BLOCK)
    for z in range(8):
        out_ref[z] = total[:, z].reshape(32, BLOCK).astype(BF)


def prods_kernel(
    info, qg_ref, w_oo, w_ot, w_ob, w_po, w_pt, w_pb, p_ref, fac_ref, c0, c1, c2, c3, prod_ref, cross_ref, v_buf
):
    cross = [jnp.zeros((4, QC), F32) for _ in range(2)]
    own = pl.multiple_of(info.yl * 1024, 1024)
    oth = pl.multiple_of((1 - info.yl) * 1024, 1024)
    for n, c in enumerate((c0, c1, c2, c3)):
        _, in_one = source(info, n)
        e = in_one.astype(jnp.int32)
        c_own, c_oth = c[:, pl.ds(own, 1024)], c[:, pl.ds(oth, 1024)]
        for half, (wo, wt, wb) in ((info.k, (w_oo, w_ot, w_ob)), (1 - info.k, (w_po, w_pt, w_pb))):
            v = dot(c_own, wo[...], 1, 0) + dot(c_oth[:, :512], wt[...], 1, 0) + dot(c_oth[:, 512:], wb[...], 1, 0)
            v_buf[:, pl.ds(pl.multiple_of(half * 256, 256), 256)] = v.astype(BF)
        rows = []
        for hh in range(4):
            hs = slice(hh * HD, (hh + 1) * HD)
            prod = dot(v_buf[:, hs], qg_ref[1, e, :, hs], 1, 1)
            prod_ref[n, :, hs] = prod
            pr = p_ref[n, :, hs] * fac_ref[n, hh : hh + 1, :]
            rows.append(jnp.sum(pr * prod, axis=0, keepdims=True))
        part = jnp.concatenate(rows, axis=0)
        cross[0] = cross[0] + jnp.where(in_one, 0.0, part)
        cross[1] = cross[1] + jnp.where(in_one, part, 0.0)
    for e in range(2):
        cross_ref[e] = cross[e]


def grads_kernel(
    info, qg_ref, p_ref, fac_ref, prod_ref, x0, x1, x2, x3, own,
    g0, g1, g2, g3, q0, q1, q2, q3, qp_buf,
):
    qp_buf[...] = jnp.zeros(qp_buf.shape, F32)
    deltas = [x0[e] + x1[e] + x2[e] + x3[e] for e in range(2)]
    for n, out in enumerate((g0, g1, g2, g3)):
        sx, in_one = source(info, n)
        e = in_one.astype(jnp.int32)
        delta = jnp.where(in_one, deltas[1], deltas[0])
        for hh in range(4):
            hs = slice(hh * HD, (hh + 1) * HD)
            pr = p_ref[n, :, hs] * fac_ref[n, hh : hh + 1, :]
            ds = (pr * (prod_ref[n, :, hs] - delta[hh : hh + 1, :])).astype(BF)
            out[:, hs] = (SCALE * dot(ds, qg_ref[0, e, :, hs], 1, 0)).astype(BF)
            qp_buf[e, :, hs] += dot(ds, own[sx, 0:256, hs], 0, 0)
    for out, e, k in (
        (q0, info.yh, info.k), (q1, info.yh, 1 - info.k), (q2, 1 - info.yh, info.k), (q3, 1 - info.yh, 1 - info.k),
    ):
        for x in range(4):
            rows = pl.ds(pl.multiple_of((x * 2 + k) * 16, 16), 16)
            out[x] = (SCALE * qp_buf[e, rows, :]).astype(BF)


def home_kernel(info, b0, b1, b2, b3, out_ref):
    for step, b in enumerate((b0, b1, b2, b3)):
        at = lax.rem(info.x + step, 4) * BLOCK
        out_ref[:, pl.ds(pl.multiple_of(at, BLOCK), BLOCK)] = b[...]


def context_kernel(info, b0, b1, b2, b3, w_oo, w_ot, w_ob, w_po, w_pt, w_pb, out_ref, own_buf, oth_buf):
    for step, b in enumerate((b0, b1, b2, b3)):
        at = pl.ds(pl.multiple_of(lax.rem(info.x + step, 4) * 256, 256), 256)
        own_buf[:, at] = b[:, pl.ds(pl.multiple_of(info.k * 256, 256), 256)]
        oth_buf[:, at] = b[:, pl.ds(pl.multiple_of((1 - info.k) * 256, 256), 256)]
    for base, parts in (
        (info.yl * 1024, ((w_oo, 0, w_po, 0), (w_oo, 512, w_po, 512))),
        ((1 - info.yl) * 1024, ((w_ot, 0, w_pt, 0), (w_ob, 0, w_pb, 0))),
    ):
        for t, (wo, lo, wp, lp) in enumerate(parts):
            acc = dot(own_buf[...], wo[lo : lo + 512, :], 1, 1) + dot(oth_buf[...], wp[lp : lp + 512, :], 1, 1)
            out_ref[:, pl.ds(pl.multiple_of(base + t * 512, 512), 512)] = acc.astype(BF)


def sum_z_kernel(info, got_ref, q0, q1, q2, q3, out_ref):
    total = jnp.zeros((32, BLOCK), F32)
    for n in range(8):
        total = total + got_ref[n].astype(F32)
    out_ref[:, 0:8, :] = total.reshape(4, 8, BLOCK)
    rows = jnp.zeros((4, 16, BLOCK), F32)
    for q in (q0, q1, q2, q3):
        rows = rows + q[...].astype(F32)
    out_ref[:, 8:24, :] = rows


def partners(a):
    core = shift(a, "k", 1)
    return core, shift(a, "yh", 1), shift(core, "yh", 1)


def go_home(parts):
    m1, p1, p2 = parts
    return shift(m1, "x", -1), shift(p2, "x", 2), shift(p1, "x", 1)


def on_device(queries, grad_out, keys, context, value_weight, plan, lengths, blocks):
    yh, xi, ki, yl, zi = (lax.axis_index(a) for a in AXES)
    keys, context = keys[0], context[0]
    run = functools.partial(call, (plan, lengths, blocks))

    pay, w_own = run(
        pack_kernel, "pack", [((4, 304, BLOCK), BF), ((128, 1024), BF)],
        [keys, queries[0], grad_out[0], value_weight], 1, 3, megabytes=60,
    )
    w_oo = lax.all_gather(w_own, "z", axis=0, tiled=True)
    pay = lax.all_to_all(pay, "x", 0, 0)
    (rows,) = run(
        unpack_kernel, "unpack", [((4, 32, BLOCK), BF)], [pay], 1, 1,
        picks={0: (lambda info, r: r.at[:, pl.ds(256, 32)], (4, 32, BLOCK))},
    )
    pay_oth = partners(rows)

    unit = (4, TOK, BLOCK)
    c_m1, c_p1, c_2 = shift(context, "x", 1), shift(context, "x", -1), shift(context, "x", 2)
    c_src = [context, c_m1, c_p1, c_2]

    p, tops, ex, qg = run(
        scores_kernel, "scores",
        [(unit, F32), ((4, 4, QC), F32), ((2, 2, 4, QC), F32), ((2, 2, QC, BLOCK), BF)],
        [pay, *pay_oth], 134, 4,
    )
    v_0, v_m1, v_p1, v_2, u_m1, u_p1, u_2, fac, c_m1, c_p1, w_oo = run(
        probs_kernel, "probs", [((TOK, BLOCK), BF)] * 7 + [((4, 4, QC), F32)],
        [qg, p, tops, ex, *partners(ex)], 134, 4, ties=[c_m1, c_p1, w_oo],
    )
    w_ot = shift(w_oo[:512], ("yh", "yl"), 1)
    w_ob = shift(w_oo[512:], ("yh", "yl"), -1)
    w_all = [w_oo, w_ot, w_ob] + [shift(w, "k", 1) for w in (w_oo, w_ot, w_ob)]
    c_src = [context, c_m1, c_p1, c_2]
    (acc,) = run(
        early_kernel, "block_early", [((2, 1024, BLOCK), F32)], [v_0, v_m1, v_p1] + c_src[:3], 1600, 8,
    )
    picks = {0: (lambda info, r: r.at[1 - info.k], (1024, BLOCK))}
    late = [acc, v_2, c_2]
    (send,) = run(send_kernel, "block_send", [((1024, BLOCK), BF)], late, 270, 4, picks=picks)
    picks = {0: (lambda info, r: r.at[info.k], (1024, BLOCK))}
    pieces, h_m1, h_p1, h_2 = run(
        keep_kernel, "block_keep", [((4, 4, 64, BLOCK), BF)], late + [shift(send, "k", 1)], 270, 5,
        picks=picks, ties=[u_m1, u_p1, u_2],
    )

    got = lax.all_to_all(pieces, ("yh", "yl"), 0, 0)
    prods, cross = run(
        prods_kernel, "prods", [(unit, F32), ((2, 4, QC), F32)],
        [qg, *w_all, p, fac] + c_src, 2300, 10, [((TOK, BLOCK), BF)],
        picks={
            i: (lambda info, r: r.at[:, pl.ds(pl.multiple_of(info.x * 256, 256), 256)], (rows, 256))
            for i, rows in ((1, 1024), (2, 512), (3, 512), (4, 1024), (5, 512), (6, 512))
        },
    )
    g_0, g_m1, g_p1, g_2, q_0, q_k, q_y, q_ky = run(
        grads_kernel, "grads", [((TOK, BLOCK), BF)] * 4 + [((4, 16, BLOCK), BF)] * 4,
        [qg, p, fac, prods, cross, *partners(cross), pay], 270, 6, [((2, QC, BLOCK), F32)],
    )
    z_in, g_m1, g_p1, g_2, q_0 = run(
        sum_kernel, "sum_y", [((8, 32, BLOCK), BF)], [got], 1, 2, ties=[g_m1, g_p1, g_2, q_0],
    )
    both = [(y * 2 + k, (1 - y) * 2 + 1 - k) for y in range(2) for k in range(2)]
    q_rows = [q_0, shift(q_k, "k", 1), shift(q_y, "yh", 1), lax.ppermute(q_ky, ("yh", "k"), both)]
    z_out = lax.all_to_all(z_in, "z", 0, 0)
    (x_in,) = run(sum_z_kernel, "sum_z", [((4, 24, BLOCK), F32)], [z_out, *q_rows], 1, 1)
    x_out = lax.all_to_all(x_in, "x", 0, 0).transpose(1, 0, 2).reshape(24, WIDTH)
    weight_grad, query_grad = x_out[:8], x_out[8:].astype(BF)

    (key_grad,) = run(
        home_kernel, "key_home", [((TOK, WIDTH), BF)], [g_0, *go_home((g_m1, g_p1, g_2))], 1, 2,
    )
    (context_grad,) = run(
        context_kernel, "context_grad", [((TOK, WIDTH), BF)],
        [v_0, *go_home((h_m1, h_p1, h_2)), *w_all], 2200, 10,
        [((TOK, 1024), BF)] * 2,
    )
    return (query_grad[None], key_grad[None], context_grad[None], weight_grad)


def solution(mesh):
    fine = Mesh(mesh.devices.reshape(2, 4, 2, 2, 8), AXES)
    fsdp = ("yl", "z")
    rows = P(fsdp, CTX, None)
    return jax.shard_map(
        on_device,
        mesh=fine,
        in_specs=(rows, rows, rows, rows, P(fsdp, None), P(fsdp, None, None), P(fsdp, None), P(fsdp, CTX)),
        out_specs=(rows, rows, rows, P(AXES, None)),
        check_vma=False,
    )
```

time: 1770 us -> 189 us (0.11); the launches traced: 1740 us -> 188 us
  waiting for transfers between devices: 1500 us -> 37.1 us
  blocking collectives: 129 us -> 0 us
  starting transfers between devices: 0.37 us -> 71.5 us
  Pallas kernels: 0 us -> 47.6 us
  local copies, waits for them, and re-layouts: 49.3 us -> 17.8 us
  matrix products: 26.4 us -> 0 us
    unnamed x6 -> x1, waiting for transfers between devices: 1270 us -> 0.02 us
    all_gather x3 -> x1, waiting for transfers between devices: 194 us -> 0.01 us  [on_device(): w_oo = lax.all_gather(w_own, 'z', axis=0, tiled=True)]
    psum x1 -> x0, blocking collectives: 65 us -> none  [on_device(): lax.psum((spread(local_sum, 0.0), spread(local_cross, 0.0)), 'ctx')]
    pmax x1 -> x0, blocking collectives: 63.9 us -> none  [on_device(): row_max = own_rows(lax.pmax(spread(local_max, neg_large), 'ctx'))]
    ppermute x0 -> x27, starting transfers between devices: none -> 50 us  [the longest x26 47.7 us: shift(): return lax.ppermute(a, axis, [(i, (i + by) % n) for i in range(n)])]
    pallas_call x0 -> x13, Pallas kernels: none -> 47.6 us  [call(): pl.pallas_call(body, in_specs=[SMEM] * 3 + [anywhere] * (n_in + n_tie), o...]
    reduce_scatter x1 -> x0, waiting for transfers between devices: 37.1 us -> none  [on_device(): lax.psum_scatter(query_terms[None], 'ctx', scatter_dimension=1, tiled=True)]
    dot_general x14 -> x0, matrix products: 26.4 us -> none  [the longest x1 8.14 us: on_device(): lax.dot_general(context[0], value_grad, (((0,), (0,)), ((), ())), preferr...]
  transfers between devices with their start and end apart: 5 -> 32, of which waited for: 5 -> 12; matrix products, arithmetic and copies ran while one was open for 3% -> 1% of each run, Pallas kernels for 0% -> 23%
where the time goes in v2:
time: 189 us; the launch traced here: 188 us
  starting transfers between devices  71.5 us (38%)
  Pallas kernels  47.6 us (25%)
  waiting for transfers between devices  37.1 us (20%)
  local copies, waits for them, and re-layouts  17.8 us (9%)
  between operations  14.3 us (8%)
    ppermute x26, starting transfers between devices, shift(): return lax.ppermute(a, axis, [(i, (i + by) % n) for i in range(n)])  47.7 us
    pallas_call x13, Pallas kernels, call(): pl.pallas_call(body, in_specs=[SMEM] * 3 + [anywhere] * (n_in + n_tie), o...  47.6 us
    ppermute x26, waiting for transfers between devices, shift(): return lax.ppermute(a, axis, [(i, (i + by) % n) for i in range(n)])  25.9 us
    unnamed x62, local copies, waits for them, and re-layouts  13.9 us
    all_to_all x1, waiting for transfers between devices, on_device(): pay = lax.all_to_all(pay, 'x', 0, 0)  11 us
    all_to_all x1, starting transfers between devices, on_device(): z_out = lax.all_to_all(z_in, 'z', 0, 0)  8.59 us
    all_to_all x1, starting transfers between devices, on_device(): pay = lax.all_to_all(pay, 'x', 0, 0)  4.87 us
    all_to_all x1, starting transfers between devices, on_device(): got = lax.all_to_all(pieces, ('yh', 'yl'), 0, 0)  4.07 us
  transfers between devices with their start and end apart: 32, of which 12 were waited for; matrix products, arithmetic and copies ran while one was open for 1% of the time, Pallas kernels for 23%

profile of v2, /device:TPU:1, one launch (start us, length us, event | category | flops | bytes accessed | tf_op | source)
XLA Modules:
  0.0 188.4 jit_solution(11709289224244497281)
XLA Ops:
  7.2 3.5 %pack.1 = (bf16[4,304,512]{2,1,0:T(8,128)(2,1)}, bf16[128,1024]{1,0:T(8,128)(2,1)}) custom-call(s32[1,2,2]{2,1,0:T(2,128)} %plan.25, s32[1,2]{1,0:T(1,128)} %lengths.25, s32[1,4]{1,0:T(1,128)} %blocks.25, bf16[256,2048]{1,0:T(8,128)(2,1)} %bitcast.9, bf16[16,2048]{1,0:T(8,128)(2,1)} %bitcast.14, bf16[16,2048]{1,0:T(8,128)(2,1)} %bitcast.15, ...), custom_call_target="tpu_custom_call" | custom-call | flops 1 | bytes 1 | tf_op jit(solution)/shard_map/pack/pallas_call | solution.py:87
  10.7 4.9 %all-to-all-start = ((bf16[4,304,512]{2,1,0:T(8,128)(2,1)}), bf16[4,304,512]{2,1,0:T(8,128)(2,1)S(1)}, u32[]{:S(2)}, u32[]{:S(2)}) async-start(bf16[4,304,512]{2,1,0:T(8,128)(2,1)} %get-tuple-element.40), calls=%async_computation | async-start | bytes 2490368 | tf_op jit(solution)/shard_map/all_to_all | solution.py:353
  20.0 11.0 %all-to-all-done.refs_0_.refs_8_ = bf16[4,304,512]{2,1,0:T(8,128)(2,1)S(1)} async-done(((bf16[4,304,512]{2,1,0:T(8,128)(2,1)}), bf16[4,304,512]{2,1,0:T(8,128)(2,1)S(1)}, u32[]{:S(2)}, u32[]{:S(2)}) %all-to-all-start) | async-done | bytes 1245216 | tf_op jit(solution)/shard_map/all_to_all | solution.py:353
  31.6 5.3 %collective-permute-start = (bf16[4,32,512]{2,1,0:T(8,128)(2,1)S(1)}, bf16[4,32,512]{2,1,0:T(8,128)(2,1)S(1)}, u32[]{:S(2)}, u32[]{:S(2)}) collective-permute-start(bf16[4,32,512]{2,1,0:T(8,128)(2,1)S(1)} %unpack.1), channel_id=1, source_target_pairs={{0,16},{16,0},{1,17},{17,1},{2,18},{18,2},{3,19},{19,3},{4,20},{20... | collective-permute-start | bytes 393224 | tf_op jit(solution)/shard_map/ppermute | solution.py:43
  40.0 3.6 %collective-permute-done.1.refs_2_ = bf16[4,32,512]{2,1,0:T(8,128)(2,1)S(1)} collective-permute-done((bf16[4,32,512]{2,1,0:T(8,128)(2,1)S(1)}, bf16[4,32,512]{2,1,0:T(8,128)(2,1)S(1)}, u32[]{:S(2)}, u32[]{:S(2)}) %collective-permute-start.1) | collective-permute-done | bytes 131104 | tf_op jit(solution)/shard_map/ppermute | solution.py:43
  43.5 2.8 %collective-permute-done.2.refs_3_ = bf16[4,32,512]{2,1,0:T(8,128)(2,1)S(1)} collective-permute-done((bf16[4,32,512]{2,1,0:T(8,128)(2,1)S(1)}, bf16[4,32,512]{2,1,0:T(8,128)(2,1)S(1)}, u32[]{:S(2)}, u32[]{:S(2)}) %collective-permute-start.2) | collective-permute-done | bytes 131104 | tf_op jit(solution)/shard_map/ppermute | solution.py:43
  46.3 2.5 %scores.1 = (f32[4,256,512]{2,1,0:T(8,128)S(1)}, f32[4,4,128]{2,1,0:T(4,128)S(1)}, f32[2,2,4,128]{3,2,1,0:T(4,128)S(1)}, bf16[2,2,128,512]{3,2,1,0:T(8,128)(2,1)S(1)}) custom-call(s32[1,2,2]{2,1,0:T(2,128)S(1)} %copy-done.22, s32[1,2]{1,0:T(1,128)S(1)} %copy-done.23, s32[1,4]{1,0:T(1,128)S(1)} %copy-done.24, ...), custom_call_target="tpu_custom_call" | custom-call | flops 1 | bytes 1 | tf_op jit(solution)/shard_map/scores/pallas_call | solution.py:87
  58.9 2.7 %probs.1 = (bf16[256,512]{1,0:T(8,128)(2,1)S(1)}, bf16[256,512]{1,0:T(8,128)(2,1)S(1)}, bf16[256,512]{1,0:T(8,128)(2,1)S(1)}, bf16[256,512]{1,0:T(8,128)(2,1)S(1...) custom-call(s32[1,2,2]{2,1,0:T(2,128)S(1)} %copy-done.22, ...), custom_call_target="tpu_custom_call", output_to_operand_aliasing={{8}: (10, {}), {9}: (11, {}), {10}: (12, {})} | custom-call | flops 1 | bytes 1 | tf_op jit(solution)/shard_map/probs/pallas_call | solution.py:87
  61.7 2.6 %fusion = (bf16[512,1024]{1,0:T(8,128)(2,1)S(1)}, bf16[512,1024]{1,0:T(8,128)(2,1)S(1)}) fusion(bf16[1024,1024]{1,0:T(8,128)(2,1)} %get-tuple-element.57.refs_1_.refs_4_), kind=kLoop, calls=%fused_computation.1 | loop fusion | bytes 4194304 | tf_op jit(solution)/shard_map/slice | solution.py:374
  69.0 5.8 %block_early.1.refs_0_ = f32[2,1024,512]{2,1,0:T(8,128)} custom-call(s32[1,2,2]{2,1,0:T(2,128)S(1)} %copy-done.22, s32[1,2]{1,0:T(1,128)S(1)} %copy-done.23, s32[1,4]{1,0:T(1,128)S(1)} %copy-done.24, bf16[256,512]{1,0:T(8,128)(2,1)S(1)} %get-tuple-element.46.refs_0_, bf16[256,512]{1,0:T(8,128)(2,1)S(1)} %get-tuple-element.47.refs_1_, ...), custom_call_target="tpu_custom_call" | custom-call | flops 1 | bytes 1 | tf_op jit(solution)/shard_map/block_early/pallas_call | solution.py:87
  76.0 3.0 %block_send.1 = bf16[1024,512]{1,0:T(8,128)(2,1)S(1)} custom-call(s32[1,2,2]{2,1,0:T(2,128)S(1)} %copy-done.22, s32[1,2]{1,0:T(1,128)S(1)} %copy-done.23, s32[1,4]{1,0:T(1,128)S(1)} %copy-done.24, f32[2,1024,512]{2,1,0:T(8,128)} %block_early.1.refs_0_, bf16[256,512]{1,0:T(8,128)(2,1)S(1)} %get-tuple-element.51.refs_1_, ...), custom_call_target="tpu_custom_call" | custom-call | flops 1 | bytes 1 | tf_op jit(solution)/shard_map/block_send/pallas_call | solution.py:87
  79.0 3.1 %collective-permute-start.9 = (bf16[1024,512]{1,0:T(8,128)(2,1)S(1)}, bf16[1024,512]{1,0:T(8,128)(2,1)S(1)}, u32[]{:S(2)}, u32[]{:S(2)}) collective-permute-start(bf16[1024,512]{1,0:T(8,128)(2,1)S(1)} %block_send.1), channel_id=1, source_target_pairs={{0,16},{16,0},{1,17},{17,1},{2,18},{18,2},{3,19},{19,3},{4,20},{20... | collective-permute-start | bytes 3145736 | tf_op jit(solution)/shard_map/ppermute | solution.py:43
  82.1 6.7 %collective-permute-done.10.refs_2_.refs_5_ = bf16[512,1024]{1,0:T(8,128)(2,1)} collective-permute-done((bf16[512,1024]{1,0:T(8,128)(2,1)S(1)}, bf16[512,1024]{1,0:T(8,128)(2,1)}, u32[]{:S(2)}, u32[]{:S(2)}) %collective-permute-start.10) | collective-permute-done | bytes 1048608 | tf_op jit(solution)/shard_map/ppermute | solution.py:43
  91.2 3.3 %block_keep.1 = (bf16[4,4,64,512]{3,2,1,0:T(8,128)(2,1)S(1)}, bf16[256,512]{1,0:T(8,128)(2,1)S(1)}, bf16[256,512]{1,0:T(8,128)(2,1)S(1)}, bf16[256,512]{1,0:T(8,128)(2,1)S(1)}) custom-call(s32[1,2,2]{2,1,0:T(2,128)S(1)} %copy-done.22, s32[1,2]{1,0:T(1,128)S(1)} %copy-done.23, ...), custom_call_target="tpu_custom_call", output_to_operand_aliasing={{1}: (7, {}), {2}: (8, {}), {3}: (9, {})} | custom-call | flops 1 | bytes 1 | tf_op jit(solution)/shard_map/block_keep/pallas_call | solution.py:87
  97.6 4.1 %all-to-all-start.1 = ((bf16[4,4,64,512]{3,2,1,0:T(8,128)(2,1)}), bf16[4,4,64,512]{3,2,1,0:T(8,128)(2,1)S(1)}, u32[]{:S(2)}, u32[]{:S(2)}) async-start(bf16[4,4,64,512]{3,2,1,0:T(8,128)(2,1)} %copy-done.9), calls=%async_computation.1 | async-start | bytes 2097152 | tf_op jit(solution)/shard_map/all_to_all | solution.py:389
  101.7 9.6 %prods.1 = (f32[4,256,512]{2,1,0:T(8,128)}, f32[2,4,128]{2,1,0:T(4,128)S(1)}) custom-call(s32[1,2,2]{2,1,0:T(2,128)S(1)} %copy-done.22, s32[1,2]{1,0:T(1,128)S(1)} %copy-done.23, s32[1,4]{1,0:T(1,128)S(1)} %copy-done.24, bf16[2,2,128,512]{3,2,1,0:T(8,128)(2,1)S(1)} %copy-done.6, bf16[1024,1024]{1,0:T(8,128)(2,1)} %get-tuple-element.57.refs_1_.refs_4_, ...), custom_call_target="tpu_custom_call" | custom-call | flops 1 | bytes 1 | tf_op jit(solution)/shard_map/prods/pallas_call | solution.py:87
  111.7 3.3 %collective-permute-start.16 = (f32[2,4,128]{2,1,0:T(4,128)S(1)}, f32[2,4,128]{2,1,0:T(4,128)S(1)}, u32[]{:S(2)}, u32[]{:S(2)}) collective-permute-start(f32[2,4,128]{2,1,0:T(4,128)S(1)} %get-tuple-element.59.refs_4_), channel_id=1, source_target_pairs={{0,128},{128,0},{1,129},{129,1},{2,130},{130,2},{3,131},{131,3},{4... | collective-permute-start | bytes 12296 | tf_op jit(solution)/shard_map/ppermute | solution.py:43
  118.9 4.0 %grads.1 = (bf16[256,512]{1,0:T(8,128)(2,1)S(1)}, bf16[256,512]{1,0:T(8,128)(2,1)S(1)}, bf16[256,512]{1,0:T(8,128)(2,1)S(1)}, bf16[256,512]{1,0:T(8,128)(2,1)S(1...) custom-call(s32[1,2,2]{2,1,0:T(2,128)S(1)} %copy-done.22, ...), custom_call_target="tpu_custom_call" | custom-call | flops 1 | bytes 1 | tf_op jit(solution)/shard_map/grads/pallas_call | solution.py:87
  130.5 8.6 %all-to-all-start.2 = ((bf16[8,32,512]{2,1,0:T(8,128)(2,1)}), bf16[8,32,512]{2,1,0:T(8,128)(2,1)S(1)}, u32[]{:S(2)}, u32[]{:S(2)}) async-start(bf16[8,32,512]{2,1,0:T(8,128)(2,1)} %get-tuple-element.64), calls=%async_computation.2 | async-start | bytes 524288 | tf_op jit(solution)/shard_map/all_to_all | solution.py:407
  142.9 2.4 %collective-permute-start.20 = (bf16[4,16,512]{2,1,0:T(8,128)(2,1)S(1)}, bf16[4,16,512]{2,1,0:T(8,128)(2,1)S(1)}, u32[]{:S(2)}, u32[]{:S(2)}) collective-permute-start(bf16[4,16,512]{2,1,0:T(8,128)(2,1)S(1)} %copy-done.28), channel_id=1, source_target_pairs={{0,144},{16,128},{128,16},{144,0},{1,145},{17,129},{129,17},{145,1... | collective-permute-start | bytes 196616 | tf_op jit(solution)/shard_map/ppermute | solution.py:406
  145.3 9.4 %collective-permute-start.25 = (bf16[256,512]{1,0:T(8,128)(2,1)S(1)}, bf16[256,512]{1,0:T(8,128)(2,1)S(1)}, u32[]{:S(2)}, u32[]{:S(2)}) collective-permute-start(bf16[256,512]{1,0:T(8,128)(2,1)S(1)} %copy-done.15), channel_id=1, source_target_pairs={{0,64},{32,96},{64,0},{96,32},{1,65},{33,97},{65,1},{97,33},{2,66}... | collective-permute-start | bytes 786440 | tf_op jit(solution)/shard_map/ppermute | solution.py:43
  161.2 3.9 %all-to-all-start.3 = ((f32[4,24,512]{2,1,0:T(8,128)}), f32[4,24,512]{2,1,0:T(8,128)S(1)}, u32[]{:S(2)}, u32[]{:S(2)}) async-start(f32[4,24,512]{2,1,0:T(8,128)} %sum_z.1), calls=%async_computation.3 | async-start | bytes 393216 | tf_op jit(solution)/shard_map/all_to_all | solution.py:409
  167.2 7.7 %context_grad.1 = bf16[256,2048]{1,0:T(8,128)(2,1)} custom-call(s32[1,2,2]{2,1,0:T(2,128)S(1)} %copy-done.22, s32[1,2]{1,0:T(1,128)S(1)} %copy-done.23, s32[1,4]{1,0:T(1,128)S(1)} %copy-done.24, bf16[256,512]{1,0:T(8,128)(2,1)S(1)} %copy-done.8, bf16[256,512]{1,0:T(8,128)(2,1)S(1)} %collective-permute-done.24.refs_1_, ...), custom_call_target="tpu_custom_call" | custom-call | flops 1 | bytes 1 | tf_op jit(solution)/shard_map/context_grad/pallas_call | solution.py:87
  174.9 3.3 %collective-permute-done.23.refs_3_ = bf16[256,512]{1,0:T(8,128)(2,1)S(1)} collective-permute-done((bf16[256,512]{1,0:T(8,128)(2,1)}, bf16[256,512]{1,0:T(8,128)(2,1)S(1)}, u32[]{:S(2)}, u32[]{:S(2)}) %collective-permute-start.23) | collective-permute-done | bytes 262176 | tf_op jit(solution)/shard_map/ppermute | solution.py:43
  (121 shorter events, 57.2 us)
Async XLA Ops:
  7.2 50.7 %all-gather.2.cloned.1.call-start = ((), (), s32[]{:S(2)}) async-start(), calls=%async_computation.4 | async-start | bytes 2359296 | tf_op jit(solution)/shard_map/all_gather | solution.py:352
  10.7 20.3 %all-to-all-start = ((bf16[4,304,512]{2,1,0:T(8,128)(2,1)}), bf16[4,304,512]{2,1,0:T(8,128)(2,1)S(1)}, u32[]{:S(2)}, u32[]{:S(2)}) async-start(bf16[4,304,512]{2,1,0:T(8,128)(2,1)} %get-tuple-element.40), calls=%async_computation | async-start | bytes 2490368 | tf_op jit(solution)/shard_map/all_to_all | solution.py:353
  15.6 39.3 %collective-permute-start.6 = (bf16[256,2048]{1,0:T(8,128)(2,1)}, bf16[256,2048]{1,0:T(8,128)(2,1)S(1)}, u32[]{:S(2)}, u32[]{:S(2)}) collective-permute-start(bf16[256,2048]{1,0:T(8,128)(2,1)} %bitcast.3.refs_3_.refs_9_), channel_id=1, source_target_pairs={{0,32},{32,64},{64,96},{96,0},{1,33},{33,65},{65,97},{97,1},{2,34}... | collective-permute-start | bytes 3145736 | tf_op jit(solution)/shard_map/ppermute | solution.py:43
  17.1 37.8 %collective-permute-start.7 = (bf16[256,2048]{1,0:T(8,128)(2,1)}, bf16[256,2048]{1,0:T(8,128)(2,1)S(1)}, u32[]{:S(2)}, u32[]{:S(2)}) collective-permute-start(bf16[256,2048]{1,0:T(8,128)(2,1)} %bitcast.3.refs_3_.refs_9_), channel_id=1, source_target_pairs={{0,96},{32,0},{64,32},{96,64},{1,97},{33,1},{65,33},{97,65},{2,98}... | collective-permute-start | bytes 3145736 | tf_op jit(solution)/shard_map/ppermute | solution.py:43
  18.3 57.7 %collective-permute-start.8 = (bf16[256,2048]{1,0:T(8,128)(2,1)}, bf16[256,2048]{1,0:T(8,128)(2,1)}, u32[]{:S(2)}, u32[]{:S(2)}) collective-permute-start(bf16[256,2048]{1,0:T(8,128)(2,1)} %bitcast.3.refs_3_.refs_9_), channel_id=1, source_target_pairs={{0,64},{32,96},{64,0},{96,32},{1,65},{33,97},{65,1},{97,33},{2,66}... | collective-permute-start | bytes 3145736 | tf_op jit(solution)/shard_map/ppermute | solution.py:43
  38.9 7.4 %collective-permute-start.2 = (bf16[4,32,512]{2,1,0:T(8,128)(2,1)S(1)}, bf16[4,32,512]{2,1,0:T(8,128)(2,1)S(1)}, u32[]{:S(2)}, u32[]{:S(2)}) collective-permute-start(bf16[4,32,512]{2,1,0:T(8,128)(2,1)S(1)} %collective-permute-done.refs_1_), channel_id=1, source_target_pairs={{0,128},{128,0},{1,129},{129,1},{2,130},{130,2},{3,131},{131,3},{4... | collective-permute-start | bytes 393224 | tf_op jit(solution)/shard_map/ppermute | solution.py:43
  64.2 24.6 %collective-permute-start.10 = (bf16[512,1024]{1,0:T(8,128)(2,1)S(1)}, bf16[512,1024]{1,0:T(8,128)(2,1)}, u32[]{:S(2)}, u32[]{:S(2)}) collective-permute-start(bf16[512,1024]{1,0:T(8,128)(2,1)S(1)} %get-tuple-element.77), channel_id=1, source_target_pairs={{0,8},{8,128},{128,136},{136,0},{1,9},{9,129},{129,137},{137,1},{2... | collective-permute-start | bytes 3145736 | tf_op jit(solution)/shard_map/ppermute | solution.py:43
  64.7 26.5 %collective-permute-start.11 = (bf16[512,1024]{1,0:T(8,128)(2,1)S(1)}, bf16[512,1024]{1,0:T(8,128)(2,1)}, u32[]{:S(2)}, u32[]{:S(2)}) collective-permute-start(bf16[512,1024]{1,0:T(8,128)(2,1)S(1)} %get-tuple-element.76), channel_id=1, source_target_pairs={{0,136},{8,0},{128,8},{136,128},{1,137},{9,1},{129,9},{137,129},{2... | collective-permute-start | bytes 3145736 | tf_op jit(solution)/shard_map/ppermute | solution.py:43
  67.0 34.7 %collective-permute-start.12 = (bf16[1024,1024]{1,0:T(8,128)(2,1)}, bf16[1024,1024]{1,0:T(8,128)(2,1)}, u32[]{:S(2)}, u32[]{:S(2)}) collective-permute-start(bf16[1024,1024]{1,0:T(8,128)(2,1)} %get-tuple-element.57.refs_1_.refs_4_), channel_id=1, source_target_pairs={{0,16},{16,0},{1,17},{17,1},{2,18},{18,2},{3,19},{19,3},{4,20},{20... | collective-permute-start | bytes 6291464 | tf_op jit(solution)/shard_map/ppermute | solution.py:43
  79.0 12.2 %collective-permute-start.9 = (bf16[1024,512]{1,0:T(8,128)(2,1)S(1)}, bf16[1024,512]{1,0:T(8,128)(2,1)S(1)}, u32[]{:S(2)}, u32[]{:S(2)}) collective-permute-start(bf16[1024,512]{1,0:T(8,128)(2,1)S(1)} %block_send.1), channel_id=1, source_target_pairs={{0,16},{16,0},{1,17},{17,1},{2,18},{18,2},{3,19},{19,3},{4,20},{20... | collective-permute-start | bytes 3145736 | tf_op jit(solution)/shard_map/ppermute | solution.py:43
  88.9 12.8 %collective-permute-start.13 = (bf16[512,1024]{1,0:T(8,128)(2,1)}, bf16[512,1024]{1,0:T(8,128)(2,1)}, u32[]{:S(2)}, u32[]{:S(2)}) collective-permute-start(bf16[512,1024]{1,0:T(8,128)(2,1)} %collective-permute-done.10.refs_2_.refs_5_), channel_id=1, source_target_pairs={{0,16},{16,0},{1,17},{17,1},{2,18},{18,2},{3,19},{19,3},{4,20},{20... | collective-permute-start | bytes 3145736 | tf_op jit(solution)/shard_map/ppermute | solution.py:43
  91.2 10.5 %collective-permute-start.14 = (bf16[512,1024]{1,0:T(8,128)(2,1)}, bf16[512,1024]{1,0:T(8,128)(2,1)}, u32[]{:S(2)}, u32[]{:S(2)}) collective-permute-start(bf16[512,1024]{1,0:T(8,128)(2,1)} %collective-permute-done.11.refs_3_.refs_6_), channel_id=1, source_target_pairs={{0,16},{16,0},{1,17},{17,1},{2,18},{18,2},{3,19},{19,3},{4,20},{20... | collective-permute-start | bytes 3145736 | tf_op jit(solution)/shard_map/ppermute | solution.py:43
  97.6 28.0 %all-to-all-start.1 = ((bf16[4,4,64,512]{3,2,1,0:T(8,128)(2,1)}), bf16[4,4,64,512]{3,2,1,0:T(8,128)(2,1)S(1)}, u32[]{:S(2)}, u32[]{:S(2)}) async-start(bf16[4,4,64,512]{3,2,1,0:T(8,128)(2,1)} %copy-done.9), calls=%async_computation.1 | async-start | bytes 2097152 | tf_op jit(solution)/shard_map/all_to_all | solution.py:389
  130.5 28.1 %all-to-all-start.2 = ((bf16[8,32,512]{2,1,0:T(8,128)(2,1)}), bf16[8,32,512]{2,1,0:T(8,128)(2,1)S(1)}, u32[]{:S(2)}, u32[]{:S(2)}) async-start(bf16[8,32,512]{2,1,0:T(8,128)(2,1)} %get-tuple-element.64), calls=%async_computation.2 | async-start | bytes 524288 | tf_op jit(solution)/shard_map/all_to_all | solution.py:407
  139.1 15.5 %collective-permute-start.24 = (bf16[256,512]{1,0:T(8,128)(2,1)S(1)}, bf16[256,512]{1,0:T(8,128)(2,1)S(1)}, u32[]{:S(2)}, u32[]{:S(2)}) collective-permute-start(bf16[256,512]{1,0:T(8,128)(2,1)S(1)} %copy-done.11), channel_id=1, source_target_pairs={{0,96},{32,0},{64,32},{96,64},{1,97},{33,1},{65,33},{97,65},{2,98}... | collective-permute-start | bytes 786440 | tf_op jit(solution)/shard_map/ppermute | solution.py:43
  140.1 15.5 %collective-permute-start.18 = (bf16[4,16,512]{2,1,0:T(8,128)(2,1)}, bf16[4,16,512]{2,1,0:T(8,128)(2,1)S(1)}, u32[]{:S(2)}, u32[]{:S(2)}) collective-permute-start(bf16[4,16,512]{2,1,0:T(8,128)(2,1)} %get-tuple-element.66), channel_id=1, source_target_pairs={{0,16},{16,0},{1,17},{17,1},{2,18},{18,2},{3,19},{19,3},{4,20},{20... | collective-permute-start | bytes 196616 | tf_op jit(solution)/shard_map/ppermute | solution.py:43
  142.1 15.2 %collective-permute-start.19 = (bf16[4,16,512]{2,1,0:T(8,128)(2,1)S(1)}, bf16[4,16,512]{2,1,0:T(8,128)(2,1)S(1)}, u32[]{:S(2)}, u32[]{:S(2)}) collective-permute-start(bf16[4,16,512]{2,1,0:T(8,128)(2,1)S(1)} %copy-done.30), channel_id=1, source_target_pairs={{0,128},{128,0},{1,129},{129,1},{2,130},{130,2},{3,131},{131,3},{4... | collective-permute-start | bytes 196616 | tf_op jit(solution)/shard_map/ppermute | solution.py:43
  142.9 14.5 %collective-permute-start.20 = (bf16[4,16,512]{2,1,0:T(8,128)(2,1)S(1)}, bf16[4,16,512]{2,1,0:T(8,128)(2,1)S(1)}, u32[]{:S(2)}, u32[]{:S(2)}) collective-permute-start(bf16[4,16,512]{2,1,0:T(8,128)(2,1)S(1)} %copy-done.28), channel_id=1, source_target_pairs={{0,144},{16,128},{128,16},{144,0},{1,145},{17,129},{129,17},{145,1... | collective-permute-start | bytes 196616 | tf_op jit(solution)/shard_map/ppermute | solution.py:406
  145.3 19.8 %collective-permute-start.25 = (bf16[256,512]{1,0:T(8,128)(2,1)S(1)}, bf16[256,512]{1,0:T(8,128)(2,1)S(1)}, u32[]{:S(2)}, u32[]{:S(2)}) collective-permute-start(bf16[256,512]{1,0:T(8,128)(2,1)S(1)} %copy-done.15), channel_id=1, source_target_pairs={{0,64},{32,96},{64,0},{96,32},{1,65},{33,97},{65,1},{97,33},{2,66}... | collective-permute-start | bytes 786440 | tf_op jit(solution)/shard_map/ppermute | solution.py:43
  154.7 12.6 %collective-permute-start.26 = (bf16[256,512]{1,0:T(8,128)(2,1)S(1)}, bf16[256,512]{1,0:T(8,128)(2,1)S(1)}, u32[]{:S(2)}, u32[]{:S(2)}) collective-permute-start(bf16[256,512]{1,0:T(8,128)(2,1)S(1)} %copy-done.13), channel_id=1, source_target_pairs={{0,32},{32,64},{64,96},{96,0},{1,33},{33,65},{65,97},{97,1},{2,34}... | collective-permute-start | bytes 786440 | tf_op jit(solution)/shard_map/ppermute | solution.py:43
  155.6 19.3 %collective-permute-start.21 = (bf16[256,512]{1,0:T(8,128)(2,1)S(1)}, bf16[256,512]{1,0:T(8,128)(2,1)S(1)}, u32[]{:S(2)}, u32[]{:S(2)}) collective-permute-start(bf16[256,512]{1,0:T(8,128)(2,1)S(1)} %get-tuple-element.70), channel_id=1, source_target_pairs={{0,96},{32,0},{64,32},{96,64},{1,97},{33,1},{65,33},{97,65},{2,98}... | collective-permute-start | bytes 786440 | tf_op jit(solution)/shard_map/ppermute | solution.py:43
  157.3 17.6 %collective-permute-start.22 = (bf16[256,512]{1,0:T(8,128)(2,1)}, bf16[256,512]{1,0:T(8,128)(2,1)S(1)}, u32[]{:S(2)}, u32[]{:S(2)}) collective-permute-start(bf16[256,512]{1,0:T(8,128)(2,1)} %copy-done.21), channel_id=1, source_target_pairs={{0,64},{32,96},{64,0},{96,32},{1,65},{33,97},{65,1},{97,33},{2,66}... | collective-permute-start | bytes 786440 | tf_op jit(solution)/shard_map/ppermute | solution.py:43
  158.1 20.2 %collective-permute-start.23 = (bf16[256,512]{1,0:T(8,128)(2,1)}, bf16[256,512]{1,0:T(8,128)(2,1)S(1)}, u32[]{:S(2)}, u32[]{:S(2)}) collective-permute-start(bf16[256,512]{1,0:T(8,128)(2,1)} %copy-done.18), channel_id=1, source_target_pairs={{0,32},{32,64},{64,96},{96,0},{1,33},{33,65},{65,97},{97,1},{2,34}... | collective-permute-start | bytes 786440 | tf_op jit(solution)/shard_map/ppermute | solution.py:43
  161.2 19.0 %all-to-all-start.3 = ((f32[4,24,512]{2,1,0:T(8,128)}), f32[4,24,512]{2,1,0:T(8,128)S(1)}, u32[]{:S(2)}, u32[]{:S(2)}) async-start(f32[4,24,512]{2,1,0:T(8,128)} %sum_z.1), calls=%async_computation.3 | async-start | bytes 393216 | tf_op jit(solution)/shard_map/all_to_all | solution.py:409
  (39 other events, 299.5 us)
Sparse Core Ops, SparseCore 0:
  10.9 41.1 all-gather.1

commit v3 on v2

v3 whole, which is shorter than its diff:
```python
import functools
import math

import jax
import jax.numpy as jnp
from jax import lax
from jax.experimental import pallas as pl
from jax.experimental.pallas import tpu as pltpu
from jax.sharding import Mesh, PartitionSpec as P

HD = 128
QC = 128
HEADS = 16
BLK = 64
TOK = 256
WIDTH = 2048
SCALE = 1.0 / math.sqrt(HD)
NEG = -1e30
BF = jnp.bfloat16
F32 = jnp.float32
CTX = ("yh", "x", "k")
AXES = ("yh", "x", "k", "yl", "z")
VMEM = pl.BlockSpec(memory_space=pltpu.VMEM)
SMEM = pl.BlockSpec(memory_space=pltpu.SMEM)

BLOCK = 256


def params(megabytes):
    return pltpu.CompilerParams(vmem_limit_bytes=megabytes << 20)


def cost(flops, size):
    return pl.CostEstimate(flops=flops, bytes_accessed=size, transcendentals=0)


def dot(a, b, ca, cb):
    return lax.dot_general(a, b, (((ca,), (cb,)), ((), ())), preferred_element_type=F32)


def shift(a, axis, by):
    n = lax.axis_size(axis)
    return lax.ppermute(a, axis, [(i, (i + by) % n) for i in range(n)])


class Info:
    def __init__(self, plan, lengths, blocks):
        self.x, self.k, self.yh, self.yl = (lax.axis_index(a) for a in ("x", "k", "yh", "yl"))
        self.start, self.width = plan[0, 0, 1], plan[0, 1, 1]
        self.lengths = [lengths[0, e] for e in range(2)]
        self.blocks = blocks


class Fetched:
    def __init__(self, src, dst, sem):
        self.copy = pltpu.make_async_copy(src, dst, sem)
        self.ref = dst
        self.copy.start()
        self.pending = True

    def __getitem__(self, at):
        self.ready()
        return self.ref[at]

    def ready(self):
        if self.pending:
            self.copy.wait()
            self.pending = False


def call(scalars, kernel, name, outs, args, flops, size, scratch=(), ties=(), picks=None, megabytes=48):
    n_in, n_out, n_tie = len(args), len(outs), len(ties)
    picks = picks or {}

    def body(plan, lengths, blocks, *refs):
        info = Info(plan, lengths, blocks)
        srcs, refs = refs[:n_in], refs[n_in + n_tie :]
        out_refs, refs = refs[:n_out], refs[n_out + n_tie :]
        bufs, sems, rest = refs[:n_in], refs[n_in], refs[n_in + 1 :]
        srcs = [picks[i][0](info, a) if i in picks else a for i, a in enumerate(srcs)]
        ins = [Fetched(a, b, sems.at[i]) for i, (a, b) in enumerate(zip(srcs, bufs))]
        kernel(info, *ins, *out_refs, *rest)
        for a in ins:
            a.ready()

    anywhere = pl.BlockSpec(memory_space=pl.ANY)
    return pl.pallas_call(
        body,
        in_specs=[SMEM] * 3 + [anywhere] * (n_in + n_tie),
        out_specs=[VMEM] * n_out + [anywhere] * n_tie,
        out_shape=[jax.ShapeDtypeStruct(shape, kind) for shape, kind in outs]
        + [jax.ShapeDtypeStruct(a.shape, a.dtype) for a in ties],
        scratch_shapes=[
            pltpu.VMEM(picks[i][1] if i in picks else a.shape, a.dtype) for i, a in enumerate(args)
        ]
        + [pltpu.SemaphoreType.DMA((n_in,))]
        + [pltpu.VMEM(shape, kind) for shape, kind in scratch],
        input_output_aliases={3 + n_in + i: n_out + i for i in range(n_tie)},
        compiler_params=params(megabytes),
        cost_estimate=cost(1, 1),
        name=name,
    )(*scalars, *args, *ties)


def in_one(info, n):
    c = info.yh * 8 + n
    return (c >= info.start) & (c < info.start + info.width)


def pack_kernel(info, k_ref, q_ref, g_ref, w_ref, out_ref, w_out):
    for b in range(4):
        at = pl.ds(pl.multiple_of(b * 512 + info.k * 256, 256), 256)
        w_out[:, b * 256 : (b + 1) * 256] = w_ref[:, at]
    row = lax.broadcasted_iota(jnp.int32, (16, BLOCK), 0)
    held = jnp.zeros((16, BLOCK), F32)
    for slot in range(TOK // BLK):
        held = jnp.where(row == slot, info.blocks[0, slot].astype(F32), held)
    for j in range(8):
        cols = slice(j * BLOCK, (j + 1) * BLOCK)
        out_ref[j, 256:272, :] = q_ref[:, cols]
        out_ref[j, 272:288, :] = g_ref[:, cols]
        out_ref[j, 288:304, :] = held.astype(BF)
        out_ref[j, 0:256, :] = k_ref[:, cols]


def unpack_kernel(info, pay, out_ref):
    out_ref[...] = pay[...]


def scores_kernel(info, own, far, p_ref, top_ref, ex_ref, qg_ref):
    for which in range(2):
        for i in range(8):
            rows = slice(i * 16, (i + 1) * 16)
            qg_ref[which, info.yh, rows, :] = own[i, 256 + which * 16 : 272 + which * 16, :]
            qg_ref[which, 1 - info.yh, rows, :] = far[i, which * 16 : (which + 1) * 16, :]
    row = lax.broadcasted_iota(jnp.int32, (BLK, QC), 0).astype(F32)
    col = lax.broadcasted_iota(jnp.int32, (BLK, QC), 1).astype(F32)
    tops, sums, ones = [], [], []
    for n in range(8):
        one = in_one(info, n)
        e = one.astype(jnp.int32)
        length = jnp.where(one, info.lengths[1], info.lengths[0]).astype(F32)
        held = own[n, 288:304, 0:QC].astype(F32)
        masks = []
        for slot in range(TOK // BLK):
            b = held[slot : slot + 1, :]
            masks.append((b >= 0.0) & (b * BLK + row <= length - QC + col))
        visible = jnp.concatenate(masks, axis=0)
        top_rows, sum_rows = [], []
        for hh in range(2):
            hs = slice(hh * HD, (hh + 1) * HD)
            masked = jnp.where(visible, dot(own[n, 0:256, hs], qg_ref[0, e, :, hs], 1, 1) * SCALE, NEG)
            top = jnp.max(masked, axis=0, keepdims=True)
            p = jnp.where(visible, jnp.exp(masked - top), 0.0)
            p_ref[n, :, hs] = p
            top_rows.append(top)
            sum_rows.append(jnp.sum(p, axis=0, keepdims=True))
        tops.append(jnp.concatenate(top_rows, axis=0))
        sums.append(jnp.concatenate(sum_rows, axis=0))
        ones.append(one)
        top_ref[n] = tops[n]
    for e in range(2):
        of_e = [one if e else jnp.logical_not(one) for one in ones]
        top = jnp.full((2, QC), NEG, F32)
        for n in range(8):
            top = jnp.maximum(top, jnp.where(of_e[n], tops[n], NEG))
        total = jnp.zeros((2, QC), F32)
        for n in range(8):
            total = total + jnp.where(of_e[n], sums[n] * jnp.exp(tops[n] - top), 0.0)
        ex_ref[0, e] = top
        ex_ref[1, e] = total


def probs_kernel(info, qg_ref, p_ref, top_ref, x0, x1, vg_ref, fac_ref):
    tops, invs = [], []
    for e in range(2):
        top = jnp.maximum(x0[0, e], x1[0, e])
        total = x0[1, e] * jnp.exp(x0[0, e] - top) + x1[1, e] * jnp.exp(x1[0, e] - top)
        tops.append(top)
        invs.append(1.0 / total)
    for n in range(8):
        one = in_one(info, n)
        e = one.astype(jnp.int32)
        factor = jnp.exp(top_ref[n] - jnp.where(one, tops[1], tops[0])) * jnp.where(one, invs[1], invs[0])
        fac_ref[n] = factor
        for hh in range(2):
            hs = slice(hh * HD, (hh + 1) * HD)
            pr = (p_ref[n, :, hs] * factor[hh : hh + 1, :]).astype(BF)
            vg_ref[n, :, hs] = dot(pr, qg_ref[1, e, :, hs], 1, 0).astype(BF)


def ring_index(info, step, other):
    return lax.rem(info.x + step, 4) * 2 + (1 - info.k if other else info.k)


def early_kernel(info, vg, a0, a1, a2, b0, b1, b2, out_ref):
    for tile in range(8):
        cols = slice(tile * 256, (tile + 1) * 256)
        acc = jnp.zeros((256, BLOCK), F32)
        for other, refs in enumerate(((a0, a1, a2), (b0, b1, b2))):
            for step, c in zip((0, 3, 1), refs):
                acc = acc + dot(c[:, cols], vg[ring_index(info, step, other)], 0, 0)
        out_ref[cols, :] = acc


def late_kernel(info, acc_ref, vg, a_top, a_bot, b_top, b_bot, out_ref):
    for tile in range(8):
        cols = slice(tile * 256, (tile + 1) * 256)
        acc = acc_ref[cols, :]
        for other, (top, bot) in enumerate(((a_top, a_bot), (b_top, b_bot))):
            left = jnp.concatenate([top[:, cols], bot[:, cols]], axis=0)
            acc = acc + dot(left, vg[ring_index(info, 2, other)], 0, 0)
        for part in range(4):
            k, yl = part // 2, part % 2
            rows = acc[part * 64 : (part + 1) * 64].astype(BF)
            out_ref[(tile // 4) * 2 + yl, (tile % 4) * 2 + k] = rows


def sum_y_kernel(info, got_ref, out_ref):
    total = jnp.zeros((8, 8, 8, BLOCK), F32)
    for n in range(4):
        total = total + got_ref[n].astype(F32).reshape(8, 8, 8, BLOCK)
    for z in range(8):
        out_ref[z] = total[:, z].reshape(64, BLOCK).astype(BF)


def prods_kernel(info, w_ref, a0, b0, a1, b1, a2, b2, a3, a4, b3, b4, qg_ref, p_ref, fac_ref,
                 prod_ref, cross_ref):
    cross = [jnp.zeros((2, QC), F32) for _ in range(2)]
    turns = (
        (0, 0, (a0,)), (0, 1, (b0,)), (3, 0, (a1,)), (3, 1, (b1,)),
        (1, 0, (a2,)), (1, 1, (b2,)), (2, 0, (a3, a4)), (2, 1, (b3, b4)),
    )
    for step, other, cs in turns:
        n = ring_index(info, step, other)
        one = in_one(info, n)
        e = one.astype(jnp.int32)
        c = jnp.concatenate([c[...] for c in cs], axis=0)
        v = dot(c, w_ref[...], 1, 0).astype(BF)
        rows = []
        for hh in range(2):
            hs = slice(hh * HD, (hh + 1) * HD)
            prod = dot(v[:, hs], qg_ref[1, e, :, hs], 1, 1)
            prod_ref[n, :, hs] = prod
            pr = p_ref[n, :, hs] * fac_ref[n, hh : hh + 1, :]
            rows.append(jnp.sum(pr * prod, axis=0, keepdims=True))
        part = jnp.concatenate(rows, axis=0)
        cross[0] = cross[0] + jnp.where(one, 0.0, part)
        cross[1] = cross[1] + jnp.where(one, part, 0.0)
    for e in range(2):
        cross_ref[e] = cross[e]


def grads_kernel(info, qg_ref, p_ref, fac_ref, prod_ref, x0, x1, own, kg_ref, q_own, q_far, qp_buf):
    qp_buf[...] = jnp.zeros(qp_buf.shape, F32)
    deltas = [x0[e] + x1[e] for e in range(2)]
    for n in range(8):
        one = in_one(info, n)
        e = one.astype(jnp.int32)
        delta = jnp.where(one, deltas[1], deltas[0])
        for hh in range(2):
            hs = slice(hh * HD, (hh + 1) * HD)
            pr = p_ref[n, :, hs] * fac_ref[n, hh : hh + 1, :]
            ds = (pr * (prod_ref[n, :, hs] - delta[hh : hh + 1, :])).astype(BF)
            kg_ref[n, 32:288, hs] = (SCALE * dot(ds, qg_ref[0, e, :, hs], 1, 0)).astype(BF)
            qp_buf[e, :, hs] += dot(ds, own[n, 0:256, hs], 0, 0)
    for out, e in ((q_own, info.yh), (q_far, 1 - info.yh)):
        out[...] = (SCALE * qp_buf[e]).astype(BF).reshape(8, 16, BLOCK)


def join_kernel(got_ref, q0_ref, q1_ref, keys_ref, out_ref, got, q0, q1, rows_ref, sems):
    got, q0, q1 = (
        Fetched(a, b, sems.at[i]) for i, (a, b) in enumerate(((got_ref, got), (q0_ref, q0), (q1_ref, q1)))
    )
    total = jnp.zeros((64, BLOCK), F32)
    for n in range(8):
        total = total + got[n].astype(F32)
    for j in range(8):
        rows = total[j * 8 : (j + 1) * 8]
        high = rows.astype(BF)
        low = rows - high.astype(F32)
        rows_ref[j, 0:16, :] = jnp.concatenate([high.astype(F32), low], axis=0).astype(BF)
        rows_ref[j, 16:32, :] = (q0[j].astype(F32) + q1[j].astype(F32)).astype(BF)
    copy = pltpu.make_async_copy(rows_ref, out_ref.at[:, pl.ds(0, 32)], sems.at[3])
    copy.start()
    copy.wait()


def finish_kernel(info, got_ref, after, w_ref, q_ref, k_ref):
    for j in range(8):
        cols = slice(j * BLOCK, (j + 1) * BLOCK)
        rows = got_ref[j, 0:16, :].astype(F32)
        w_ref[:, cols] = rows[0:8] + rows[8:16]
        q_ref[:, cols] = got_ref[j, 16:32, :]
        k_ref[:, cols] = got_ref[j, 32:288, :]


def context_kernel(info, home, w_own, w_oth, out_ref):
    left = [
        jnp.concatenate([home[b * 2 + k] for b in range(4)], axis=1) for k in (info.k, 1 - info.k)
    ]
    for t in range(4):
        rows = slice(t * 512, (t + 1) * 512)
        out_ref[:, rows] = (dot(left[0], w_own[rows, :], 1, 1) + dot(left[1], w_oth[rows, :], 1, 1)).astype(BF)


def halves_kernel(info, after, m1, p1, m1_out, p1_out):
    m1_out[...] = m1[...]
    p1_out[...] = p1[...]


def on_device(queries, grad_out, keys, context, value_weight, plan, lengths, blocks):
    keys, context = keys[0], context[0]
    run = functools.partial(call, (plan, lengths, blocks))
    ring = ("x", "k")

    pay, w_own = run(
        pack_kernel, "pack", [((8, 304, BLOCK), BF), ((128, 1024), BF)],
        [keys, queries[0], grad_out[0], value_weight], 1, 3, megabytes=60,
    )
    w_own = lax.all_gather(w_own, ("yl", "z"), axis=0, tiled=True)
    pay = lax.all_to_all(pay, ring, 0, 0)
    (rows,) = run(
        unpack_kernel, "unpack", [((8, 32, BLOCK), BF)], [pay], 1, 1,
        picks={0: (lambda info, r: r.at[:, pl.ds(256, 32)], (8, 32, BLOCK))},
    )
    far = shift(rows, "yh", 1)

    c_m1, c_p1 = shift(context, "x", 1), shift(context, "x", -1)

    unit = (8, TOK, BLOCK)
    p, tops, ex, qg = run(
        scores_kernel, "scores",
        [(unit, F32), ((8, 2, QC), F32), ((2, 2, 2, QC), F32), ((2, 2, QC, BLOCK), BF)],
        [pay, far], 134, 4,
    )
    m1_top, p1_bot = run(
        halves_kernel, "halves", [((128, WIDTH), BF)] * 2, [tops, c_m1, c_p1], 1, 3,
        picks={
            1: (lambda info, r: r.at[pl.ds(0, 128)], (128, WIDTH)),
            2: (lambda info, r: r.at[pl.ds(128, 128)], (128, WIDTH)),
        },
    )
    c_own = [context, c_m1, c_p1, shift(m1_top, "x", 1), shift(p1_bot, "x", -1)]
    c_oth = [shift(c, "k", 1) for c in c_own]

    vg, fac = run(
        probs_kernel, "probs", [(unit, BF), ((8, 2, QC), F32)],
        [qg, p, tops, ex, shift(ex, "yh", 1)], 134, 4,
    )
    home = lax.all_to_all(vg, ring, 0, 0)
    (acc,) = run(
        early_kernel, "block_early", [((WIDTH, BLOCK), F32)], [vg] + c_own[:3] + c_oth[:3], 1600, 8,
    )
    pieces, home = run(
        late_kernel, "block_late", [((4, 8, 64, BLOCK), BF)], [acc, vg] + c_own[3:] + c_oth[3:], 540, 4,
        ties=[home],
    )

    got = lax.all_to_all(pieces, ("yh", "yl"), 0, 0)
    pairs = [c for both in zip(c_own[:3], c_oth[:3]) for c in both]
    prods, cross = run(
        prods_kernel, "prods", [(unit, F32), ((2, 2, QC), F32)],
        [w_own] + pairs + c_own[3:] + c_oth[3:] + [qg, p, fac], 2300, 10,
        picks={0: (lambda info, r: r.at[:, pl.ds(pl.multiple_of(info.x * 256, 256), 256)], (WIDTH, BLOCK))},
    )
    z_in, cross, w_own = run(
        sum_y_kernel, "sum_y", [((8, 64, BLOCK), BF)], [got], 1, 2, ties=[cross, w_own], megabytes=60,
    )
    z_out = lax.all_to_all(z_in, "z", 0, 0)
    key_part, q_own, q_far = run(
        grads_kernel, "grads", [((8, 288, BLOCK), BF), ((8, 16, BLOCK), BF), ((8, 16, BLOCK), BF)],
        [qg, p, fac, prods, cross, shift(cross, "yh", 1), pay], 270, 6, [((2, QC, BLOCK), F32)],
    )
    anywhere = pl.BlockSpec(memory_space=pl.ANY)
    rows = (8, 16, BLOCK)
    joined = pl.pallas_call(
        join_kernel,
        in_specs=[anywhere] * 4,
        out_specs=anywhere,
        out_shape=jax.ShapeDtypeStruct((8, 288, BLOCK), BF),
        scratch_shapes=[pltpu.VMEM(shape, BF) for shape in ((8, 64, BLOCK), rows, rows, (8, 32, BLOCK))]
        + [pltpu.SemaphoreType.DMA((4,))],
        input_output_aliases={3: 0},
        compiler_params=params(60),
        cost_estimate=cost(1, 1),
        name="join",
    )(z_out, q_own, shift(q_far, "yh", 1), key_part)
    joined = lax.all_to_all(joined, ring, 0, 0)
    (context_grad,) = run(
        context_kernel, "context_grad", [((TOK, WIDTH), BF)], [home, w_own, shift(w_own, "k", 1)], 2200, 10,
    )
    weight_grad, query_grad, key_grad = run(
        finish_kernel, "finish", [((8, WIDTH), F32), ((16, WIDTH), BF), ((TOK, WIDTH), BF)], [joined, context_grad], 1, 3,
        picks={1: (lambda info, r: r.at[pl.ds(0, 16), pl.ds(0, 128)], (16, 128))},
    )
    return (query_grad[None], key_grad[None], context_grad[None], weight_grad)


def solution(mesh):
    fine = Mesh(mesh.devices.reshape(2, 4, 2, 2, 8), AXES)
    fsdp = ("yl", "z")
    rows = P(fsdp, CTX, None)
    return jax.shard_map(
        on_device,
        mesh=fine,
        in_specs=(rows, rows, rows, rows, P(fsdp, None), P(fsdp, None, None), P(fsdp, None), P(fsdp, CTX)),
        out_specs=(rows, rows, rows, P(AXES, None)),
        check_vma=False,
    )
```

time: 189 us -> 173 us (0.915)
  starting transfers between devices: 71.5 us -> 56 us
  local copies, waits for them, and re-layouts: 17.8 us -> 9.82 us
  waiting for transfers between devices: 37.1 us -> 41.9 us
  Pallas kernels: 47.6 us -> 50.6 us
    ppermute x26 -> x14, starting transfers between devices: 47.7 us -> 26.5 us  [shift(): return lax.ppermute(a, axis, [(i, (i + by) % n) for i in range(n)])]
    all_to_all x2 -> x3, waiting for transfers between devices: 11.2 us -> 22.7 us  [the longest x1 14.6 us: on_device(): pay = lax.all_to_all(pay, ring, 0, 0)]
    all_to_all x2 -> x3, starting transfers between devices: 8.78 us -> 17.9 us  [the longest x1 6.72 us: on_device(): pay = lax.all_to_all(pay, ring, 0, 0)]
    ppermute x26 -> x14, waiting for transfers between devices: 25.9 us -> 19.2 us  [shift(): return lax.ppermute(a, axis, [(i, (i + by) % n) for i in range(n)])]
    unnamed x62 -> x44, local copies, waits for them, and re-layouts: 13.9 us -> 9.82 us
    slice x4 -> x0, local copies, waits for them, and re-layouts: 3.25 us -> none  [the longest x1 2.55 us: on_device(): w_ob = shift(w_oo[512:], ('yh', 'yl'), -1)]
    ppermute x1 -> x0, starting transfers between devices: 2.36 us -> none  [on_device(): lax.ppermute(q_ky, ('yh', 'k'), both)]
    pallas_call x13 -> x12, Pallas kernels: 47.6 us -> 48.8 us  [call(): pl.pallas_call(body, in_specs=[SMEM] * 3 + [anywhere] * (n_in + n_tie), o...]
  transfers between devices with their start and end apart: 32 -> 20, of which waited for: 12 -> 7; matrix products, arithmetic and copies ran while one was open for 1% -> 0% of each run, Pallas kernels for 23% -> 24%
where the time goes in v3:
time: 173 us
  starting transfers between devices  56 us (32%)
  Pallas kernels  50.6 us (29%)
  waiting for transfers between devices  41.9 us (24%)
  between operations  14.4 us (8%)
  local copies, waits for them, and re-layouts  9.82 us (6%)
    pallas_call x12, Pallas kernels, call(): pl.pallas_call(body, in_specs=[SMEM] * 3 + [anywhere] * (n_in + n_tie), o...  48.8 us
    ppermute x14, starting transfers between devices, shift(): return lax.ppermute(a, axis, [(i, (i + by) % n) for i in range(n)])  26.5 us
    ppermute x14, waiting for transfers between devices, shift(): return lax.ppermute(a, axis, [(i, (i + by) % n) for i in range(n)])  19.2 us
    all_to_all x1, waiting for transfers between devices, on_device(): pay = lax.all_to_all(pay, ring, 0, 0)  14.6 us
    unnamed x44, local copies, waits for them, and re-layouts  9.82 us
    all_to_all x1, waiting for transfers between devices, on_device(): joined = lax.all_to_all(joined, ring, 0, 0)  7.84 us
    all_to_all x1, starting transfers between devices, on_device(): z_out = lax.all_to_all(z_in, 'z', 0, 0)  7.27 us
    all_to_all x1, starting transfers between devices, on_device(): pay = lax.all_to_all(pay, ring, 0, 0)  6.72 us
  transfers between devices with their start and end apart: 20, of which 7 were waited for; matrix products, arithmetic and copies ran while one was open for 0% of the time, Pallas kernels for 24%

profile of v3, /device:TPU:1, one launch (start us, length us, event | category | flops | bytes accessed | tf_op | source)
XLA Modules:
  0.0 172.7 jit_solution(45439971448933401)
XLA Ops:
  7.3 3.5 %pack.1 = (bf16[8,304,256]{2,1,0:T(8,128)(2,1)}, bf16[128,1024]{1,0:T(8,128)(2,1)}) custom-call(s32[1,2,2]{2,1,0:T(2,128)} %plan.23, s32[1,2]{1,0:T(1,128)} %lengths.23, s32[1,4]{1,0:T(1,128)} %blocks.23, bf16[256,2048]{1,0:T(8,128)(2,1)} %bitcast.13, bf16[16,2048]{1,0:T(8,128)(2,1)} %bitcast.14, bf16[16,2048]{1,0:T(8,128)(2,1)} %bitcast.15, ...), custom_call_target="tpu_custom_call" | custom-call | flops 1 | bytes 1 | tf_op jit(solution)/shard_map/pack/pallas_call | solution.py:87
  10.8 6.7 %all-to-all-start = ((bf16[8,304,256]{2,1,0:T(8,128)(2,1)}), bf16[8,304,256]{2,1,0:T(8,128)(2,1)S(1)}, u32[]{:S(2)}, u32[]{:S(2)}) async-start(bf16[8,304,256]{2,1,0:T(8,128)(2,1)} %get-tuple-element.27), calls=%async_computation | async-start | bytes 2490368 | tf_op jit(solution)/shard_map/all_to_all | solution.py:322
  20.2 14.6 %all-to-all-done.refs_0_.refs_6_ = bf16[8,304,256]{2,1,0:T(8,128)(2,1)S(1)} async-done(((bf16[8,304,256]{2,1,0:T(8,128)(2,1)}), bf16[8,304,256]{2,1,0:T(8,128)(2,1)S(1)}, u32[]{:S(2)}, u32[]{:S(2)}) %all-to-all-start) | async-done | bytes 1245216 | tf_op jit(solution)/shard_map/all_to_all | solution.py:322
  37.4 10.8 %collective-permute-done.refs_1_ = bf16[8,32,256]{2,1,0:T(8,128)(2,1)S(1)} collective-permute-done((bf16[8,32,256]{2,1,0:T(8,128)(2,1)S(1)}, bf16[8,32,256]{2,1,0:T(8,128)(2,1)S(1)}, u32[]{:S(2)}, u32[]{:S(2)}) %collective-permute-start) | collective-permute-done | bytes 131104 | tf_op jit(solution)/shard_map/ppermute | solution.py:43
  50.4 2.8 %collective-permute-start.1 = (f32[2,2,2,128]{3,2,1,0:T(2,128)S(1)}, f32[2,2,2,128]{3,2,1,0:T(2,128)S(1)}, u32[]{:S(2)}, u32[]{:S(2)}) collective-permute-start(f32[2,2,2,128]{3,2,1,0:T(2,128)S(1)} %get-tuple-element.31.refs_3_), channel_id=1, source_target_pairs={{0,128},{128,0},{1,129},{129,1},{2,130},{130,2},{3,131},{131,3},{4... | collective-permute-start | bytes 12296 | tf_op jit(solution)/shard_map/ppermute | solution.py:43
  53.2 4.0 %collective-permute-start.4 = (bf16[256,2048]{1,0:T(8,128)(2,1)S(1)}, bf16[256,2048]{1,0:T(8,128)(2,1)}, u32[]{:S(2)}, u32[]{:S(2)}) collective-permute-start(bf16[256,2048]{1,0:T(8,128)(2,1)S(1)} %bitcast.9), channel_id=1, source_target_pairs={{0,16},{16,0},{1,17},{17,1},{2,18},{18,2},{3,19},{19,3},{4,20},{20... | collective-permute-start | bytes 3145736 | tf_op jit(solution)/shard_map/ppermute | solution.py:43
  57.9 2.8 %halves.1 = (bf16[128,2048]{1,0:T(8,128)(2,1)}, bf16[128,2048]{1,0:T(8,128)(2,1)}) custom-call(s32[1,2,2]{2,1,0:T(2,128)S(1)} %copy-done.12, s32[1,2]{1,0:T(1,128)S(1)} %copy-done.14, s32[1,4]{1,0:T(1,128)S(1)} %copy-done.16, f32[8,2,128]{2,1,0:T(2,128)S(1)} %get-tuple-element.30.refs_2_.refs_0_, ...), custom_call_target="tpu_custom_call" | custom-call | flops 1 | bytes 1 | tf_op jit(solution)/shard_map/halves/pallas_call | solution.py:87
  60.8 2.7 %collective-permute-start.8 = (bf16[128,2048]{1,0:T(8,128)(2,1)}, bf16[128,2048]{1,0:T(8,128)(2,1)}, u32[]{:S(2)}, u32[]{:S(2)}) collective-permute-start(bf16[128,2048]{1,0:T(8,128)(2,1)} %get-tuple-element.34), channel_id=1, source_target_pairs={{0,96},{32,0},{64,32},{96,64},{1,97},{33,1},{65,33},{97,65},{2,98}... | collective-permute-start | bytes 1572872 | tf_op jit(solution)/shard_map/ppermute | solution.py:43
  63.4 2.2 %probs.1 = (bf16[8,256,256]{2,1,0:T(8,128)(2,1)}, f32[8,2,128]{2,1,0:T(2,128)S(1)}) custom-call(s32[1,2,2]{2,1,0:T(2,128)S(1)} %copy-done.12, s32[1,2]{1,0:T(1,128)S(1)} %copy-done.14, s32[1,4]{1,0:T(1,128)S(1)} %copy-done.16, bf16[2,2,128,256]{3,2,1,0:T(8,128)(2,1)S(1)} %get-tuple-element.28.refs_0_.refs_11_, ...), custom_call_target="tpu_custom_call" | custom-call | flops 1 | bytes 1 | tf_op jit(solution)/shard_map/probs/pallas_call | solution.py:87
  65.7 4.5 %all-to-all-start.1 = ((bf16[8,256,256]{2,1,0:T(8,128)(2,1)}), bf16[8,256,256]{2,1,0:T(8,128)(2,1)S(1)}, u32[]{:S(2)}, u32[]{:S(2)}) async-start(bf16[8,256,256]{2,1,0:T(8,128)(2,1)} %get-tuple-element.32.refs_0_.refs_1_), calls=%async_computation.1 | async-start | bytes 2097152 | tf_op jit(solution)/shard_map/all_to_all | solution.py:351
  70.2 5.5 %collective-permute-done.7.refs_2_.refs_7_ = bf16[128,2048]{1,0:T(8,128)(2,1)} collective-permute-done((bf16[128,2048]{1,0:T(8,128)(2,1)}, bf16[128,2048]{1,0:T(8,128)(2,1)}, u32[]{:S(2)}, u32[]{:S(2)}) %collective-permute-start.7) | collective-permute-done | bytes 524320 | tf_op jit(solution)/shard_map/ppermute | solution.py:43
  75.8 3.2 %collective-permute-start.9 = (bf16[128,2048]{1,0:T(8,128)(2,1)}, bf16[128,2048]{1,0:T(8,128)(2,1)}, u32[]{:S(2)}, u32[]{:S(2)}) collective-permute-start(bf16[128,2048]{1,0:T(8,128)(2,1)} %collective-permute-done.7.refs_2_.refs_7_), channel_id=1, source_target_pairs={{0,16},{16,0},{1,17},{17,1},{2,18},{18,2},{3,19},{19,3},{4,20},{20... | collective-permute-start | bytes 1572872 | tf_op jit(solution)/shard_map/ppermute | solution.py:43
  79.0 6.6 %block_early.1.refs_0_ = f32[2048,256]{1,0:T(8,128)} custom-call(s32[1,2,2]{2,1,0:T(2,128)S(1)} %copy-done.12, s32[1,2]{1,0:T(1,128)S(1)} %copy-done.14, s32[1,4]{1,0:T(1,128)S(1)} %copy-done.16, bf16[8,256,256]{2,1,0:T(8,128)(2,1)} %get-tuple-element.32.refs_0_.refs_1_, bf16[256,2048]{1,0:T(8,128)(2,1)S(1)} %bitcast.10, ...), custom_call_target="tpu_custom_call" | custom-call | flops 1 | bytes 1 | tf_op jit(solution)/shard_map/block_early/pallas_call | solution.py:87
  86.0 3.8 %block_late.1 = (bf16[4,8,64,256]{3,2,1,0:T(8,128)(2,1)S(1)}, bf16[8,256,256]{2,1,0:T(8,128)(2,1)S(1)}) custom-call(s32[1,2,2]{2,1,0:T(2,128)S(1)} %copy-done.12, s32[1,2]{1,0:T(1,128)S(1)} %copy-done.14, s32[1,4]{1,0:T(1,128)S(1)} %copy-done.16, f32[2048,256]{1,0:T(8,128)} %block_early.1.refs_0_, ...), custom_call_target="tpu_custom_call", output_to_operand_aliasing={{1}: (9, {})} | custom-call | flops 1 | bytes 1 | tf_op jit(solution)/shard_map/block_late/pallas_call | solution.py:87
  90.7 4.2 %all-to-all-start.2 = ((bf16[4,8,64,256]{3,2,1,0:T(8,128)(2,1)}), bf16[4,8,64,256]{3,2,1,0:T(8,128)(2,1)}, u32[]{:S(2)}, u32[]{:S(2)}) async-start(bf16[4,8,64,256]{3,2,1,0:T(8,128)(2,1)} %copy-done.11), calls=%async_computation.2 | async-start | bytes 2097152 | tf_op jit(solution)/shard_map/all_to_all | solution.py:360
  96.0 12.4 %prods.1 = (f32[8,256,256]{2,1,0:T(8,128)}, f32[2,2,128]{2,1,0:T(2,128)S(1)}) custom-call(s32[1,2,2]{2,1,0:T(2,128)S(1)} %copy-done.12, s32[1,2]{1,0:T(1,128)S(1)} %copy-done.14, s32[1,4]{1,0:T(1,128)S(1)} %copy-done.16, bf16[2048,1024]{1,0:T(8,128)(2,1)} %all-gather.2.cloned.1.call-done.refs_0_.refs_2_, bf16[256,2048]{1,0:T(8,128)(2,1)S(1)} %bitcast.11, ...), custom_call_target="tpu_custom_call" | custom-call | flops 1 | bytes 1 | tf_op jit(solution)/shard_map/prods/pallas_call | solution.py:87
  109.0 2.9 %sum_y.1 = (bf16[8,64,256]{2,1,0:T(8,128)(2,1)}, f32[2,2,128]{2,1,0:T(2,128)}, bf16[2048,1024]{1,0:T(8,128)(2,1)}) custom-call(s32[1,2,2]{2,1,0:T(2,128)} %plan.23, s32[1,2]{1,0:T(1,128)} %lengths.23, s32[1,4]{1,0:T(1,128)} %blocks.23, bf16[4,8,64,256]{3,2,1,0:T(8,128)(2,1)} %all-to-all-done.2.refs_0_, ...), custom_call_target="tpu_custom_call", output_to_operand_aliasing={{1}: (4, {}), {2}: (5, {})} | custom-call | flops 1 | bytes 1 | tf_op jit(solution)/shard_map/sum_y/pallas_call | solution.py:87
  114.1 7.3 %all-to-all-start.3 = ((bf16[8,64,256]{2,1,0:T(8,128)(2,1)}), bf16[8,64,256]{2,1,0:T(8,128)(2,1)}, u32[]{:S(2)}, u32[]{:S(2)}) async-start(bf16[8,64,256]{2,1,0:T(8,128)(2,1)} %get-tuple-element.39), calls=%async_computation.3 | async-start | bytes 524288 | tf_op jit(solution)/shard_map/all_to_all | solution.py:370
  121.4 3.2 %collective-permute-start.11 = (f32[2,2,128]{2,1,0:T(2,128)}, f32[2,2,128]{2,1,0:T(2,128)S(1)}, u32[]{:S(2)}, u32[]{:S(2)}) collective-permute-start(f32[2,2,128]{2,1,0:T(2,128)} %get-tuple-element.41.refs_4_), channel_id=1, source_target_pairs={{0,128},{128,0},{1,129},{129,1},{2,130},{130,2},{3,131},{131,3},{4... | collective-permute-start | bytes 6152 | tf_op jit(solution)/shard_map/ppermute | solution.py:43
  127.4 3.4 %grads.1 = (bf16[8,288,256]{2,1,0:T(8,128)(2,1)S(1)}, bf16[8,16,256]{2,1,0:T(8,128)(2,1)S(1)}, bf16[8,16,256]{2,1,0:T(8,128)(2,1)S(1)}) custom-call(s32[1,2,2]{2,1,0:T(2,128)S(1)} %copy-done.13, s32[1,2]{1,0:T(1,128)S(1)} %copy-done.15, s32[1,4]{1,0:T(1,128)S(1)} %copy-done.17, bf16[2,2,128,256]{3,2,1,0:T(8,128)(2,1)S(1)} %copy-done.10, ...), custom_call_target="tpu_custom_call" | custom-call | flops 1 | bytes 1 | tf_op jit(solution)/shard_map/grads/pallas_call | solution.py:87
  132.4 3.0 %collective-permute-start.12 = (bf16[8,16,256]{2,1,0:T(8,128)(2,1)S(1)}, bf16[8,16,256]{2,1,0:T(8,128)(2,1)S(1)}, u32[]{:S(2)}, u32[]{:S(2)}) collective-permute-start(bf16[8,16,256]{2,1,0:T(8,128)(2,1)S(1)} %get-tuple-element.43), channel_id=1, source_target_pairs={{0,128},{128,0},{1,129},{129,1},{2,130},{130,2},{3,131},{131,3},{4... | collective-permute-start | bytes 196616 | tf_op jit(solution)/shard_map/ppermute | solution.py:43
  139.5 6.6 %all-to-all-start.4 = ((bf16[8,288,256]{2,1,0:T(8,128)(2,1)}), bf16[8,288,256]{2,1,0:T(8,128)(2,1)S(1)}, u32[]{:S(2)}, u32[]{:S(2)}) async-start(bf16[8,288,256]{2,1,0:T(8,128)(2,1)} %join.1), calls=%async_computation.4 | async-start | bytes 2359296 | tf_op jit(solution)/shard_map/all_to_all | solution.py:389
  148.3 6.5 %context_grad.1.refs_1_ = bf16[256,2048]{1,0:T(8,128)(2,1)} custom-call(s32[1,2,2]{2,1,0:T(2,128)S(1)} %copy-done.13, s32[1,2]{1,0:T(1,128)S(1)} %copy-done.15, s32[1,4]{1,0:T(1,128)S(1)} %copy-done.17, bf16[8,256,256]{2,1,0:T(8,128)(2,1)S(1)} %copy-done.4, bf16[2048,1024]{1,0:T(8,128)(2,1)S(1)} %copy-done, bf16[2048,1024]{1,0:T(8,128)(2,1)} %collective-permute-done.13.refs_2_), custom_call_target="tpu_custom_call" | custom-call | flops 1 | bytes 1 | tf_op jit(solution)/shard_map/context_grad/pallas_call | solution.py:87
  154.8 7.8 %all-to-all-done.4.refs_0_ = bf16[8,288,256]{2,1,0:T(8,128)(2,1)S(1)} async-done(((bf16[8,288,256]{2,1,0:T(8,128)(2,1)}), bf16[8,288,256]{2,1,0:T(8,128)(2,1)S(1)}, u32[]{:S(2)}, u32[]{:S(2)}) %all-to-all-start.4) | async-done | bytes 1179680 | tf_op jit(solution)/shard_map/all_to_all | solution.py:389
  (74 shorter events, 27.3 us)
Async XLA Ops:
  7.2 87.8 %all-gather.2.cloned.1.call-start = ((), (), s32[]{:S(2)}) async-start(), calls=%async_computation.5 | async-start | bytes 4456448 | tf_op jit(solution)/shard_map/all_gather | solution.py:321
  7.2 27.5 %copy-start.12 = (s32[1,2,2]{2,1,0:T(2,128)S(1)}, s32[1,2,2]{2,1,0:T(2,128)}, u32[]{:S(2)}) copy-start(s32[1,2,2]{2,1,0:T(2,128)} %plan.23) | copy-start | bytes 52
  7.2 27.5 %copy-start.14 = (s32[1,2]{1,0:T(1,128)S(1)}, s32[1,2]{1,0:T(1,128)}, u32[]{:S(2)}) copy-start(s32[1,2]{1,0:T(1,128)} %lengths.23) | copy-start | bytes 28
  7.2 27.5 %copy-start.16 = (s32[1,4]{1,0:T(1,128)S(1)}, s32[1,4]{1,0:T(1,128)}, u32[]{:S(2)}) copy-start(s32[1,4]{1,0:T(1,128)} %blocks.23) | copy-start | bytes 52
  10.8 24.0 %all-to-all-start = ((bf16[8,304,256]{2,1,0:T(8,128)(2,1)}), bf16[8,304,256]{2,1,0:T(8,128)(2,1)S(1)}, u32[]{:S(2)}, u32[]{:S(2)}) async-start(bf16[8,304,256]{2,1,0:T(8,128)(2,1)} %get-tuple-element.27), calls=%async_computation | async-start | bytes 2490368 | tf_op jit(solution)/shard_map/all_to_all | solution.py:322
  17.5 39.8 %collective-permute-start.2 = (bf16[256,2048]{1,0:T(8,128)(2,1)S(1)}, bf16[256,2048]{1,0:T(8,128)(2,1)}, u32[]{:S(2)}, u32[]{:S(2)}) collective-permute-start(bf16[256,2048]{1,0:T(8,128)(2,1)S(1)} %bitcast.7), channel_id=1, source_target_pairs={{0,32},{32,64},{64,96},{96,0},{1,33},{33,65},{65,97},{97,1},{2,34}... | collective-permute-start | bytes 3145736 | tf_op jit(solution)/shard_map/ppermute | solution.py:43
  18.9 39.0 %collective-permute-start.3 = (bf16[256,2048]{1,0:T(8,128)(2,1)S(1)}, bf16[256,2048]{1,0:T(8,128)(2,1)}, u32[]{:S(2)}, u32[]{:S(2)}) collective-permute-start(bf16[256,2048]{1,0:T(8,128)(2,1)S(1)} %bitcast.8), channel_id=1, source_target_pairs={{0,96},{32,0},{64,32},{96,64},{1,97},{33,1},{65,33},{97,65},{2,98}... | collective-permute-start | bytes 3145736 | tf_op jit(solution)/shard_map/ppermute | solution.py:43
  35.4 12.9 %collective-permute-start = (bf16[8,32,256]{2,1,0:T(8,128)(2,1)S(1)}, bf16[8,32,256]{2,1,0:T(8,128)(2,1)S(1)}, u32[]{:S(2)}, u32[]{:S(2)}) collective-permute-start(bf16[8,32,256]{2,1,0:T(8,128)(2,1)S(1)} %unpack.1), channel_id=1, source_target_pairs={{0,128},{128,0},{1,129},{129,1},{2,130},{130,2},{3,131},{131,3},{4... | collective-permute-start | bytes 393224 | tf_op jit(solution)/shard_map/ppermute | solution.py:43
  50.4 10.4 %collective-permute-start.1 = (f32[2,2,2,128]{3,2,1,0:T(2,128)S(1)}, f32[2,2,2,128]{3,2,1,0:T(2,128)S(1)}, u32[]{:S(2)}, u32[]{:S(2)}) collective-permute-start(f32[2,2,2,128]{3,2,1,0:T(2,128)S(1)} %get-tuple-element.31.refs_3_), channel_id=1, source_target_pairs={{0,128},{128,0},{1,129},{129,1},{2,130},{130,2},{3,131},{131,3},{4... | collective-permute-start | bytes 12296 | tf_op jit(solution)/shard_map/ppermute | solution.py:43
  53.2 25.8 %collective-permute-start.4 = (bf16[256,2048]{1,0:T(8,128)(2,1)S(1)}, bf16[256,2048]{1,0:T(8,128)(2,1)}, u32[]{:S(2)}, u32[]{:S(2)}) collective-permute-start(bf16[256,2048]{1,0:T(8,128)(2,1)S(1)} %bitcast.9), channel_id=1, source_target_pairs={{0,16},{16,0},{1,17},{17,1},{2,18},{18,2},{3,19},{19,3},{4,20},{20... | collective-permute-start | bytes 3145736 | tf_op jit(solution)/shard_map/ppermute | solution.py:43
  57.2 21.8 %collective-permute-start.5 = (bf16[256,2048]{1,0:T(8,128)(2,1)}, bf16[256,2048]{1,0:T(8,128)(2,1)}, u32[]{:S(2)}, u32[]{:S(2)}) collective-permute-start(bf16[256,2048]{1,0:T(8,128)(2,1)} %collective-permute-done.2.refs_2_.refs_1_.refs_3_), channel_id=1, source_target_pairs={{0,16},{16,0},{1,17},{17,1},{2,18},{18,2},{3,19},{19,3},{4,20},{20... | collective-permute-start | bytes 3145736 | tf_op jit(solution)/shard_map/ppermute | solution.py:43
  57.9 21.1 %collective-permute-start.6 = (bf16[256,2048]{1,0:T(8,128)(2,1)}, bf16[256,2048]{1,0:T(8,128)(2,1)}, u32[]{:S(2)}, u32[]{:S(2)}) collective-permute-start(bf16[256,2048]{1,0:T(8,128)(2,1)} %collective-permute-done.3.refs_3_.refs_2_.refs_5_), channel_id=1, source_target_pairs={{0,16},{16,0},{1,17},{17,1},{2,18},{18,2},{3,19},{19,3},{4,20},{20... | collective-permute-start | bytes 3145736 | tf_op jit(solution)/shard_map/ppermute | solution.py:43
  60.7 15.1 %collective-permute-start.7 = (bf16[128,2048]{1,0:T(8,128)(2,1)}, bf16[128,2048]{1,0:T(8,128)(2,1)}, u32[]{:S(2)}, u32[]{:S(2)}) collective-permute-start(bf16[128,2048]{1,0:T(8,128)(2,1)} %get-tuple-element.33), channel_id=1, source_target_pairs={{0,32},{32,64},{64,96},{96,0},{1,33},{33,65},{65,97},{97,1},{2,34}... | collective-permute-start | bytes 1572872 | tf_op jit(solution)/shard_map/ppermute | solution.py:43
  60.8 18.2 %collective-permute-start.8 = (bf16[128,2048]{1,0:T(8,128)(2,1)}, bf16[128,2048]{1,0:T(8,128)(2,1)}, u32[]{:S(2)}, u32[]{:S(2)}) collective-permute-start(bf16[128,2048]{1,0:T(8,128)(2,1)} %get-tuple-element.34), channel_id=1, source_target_pairs={{0,96},{32,0},{64,32},{96,64},{1,97},{33,1},{65,33},{97,65},{2,98}... | collective-permute-start | bytes 1572872 | tf_op jit(solution)/shard_map/ppermute | solution.py:43
  65.7 20.2 %all-to-all-start.1 = ((bf16[8,256,256]{2,1,0:T(8,128)(2,1)}), bf16[8,256,256]{2,1,0:T(8,128)(2,1)S(1)}, u32[]{:S(2)}, u32[]{:S(2)}) async-start(bf16[8,256,256]{2,1,0:T(8,128)(2,1)} %get-tuple-element.32.refs_0_.refs_1_), calls=%async_computation.1 | async-start | bytes 2097152 | tf_op jit(solution)/shard_map/all_to_all | solution.py:351
  75.8 10.2 %collective-permute-start.9 = (bf16[128,2048]{1,0:T(8,128)(2,1)}, bf16[128,2048]{1,0:T(8,128)(2,1)}, u32[]{:S(2)}, u32[]{:S(2)}) collective-permute-start(bf16[128,2048]{1,0:T(8,128)(2,1)} %collective-permute-done.7.refs_2_.refs_7_), channel_id=1, source_target_pairs={{0,16},{16,0},{1,17},{17,1},{2,18},{18,2},{3,19},{19,3},{4,20},{20... | collective-permute-start | bytes 1572872 | tf_op jit(solution)/shard_map/ppermute | solution.py:43
  79.0 7.0 %collective-permute-start.10 = (bf16[128,2048]{1,0:T(8,128)(2,1)}, bf16[128,2048]{1,0:T(8,128)(2,1)}, u32[]{:S(2)}, u32[]{:S(2)}) collective-permute-start(bf16[128,2048]{1,0:T(8,128)(2,1)} %collective-permute-done.8.refs_3_.refs_8_), channel_id=1, source_target_pairs={{0,16},{16,0},{1,17},{17,1},{2,18},{18,2},{3,19},{19,3},{4,20},{20... | collective-permute-start | bytes 1572872 | tf_op jit(solution)/shard_map/ppermute | solution.py:43
  90.7 17.7 %copy-start.3 = (bf16[8,256,256]{2,1,0:T(8,128)(2,1)}, bf16[8,256,256]{2,1,0:T(8,128)(2,1)S(1)}, u32[]{:S(2)}) copy-start(bf16[8,256,256]{2,1,0:T(8,128)(2,1)S(1)} %get-tuple-element.45.refs_0_) | copy-start | bytes 3145732
  90.7 18.3 %all-to-all-start.2 = ((bf16[4,8,64,256]{3,2,1,0:T(8,128)(2,1)}), bf16[4,8,64,256]{3,2,1,0:T(8,128)(2,1)}, u32[]{:S(2)}, u32[]{:S(2)}) async-start(bf16[4,8,64,256]{3,2,1,0:T(8,128)(2,1)} %copy-done.11), calls=%async_computation.2 | async-start | bytes 2097152 | tf_op jit(solution)/shard_map/all_to_all | solution.py:360
  111.9 34.2 %collective-permute-start.13 = (bf16[2048,1024]{1,0:T(8,128)(2,1)}, bf16[2048,1024]{1,0:T(8,128)(2,1)}, u32[]{:S(2)}, u32[]{:S(2)}) collective-permute-start(bf16[2048,1024]{1,0:T(8,128)(2,1)} %get-tuple-element.46.refs_1_), channel_id=1, source_target_pairs={{0,16},{16,0},{1,17},{17,1},{2,18},{18,2},{3,19},{19,3},{4,20},{20... | collective-permute-start | bytes 12582920 | tf_op jit(solution)/shard_map/ppermute | solution.py:43
  114.1 22.9 %all-to-all-start.3 = ((bf16[8,64,256]{2,1,0:T(8,128)(2,1)}), bf16[8,64,256]{2,1,0:T(8,128)(2,1)}, u32[]{:S(2)}, u32[]{:S(2)}) async-start(bf16[8,64,256]{2,1,0:T(8,128)(2,1)} %get-tuple-element.39), calls=%async_computation.3 | async-start | bytes 524288 | tf_op jit(solution)/shard_map/all_to_all | solution.py:370
  121.4 4.4 %collective-permute-start.11 = (f32[2,2,128]{2,1,0:T(2,128)}, f32[2,2,128]{2,1,0:T(2,128)S(1)}, u32[]{:S(2)}, u32[]{:S(2)}) collective-permute-start(f32[2,2,128]{2,1,0:T(2,128)} %get-tuple-element.41.refs_4_), channel_id=1, source_target_pairs={{0,128},{128,0},{1,129},{129,1},{2,130},{130,2},{3,131},{131,3},{4... | collective-permute-start | bytes 6152 | tf_op jit(solution)/shard_map/ppermute | solution.py:43
  132.4 4.6 %collective-permute-start.12 = (bf16[8,16,256]{2,1,0:T(8,128)(2,1)S(1)}, bf16[8,16,256]{2,1,0:T(8,128)(2,1)S(1)}, u32[]{:S(2)}, u32[]{:S(2)}) collective-permute-start(bf16[8,16,256]{2,1,0:T(8,128)(2,1)S(1)} %get-tuple-element.43), channel_id=1, source_target_pairs={{0,128},{128,0},{1,129},{129,1},{2,130},{130,2},{3,131},{131,3},{4... | collective-permute-start | bytes 196616 | tf_op jit(solution)/shard_map/ppermute | solution.py:43
  139.5 23.2 %all-to-all-start.4 = ((bf16[8,288,256]{2,1,0:T(8,128)(2,1)}), bf16[8,288,256]{2,1,0:T(8,128)(2,1)S(1)}, u32[]{:S(2)}, u32[]{:S(2)}) async-start(bf16[8,288,256]{2,1,0:T(8,128)(2,1)} %join.1), calls=%async_computation.4 | async-start | bytes 2359296 | tf_op jit(solution)/shard_map/all_to_all | solution.py:389
  (18 other events, 126.0 us)
Sparse Core Ops, SparseCore 0:
  10.9 71.9 all-gather.1

commit v4 on v3

--- a/solution.py
+++ b/solution.py
@@ -68,17 +68,24 @@
             self.pending = False
 
 
-def call(scalars, kernel, name, outs, args, flops, size, scratch=(), ties=(), picks=None, megabytes=48):
+def call(scalars, kernel, name, outs, args, flops, size, scratch=(), ties=(), picks=None, stack=(), megabytes=48):
     n_in, n_out, n_tie = len(args), len(outs), len(ties)
     picks = picks or {}
+    plain = [i for i in range(n_in) if i not in stack]
+    tall = sum(args[i].shape[0] for i in stack)
 
     def body(plan, lengths, blocks, *refs):
         info = Info(plan, lengths, blocks)
         srcs, refs = refs[:n_in], refs[n_in + n_tie :]
         out_refs, refs = refs[:n_out], refs[n_out + n_tie :]
-        bufs, sems, rest = refs[:n_in], refs[n_in], refs[n_in + 1 :]
+        bufs, refs = dict(zip(plain, refs)), refs[len(plain) :]
+        sems, rest = refs[0], refs[1:]
+        at = 0
+        for i in stack:
+            bufs[i] = rest[0].at[pl.ds(at, args[i].shape[0])]
+            at += args[i].shape[0]
         srcs = [picks[i][0](info, a) if i in picks else a for i, a in enumerate(srcs)]
-        ins = [Fetched(a, b, sems.at[i]) for i, (a, b) in enumerate(zip(srcs, bufs))]
+        ins = [Fetched(a, bufs[i], sems.at[i]) for i, a in enumerate(srcs)]
         kernel(info, *ins, *out_refs, *rest)
         for a in ins:
             a.ready()
@@ -91,9 +98,10 @@
         out_shape=[jax.ShapeDtypeStruct(shape, kind) for shape, kind in outs]
         + [jax.ShapeDtypeStruct(a.shape, a.dtype) for a in ties],
         scratch_shapes=[
-            pltpu.VMEM(picks[i][1] if i in picks else a.shape, a.dtype) for i, a in enumerate(args)
+            pltpu.VMEM(picks[i][1] if i in picks else args[i].shape, args[i].dtype) for i in plain
         ]
         + [pltpu.SemaphoreType.DMA((n_in,))]
+        + ([pltpu.VMEM((tall, args[stack[0]].shape[1]), args[stack[0]].dtype)] if stack else [])
         + [pltpu.VMEM(shape, kind) for shape, kind in scratch],
         input_output_aliases={3 + n_in + i: n_out + i for i in range(n_tie)},
         compiler_params=params(megabytes),
@@ -193,7 +201,8 @@
     return lax.rem(info.x + step, 4) * 2 + (1 - info.k if other else info.k)
 
 
-def early_kernel(info, vg, a0, a1, a2, b0, b1, b2, out_ref):
+def early_kernel(info, vg, a0, a1, a2, b0, b1, b2, out_ref, mark_ref):
+    mark_ref[...] = jnp.zeros(mark_ref.shape, F32)
     for tile in range(8):
         cols = slice(tile * 256, (tile + 1) * 256)
         acc = jnp.zeros((256, BLOCK), F32)
@@ -225,18 +234,19 @@
 
 
 def prods_kernel(info, w_ref, a0, b0, a1, b1, a2, b2, a3, a4, b3, b4, qg_ref, p_ref, fac_ref,
-                 prod_ref, cross_ref):
+                 prod_ref, cross_ref, c_buf, v_buf):
     cross = [jnp.zeros((2, QC), F32) for _ in range(2)]
+    for c in (a0, b0, a1, b1, a2, b2, a3, a4, b3, b4):
+        c.ready()
+    v_buf[...] = dot(c_buf[...], w_ref[...], 1, 0).astype(BF)
     turns = (
-        (0, 0, (a0,)), (0, 1, (b0,)), (3, 0, (a1,)), (3, 1, (b1,)),
-        (1, 0, (a2,)), (1, 1, (b2,)), (2, 0, (a3, a4)), (2, 1, (b3, b4)),
-    )
-    for step, other, cs in turns:
+        (0, 0), (0, 1), (3, 0), (3, 1), (1, 0), (1, 1), (2, 0), (2, 1),
+    )
+    for at, (step, other) in enumerate(turns):
         n = ring_index(info, step, other)
         one = in_one(info, n)
         e = one.astype(jnp.int32)
-        c = jnp.concatenate([c[...] for c in cs], axis=0)
-        v = dot(c, w_ref[...], 1, 0).astype(BF)
+        v = v_buf[at * TOK : (at + 1) * TOK, :]
         rows = []
         for hh in range(2):
             hs = slice(hh * HD, (hh + 1) * HD)
@@ -251,10 +261,11 @@
         cross_ref[e] = cross[e]
 
 
-def grads_kernel(info, qg_ref, p_ref, fac_ref, prod_ref, x0, x1, own, kg_ref, q_own, q_far, qp_buf):
+def grads_kernel(info, qg_ref, p_ref, fac_ref, prod_ref, x0, x1, own, g0, g1, g2, g3, q_own, q_far, qp_buf):
     qp_buf[...] = jnp.zeros(qp_buf.shape, F32)
     deltas = [x0[e] + x1[e] for e in range(2)]
-    for n in range(8):
+    for step, k in ((step, k) for step in range(4) for k in range(2)):
+        n = lax.rem(info.x + step, 4) * 2 + k
         one = in_one(info, n)
         e = one.astype(jnp.int32)
         delta = jnp.where(one, deltas[1], deltas[0])
@@ -262,37 +273,43 @@
             hs = slice(hh * HD, (hh + 1) * HD)
             pr = p_ref[n, :, hs] * fac_ref[n, hh : hh + 1, :]
             ds = (pr * (prod_ref[n, :, hs] - delta[hh : hh + 1, :])).astype(BF)
-            kg_ref[n, 32:288, hs] = (SCALE * dot(ds, qg_ref[0, e, :, hs], 1, 0)).astype(BF)
+            (g0, g1, g2, g3)[step][k, :, hs] = (SCALE * dot(ds, qg_ref[0, e, :, hs], 1, 0)).astype(BF)
             qp_buf[e, :, hs] += dot(ds, own[n, 0:256, hs], 0, 0)
     for out, e in ((q_own, info.yh), (q_far, 1 - info.yh)):
         out[...] = (SCALE * qp_buf[e]).astype(BF).reshape(8, 16, BLOCK)
 
 
-def join_kernel(got_ref, q0_ref, q1_ref, keys_ref, out_ref, got, q0, q1, rows_ref, sems):
-    got, q0, q1 = (
-        Fetched(a, b, sems.at[i]) for i, (a, b) in enumerate(((got_ref, got), (q0_ref, q0), (q1_ref, q1)))
-    )
+def turn_kernel(info, g0, g1, g2, g3, keep_ref, send_ref):
+    for step, g in enumerate((g0, g1, g2, g3)):
+        keep_ref[step] = g[info.k]
+        send_ref[step] = g[1 - info.k]
+
+
+def key_kernel(info, keep, got, out_ref):
+    for step in range(4):
+        for other, part in enumerate((keep, got)):
+            at = ring_index(info, 4 - step, other) * BLOCK
+            out_ref[:, pl.ds(pl.multiple_of(at, BLOCK), BLOCK)] = part[step]
+
+
+def join_kernel(info, got_ref, q0, q1, out_ref):
     total = jnp.zeros((64, BLOCK), F32)
     for n in range(8):
-        total = total + got[n].astype(F32)
+        total = total + got_ref[n].astype(F32)
     for j in range(8):
-        rows = total[j * 8 : (j + 1) * 8]
-        high = rows.astype(BF)
-        low = rows - high.astype(F32)
-        rows_ref[j, 0:16, :] = jnp.concatenate([high.astype(F32), low], axis=0).astype(BF)
-        rows_ref[j, 16:32, :] = (q0[j].astype(F32) + q1[j].astype(F32)).astype(BF)
-    copy = pltpu.make_async_copy(rows_ref, out_ref.at[:, pl.ds(0, 32)], sems.at[3])
-    copy.start()
-    copy.wait()
-
-
-def finish_kernel(info, got_ref, after, w_ref, q_ref, k_ref):
+        out_ref[j, 0:8, :] = total[j * 8 : (j + 1) * 8]
+        out_ref[j, 8:24, :] = q0[j].astype(F32) + q1[j].astype(F32)
+
+
+def finish_kernel(info, got_ref, after, after_too, w_ref, q_ref):
     for j in range(8):
         cols = slice(j * BLOCK, (j + 1) * BLOCK)
-        rows = got_ref[j, 0:16, :].astype(F32)
-        w_ref[:, cols] = rows[0:8] + rows[8:16]
-        q_ref[:, cols] = got_ref[j, 16:32, :]
-        k_ref[:, cols] = got_ref[j, 32:288, :]
+        w_ref[:, cols] = got_ref[j, 0:8, :]
+        q_ref[:, cols] = got_ref[j, 8:24, :].astype(BF)
+
+
+def after_kernel(info, a, out_ref):
+    out_ref[...] = a[...]
 
 
 def context_kernel(info, home, w_own, w_oth, out_ref):
@@ -304,9 +321,17 @@
         out_ref[:, rows] = (dot(left[0], w_own[rows, :], 1, 1) + dot(left[1], w_oth[rows, :], 1, 1)).astype(BF)
 
 
-def halves_kernel(info, after, m1, p1, m1_out, p1_out):
-    m1_out[...] = m1[...]
-    p1_out[...] = p1[...]
+def halves_kernel(after, m1, p1, top_ref, bot_ref, m1_out, p1_out, top, bot, sems):
+    copies = [
+        pltpu.make_async_copy(m1.at[pl.ds(0, 128)], top, sems.at[0]),
+        pltpu.make_async_copy(p1.at[pl.ds(128, 128)], bot, sems.at[1]),
+    ]
+    for c in copies:
+        c.start()
+    for c in copies:
+        c.wait()
+    top_ref[...] = top[...]
+    bot_ref[...] = bot[...]
 
 
 def on_device(queries, grad_out, keys, context, value_weight, plan, lengths, blocks):
@@ -334,24 +359,35 @@
         [(unit, F32), ((8, 2, QC), F32), ((2, 2, 2, QC), F32), ((2, 2, QC, BLOCK), BF)],
         [pay, far], 134, 4,
     )
-    m1_top, p1_bot = run(
-        halves_kernel, "halves", [((128, WIDTH), BF)] * 2, [tops, c_m1, c_p1], 1, 3,
-        picks={
-            1: (lambda info, r: r.at[pl.ds(0, 128)], (128, WIDTH)),
-            2: (lambda info, r: r.at[pl.ds(128, 128)], (128, WIDTH)),
-        },
-    )
+    ex_far = shift(ex, "yh", 1)
+    anywhere = pl.BlockSpec(memory_space=pl.ANY)
+    half = jax.ShapeDtypeStruct((128, WIDTH), BF)
+    whole = jax.ShapeDtypeStruct((TOK, WIDTH), BF)
+    m1_top, p1_bot, c_m1, c_p1 = pl.pallas_call(
+        halves_kernel,
+        in_specs=[anywhere] * 3,
+        out_specs=[VMEM, VMEM, anywhere, anywhere],
+        out_shape=[half, half, whole, whole],
+        scratch_shapes=[pltpu.VMEM((128, WIDTH), BF)] * 2 + [pltpu.SemaphoreType.DMA((2,))],
+        input_output_aliases={1: 2, 2: 3},
+        compiler_params=params(60),
+        cost_estimate=cost(1, 1),
+        name="halves",
+    )(ex_far, c_m1, c_p1)
     c_own = [context, c_m1, c_p1, shift(m1_top, "x", 1), shift(p1_bot, "x", -1)]
-    c_oth = [shift(c, "k", 1) for c in c_own]
+    c_oth = [shift(c, "k", 1) for c in c_own[:3]]
 
     vg, fac = run(
         probs_kernel, "probs", [(unit, BF), ((8, 2, QC), F32)],
-        [qg, p, tops, ex, shift(ex, "yh", 1)], 134, 4,
+        [qg, p, tops, ex, ex_far], 134, 4,
     )
     home = lax.all_to_all(vg, ring, 0, 0)
-    (acc,) = run(
-        early_kernel, "block_early", [((WIDTH, BLOCK), F32)], [vg] + c_own[:3] + c_oth[:3], 1600, 8,
-    )
+    acc, mark = run(
+        early_kernel, "block_early", [((WIDTH, BLOCK), F32), ((8, 128), F32)], [vg] + c_own[:3] + c_oth[:3], 1600, 8,
+    )
+    _, c_2a, c_2b = run(after_kernel, "after", [((8, 128), F32)], [mark], 1, 1, ties=c_own[3:])
+    c_own[3:] = [c_2a, c_2b]
+    c_oth = c_oth + [shift(c_2a, "k", 1), shift(c_2b, "k", 1)]
     pieces, home = run(
         late_kernel, "block_late", [((4, 8, 64, BLOCK), BF)], [acc, vg] + c_own[3:] + c_oth[3:], 540, 4,
         ties=[home],
@@ -361,38 +397,36 @@
     pairs = [c for both in zip(c_own[:3], c_oth[:3]) for c in both]
     prods, cross = run(
         prods_kernel, "prods", [(unit, F32), ((2, 2, QC), F32)],
-        [w_own] + pairs + c_own[3:] + c_oth[3:] + [qg, p, fac], 2300, 10,
+        [w_own] + pairs + c_own[3:] + c_oth[3:] + [qg, p, fac], 2300, 10, [((WIDTH, BLOCK), BF)],
+        stack=tuple(range(1, 11)),
         picks={0: (lambda info, r: r.at[:, pl.ds(pl.multiple_of(info.x * 256, 256), 256)], (WIDTH, BLOCK))},
     )
-    z_in, cross, w_own = run(
-        sum_y_kernel, "sum_y", [((8, 64, BLOCK), BF)], [got], 1, 2, ties=[cross, w_own], megabytes=60,
+    g_0, g_1, g_2, g_3, q_own, q_far = run(
+        grads_kernel, "grads", [((2, TOK, BLOCK), BF)] * 4 + [((8, 16, BLOCK), BF)] * 2,
+        [qg, p, fac, prods, cross, shift(cross, "yh", 1), pay], 270, 6, [((2, QC, BLOCK), F32)],
+    )
+    z_in, q_own = run(
+        sum_y_kernel, "sum_y", [((8, 64, BLOCK), BF)], [got], 1, 2, ties=[q_own], megabytes=60,
     )
     z_out = lax.all_to_all(z_in, "z", 0, 0)
-    key_part, q_own, q_far = run(
-        grads_kernel, "grads", [((8, 288, BLOCK), BF), ((8, 16, BLOCK), BF), ((8, 16, BLOCK), BF)],
-        [qg, p, fac, prods, cross, shift(cross, "yh", 1), pay], 270, 6, [((2, QC, BLOCK), F32)],
-    )
-    anywhere = pl.BlockSpec(memory_space=pl.ANY)
-    rows = (8, 16, BLOCK)
-    joined = pl.pallas_call(
-        join_kernel,
-        in_specs=[anywhere] * 4,
-        out_specs=anywhere,
-        out_shape=jax.ShapeDtypeStruct((8, 288, BLOCK), BF),
-        scratch_shapes=[pltpu.VMEM(shape, BF) for shape in ((8, 64, BLOCK), rows, rows, (8, 32, BLOCK))]
-        + [pltpu.SemaphoreType.DMA((4,))],
-        input_output_aliases={3: 0},
-        compiler_params=params(60),
-        cost_estimate=cost(1, 1),
-        name="join",
-    )(z_out, q_own, shift(q_far, "yh", 1), key_part)
+    g_far = [shift(g_1, "x", 1), shift(g_2, "x", 2), shift(g_3, "x", -1)]
+    joined, w_own, *g_far = run(
+        join_kernel, "join", [((8, 24, BLOCK), F32)], [z_out, q_own, shift(q_far, "yh", 1)], 1, 1,
+        ties=[w_own, *g_far],
+    )
+    keep, send = run(
+        turn_kernel, "turn", [((4, TOK, BLOCK), BF)] * 2,
+        [g_0, *g_far], 1, 2,
+    )
+    (key_grad,) = run(key_kernel, "key_home", [((TOK, WIDTH), BF)], [keep, shift(send, "k", 1)], 1, 2)
+
     joined = lax.all_to_all(joined, ring, 0, 0)
     (context_grad,) = run(
         context_kernel, "context_grad", [((TOK, WIDTH), BF)], [home, w_own, shift(w_own, "k", 1)], 2200, 10,
     )
-    weight_grad, query_grad, key_grad = run(
-        finish_kernel, "finish", [((8, WIDTH), F32), ((16, WIDTH), BF), ((TOK, WIDTH), BF)], [joined, context_grad], 1, 3,
-        picks={1: (lambda info, r: r.at[pl.ds(0, 16), pl.ds(0, 128)], (16, 128))},
+    weight_grad, query_grad = run(
+        finish_kernel, "finish", [((8, WIDTH), F32), ((16, WIDTH), BF)], [joined, context_grad, key_grad], 1, 1,
+        picks={i: (lambda info, r: r.at[pl.ds(0, 16), pl.ds(0, 128)], (16, 128)) for i in (1, 2)},
     )
     return (query_grad[None], key_grad[None], context_grad[None], weight_grad)
 

time: 173 us -> 171 us (0.988)
  local copies, waits for them, and re-layouts: 9.82 us -> 5.94 us
    all_to_all x1, waiting for transfers between devices: 7.84 us -> 0.01 us  [on_device(): joined = lax.all_to_all(joined, ring, 0, 0)]
    all_to_all x1, waiting for transfers between devices: 0.3 us -> 5.8 us  [on_device(): home = lax.all_to_all(vg, ring, 0, 0)]
    unnamed x44 -> x38, local copies, waits for them, and re-layouts: 9.82 us -> 5.94 us
    ppermute x14 -> x18, waiting for transfers between devices: 19.2 us -> 22.6 us  [shift(): return lax.ppermute(a, axis, [(i, (i + by) % n) for i in range(n)])]
    all_to_all x1, starting transfers between devices: 6.65 us -> 4.39 us  [on_device(): joined = lax.all_to_all(joined, ring, 0, 0)]
    ppermute x14 -> x18, starting transfers between devices: 26.5 us -> 28.6 us  [shift(): return lax.ppermute(a, axis, [(i, (i + by) % n) for i in range(n)])]
    pallas_call x12 -> x15, Pallas kernels: 48.8 us -> 49.5 us  [call(): pl.pallas_call(body, in_specs=[SMEM] * 3 + [anywhere] * (n_in + n_tie), o...]
  transfers between devices with their start and end apart: 20 -> 24, of which waited for: 7 -> 9; matrix products, arithmetic and copies ran while one was open for 0% -> 0% of each run, Pallas kernels for 24% -> 25%
where the time goes in v4:
time: 171 us; the launch traced here: 170 us
  starting transfers between devices  55.2 us (32%)
  Pallas kernels  51.7 us (30%)
  waiting for transfers between devices  43 us (25%)
  between operations  14.4 us (8%)
  local copies, waits for them, and re-layouts  5.94 us (3%)
    pallas_call x15, Pallas kernels, call(): pl.pallas_call(body, in_specs=[SMEM] * 3 + [anywhere] * (n_in + n_tie), o...  49.5 us
    ppermute x18, starting transfers between devices, shift(): return lax.ppermute(a, axis, [(i, (i + by) % n) for i in range(n)])  28.6 us
    ppermute x18, waiting for transfers between devices, shift(): return lax.ppermute(a, axis, [(i, (i + by) % n) for i in range(n)])  22.6 us
    all_to_all x1, waiting for transfers between devices, on_device(): pay = lax.all_to_all(pay, ring, 0, 0)  14.6 us
    all_to_all x1, starting transfers between devices, on_device(): pay = lax.all_to_all(pay, ring, 0, 0)  6.72 us
    all_to_all x1, starting transfers between devices, on_device(): z_out = lax.all_to_all(z_in, 'z', 0, 0)  6.01 us
    unnamed x38, local copies, waits for them, and re-layouts  5.94 us
    all_to_all x1, waiting for transfers between devices, on_device(): home = lax.all_to_all(vg, ring, 0, 0)  5.8 us
  transfers between devices with their start and end apart: 24, of which 9 were waited for; matrix products, arithmetic and copies ran while one was open for 0% of the time, Pallas kernels for 25%

profile of v4, /device:TPU:1, one launch (start us, length us, event | category | flops | bytes accessed | tf_op | source)
XLA Modules:
  0.0 170.3 jit_solution(12523885987247187983)
XLA Ops:
  7.2 3.5 %pack.1 = (bf16[8,304,256]{2,1,0:T(8,128)(2,1)}, bf16[128,1024]{1,0:T(8,128)(2,1)}) custom-call(s32[1,2,2]{2,1,0:T(2,128)} %plan.29, s32[1,2]{1,0:T(1,128)} %lengths.29, s32[1,4]{1,0:T(1,128)} %blocks.29, bf16[256,2048]{1,0:T(8,128)(2,1)} %bitcast.9, bf16[16,2048]{1,0:T(8,128)(2,1)} %bitcast.10, bf16[16,2048]{1,0:T(8,128)(2,1)} %bitcast.11, ...), custom_call_target="tpu_custom_call" | custom-call | flops 1 | bytes 1 | tf_op jit(solution)/shard_map/pack/pallas_call | solution.py:94
  10.8 6.7 %all-to-all-start = ((bf16[8,304,256]{2,1,0:T(8,128)(2,1)}), bf16[8,304,256]{2,1,0:T(8,128)(2,1)S(1)}, u32[]{:S(2)}, u32[]{:S(2)}) async-start(bf16[8,304,256]{2,1,0:T(8,128)(2,1)} %get-tuple-element.41), calls=%async_computation | async-start | bytes 2490368 | tf_op jit(solution)/shard_map/all_to_all | solution.py:347
  20.2 14.6 %all-to-all-done.refs_0_.refs_6_ = bf16[8,304,256]{2,1,0:T(8,128)(2,1)S(1)} async-done(((bf16[8,304,256]{2,1,0:T(8,128)(2,1)}), bf16[8,304,256]{2,1,0:T(8,128)(2,1)S(1)}, u32[]{:S(2)}, u32[]{:S(2)}) %all-to-all-start) | async-done | bytes 1245216 | tf_op jit(solution)/shard_map/all_to_all | solution.py:347
  37.4 10.8 %collective-permute-done.refs_1_ = bf16[8,32,256]{2,1,0:T(8,128)(2,1)S(1)} collective-permute-done((bf16[8,32,256]{2,1,0:T(8,128)(2,1)S(1)}, bf16[8,32,256]{2,1,0:T(8,128)(2,1)S(1)}, u32[]{:S(2)}, u32[]{:S(2)}) %collective-permute-start) | collective-permute-done | bytes 131104 | tf_op jit(solution)/shard_map/ppermute | solution.py:43
  50.4 2.8 %collective-permute-start.1 = (f32[2,2,2,128]{3,2,1,0:T(2,128)S(1)}, f32[2,2,2,128]{3,2,1,0:T(2,128)S(1)}, u32[]{:S(2)}, u32[]{:S(2)}) collective-permute-start(f32[2,2,2,128]{3,2,1,0:T(2,128)S(1)} %get-tuple-element.45.refs_3_), channel_id=1, source_target_pairs={{0,128},{128,0},{1,129},{129,1},{2,130},{130,2},{3,131},{131,3},{4... | collective-permute-start | bytes 12296 | tf_op jit(solution)/shard_map/ppermute | solution.py:43
  53.2 4.0 %collective-permute-start.4 = (bf16[256,2048]{1,0:T(8,128)(2,1)}, bf16[256,2048]{1,0:T(8,128)(2,1)}, u32[]{:S(2)}, u32[]{:S(2)}) collective-permute-start(bf16[256,2048]{1,0:T(8,128)(2,1)} %bitcast.3.refs_1_), channel_id=1, source_target_pairs={{0,16},{16,0},{1,17},{17,1},{2,18},{18,2},{3,19},{19,3},{4,20},{20... | collective-permute-start | bytes 3145736 | tf_op jit(solution)/shard_map/ppermute | solution.py:43
  57.8 2.3 %halves.1 = (bf16[128,2048]{1,0:T(8,128)(2,1)}, bf16[128,2048]{1,0:T(8,128)(2,1)}, bf16[256,2048]{1,0:T(8,128)(2,1)}, bf16[256,2048]{1,0:T(8,128)(2,1)}) custom-call(f32[2,2,2,128]{3,2,1,0:T(2,128)} %copy-done.17, bf16[256,2048]{1,0:T(8,128)(2,1)} %collective-permute-done.2.m1, ...), custom_call_target="tpu_custom_call", output_to_operand_aliasing={{2}: (1, {}), {3}: (2, {})} | custom-call | flops 1 | bytes 1 | tf_op jit(solution)/shard_map/halves/pallas_call | solution.py:366
  61.9 2.7 %collective-permute-start.8 = (bf16[128,2048]{1,0:T(8,128)(2,1)}, bf16[128,2048]{1,0:T(8,128)(2,1)}, u32[]{:S(2)}, u32[]{:S(2)}) collective-permute-start(bf16[128,2048]{1,0:T(8,128)(2,1)} %get-tuple-element.52), channel_id=1, source_target_pairs={{0,96},{32,0},{64,32},{96,64},{1,97},{33,1},{65,33},{97,65},{2,98}... | collective-permute-start | bytes 1572872 | tf_op jit(solution)/shard_map/ppermute | solution.py:43
  67.5 4.6 %all-to-all-start.1 = ((bf16[8,256,256]{2,1,0:T(8,128)(2,1)}), bf16[8,256,256]{2,1,0:T(8,128)(2,1)S(1)}, u32[]{:S(2)}, u32[]{:S(2)}) async-start(bf16[8,256,256]{2,1,0:T(8,128)(2,1)} %copy-done.2), calls=%async_computation.1 | async-start | bytes 2097152 | tf_op jit(solution)/shard_map/all_to_all | solution.py:384
  72.1 6.8 %block_early.1 = (f32[2048,256]{1,0:T(8,128)}, f32[8,128]{1,0:T(8,128)S(1)}) custom-call(s32[1,2,2]{2,1,0:T(2,128)S(1)} %copy-done.11, s32[1,2]{1,0:T(1,128)S(1)} %copy-done.13, s32[1,4]{1,0:T(1,128)S(1)} %copy-done.15, bf16[8,256,256]{2,1,0:T(8,128)(2,1)S(1)} %copy-done.3, bf16[256,2048]{1,0:T(8,128)(2,1)} %bitcast.3.refs_1_, ...), custom_call_target="tpu_custom_call" | custom-call | flops 1 | bytes 1 | tf_op jit(solution)/shard_map/block_early/pallas_call | solution.py:94
  81.6 5.8 %all-to-all-done.1.refs_6_ = bf16[8,256,256]{2,1,0:T(8,128)(2,1)S(1)} async-done(((bf16[8,256,256]{2,1,0:T(8,128)(2,1)}), bf16[8,256,256]{2,1,0:T(8,128)(2,1)S(1)}, u32[]{:S(2)}, u32[]{:S(2)}) %all-to-all-start.1) | async-done | bytes 1048608 | tf_op jit(solution)/shard_map/all_to_all | solution.py:384
  87.4 3.5 %block_late.1 = (bf16[4,8,64,256]{3,2,1,0:T(8,128)(2,1)S(1)}, bf16[8,256,256]{2,1,0:T(8,128)(2,1)S(1)}) custom-call(s32[1,2,2]{2,1,0:T(2,128)S(1)} %copy-done.11, s32[1,2]{1,0:T(1,128)S(1)} %copy-done.13, s32[1,4]{1,0:T(1,128)S(1)} %copy-done.15, f32[2048,256]{1,0:T(8,128)} %get-tuple-element.49.refs_0_, ...), custom_call_target="tpu_custom_call", output_to_operand_aliasing={{1}: (9, {})} | custom-call | flops 1 | bytes 1 | tf_op jit(solution)/shard_map/block_late/pallas_call | solution.py:94
  91.9 4.9 %all-to-all-start.2 = ((bf16[4,8,64,256]{3,2,1,0:T(8,128)(2,1)}), bf16[4,8,64,256]{3,2,1,0:T(8,128)(2,1)}, u32[]{:S(2)}, u32[]{:S(2)}) async-start(bf16[4,8,64,256]{3,2,1,0:T(8,128)(2,1)} %copy-done.8), calls=%async_computation.2 | async-start | bytes 2097152 | tf_op jit(solution)/shard_map/all_to_all | solution.py:396
  96.8 9.9 %prods.1 = (f32[8,256,256]{2,1,0:T(8,128)}, f32[2,2,128]{2,1,0:T(2,128)S(1)}) custom-call(s32[1,2,2]{2,1,0:T(2,128)S(1)} %copy-done.11, s32[1,2]{1,0:T(1,128)S(1)} %copy-done.13, s32[1,4]{1,0:T(1,128)S(1)} %copy-done.15, bf16[2048,1024]{1,0:T(8,128)(2,1)} %all-gather.2.cloned.1.call-done.refs_0_.refs_3_, bf16[256,2048]{1,0:T(8,128)(2,1)} %bitcast.3.refs_1_, ...), custom_call_target="tpu_custom_call" | custom-call | flops 1 | bytes 1 | tf_op jit(solution)/shard_map/prods/pallas_call | solution.py:94
  106.6 3.1 %collective-permute-start.11 = (f32[2,2,128]{2,1,0:T(2,128)S(1)}, f32[2,2,128]{2,1,0:T(2,128)S(1)}, u32[]{:S(2)}, u32[]{:S(2)}) collective-permute-start(f32[2,2,128]{2,1,0:T(2,128)S(1)} %get-tuple-element.59.refs_4_), channel_id=1, source_target_pairs={{0,128},{128,0},{1,129},{129,1},{2,130},{130,2},{3,131},{131,3},{4... | collective-permute-start | bytes 6152 | tf_op jit(solution)/shard_map/ppermute | solution.py:43
  111.2 4.2 %grads.1 = (bf16[2,256,256]{2,1,0:T(8,128)(2,1)S(1)}, bf16[2,256,256]{2,1,0:T(8,128)(2,1)}, bf16[2,256,256]{2,1,0:T(8,128)(2,1)}, bf16[2,256,256]{2,1,0:T(8,128)...) custom-call(s32[1,2,2]{2,1,0:T(2,128)S(1)} %copy-done.11, s32[1,2]{1,0:T(1,128)S(1)} %copy-done.13, ...), custom_call_target="tpu_custom_call" | custom-call | flops 1 | bytes 1 | tf_op jit(solution)/shard_map/grads/pallas_call | solution.py:94
  116.0 2.8 %sum_y.1 = (bf16[8,64,256]{2,1,0:T(8,128)(2,1)}, bf16[8,16,256]{2,1,0:T(8,128)(2,1)}) custom-call(s32[1,2,2]{2,1,0:T(2,128)} %plan.29, s32[1,2]{1,0:T(1,128)} %lengths.29, s32[1,4]{1,0:T(1,128)} %blocks.29, bf16[4,8,64,256]{3,2,1,0:T(8,128)(2,1)} %all-to-all-done.2.refs_0_, bf16[8,16,256]{2,1,0:T(8,128)(2,1)} %copy-done.9), custom_call_target="tpu_custom_call", output_to_operand_aliasing={{1}: (4, {})} | custom-call | flops 1 | bytes 1 | tf_op jit(solution)/shard_map/sum_y/pallas_call | solution.py:94
  118.8 6.0 %all-to-all-start.3 = ((bf16[8,64,256]{2,1,0:T(8,128)(2,1)}), bf16[8,64,256]{2,1,0:T(8,128)(2,1)S(1)}, u32[]{:S(2)}, u32[]{:S(2)}) async-start(bf16[8,64,256]{2,1,0:T(8,128)(2,1)} %get-tuple-element.61), calls=%async_computation.3 | async-start | bytes 524288 | tf_op jit(solution)/shard_map/all_to_all | solution.py:411
  127.9 2.4 %collective-permute-start.12 = (bf16[8,16,256]{2,1,0:T(8,128)(2,1)S(1)}, bf16[8,16,256]{2,1,0:T(8,128)(2,1)S(1)}, u32[]{:S(2)}, u32[]{:S(2)}) collective-permute-start(bf16[8,16,256]{2,1,0:T(8,128)(2,1)S(1)} %get-tuple-element.63), channel_id=1, source_target_pairs={{0,128},{128,0},{1,129},{129,1},{2,130},{130,2},{3,131},{131,3},{4... | collective-permute-start | bytes 196616 | tf_op jit(solution)/shard_map/ppermute | solution.py:43
  130.3 2.2 %collective-permute-done.12.refs_2_ = bf16[8,16,256]{2,1,0:T(8,128)(2,1)S(1)} collective-permute-done((bf16[8,16,256]{2,1,0:T(8,128)(2,1)S(1)}, bf16[8,16,256]{2,1,0:T(8,128)(2,1)S(1)}, u32[]{:S(2)}, u32[]{:S(2)}) %collective-permute-start.12) | collective-permute-done | bytes 65568 | tf_op jit(solution)/shard_map/ppermute | solution.py:43
  135.1 3.8 %collective-permute-done.15.refs_6_ = bf16[2,256,256]{2,1,0:T(8,128)(2,1)S(1)} collective-permute-done((bf16[2,256,256]{2,1,0:T(8,128)(2,1)}, bf16[2,256,256]{2,1,0:T(8,128)(2,1)S(1)}, u32[]{:S(2)}, u32[]{:S(2)}) %collective-permute-start.15) | collective-permute-done | bytes 262176 | tf_op jit(solution)/shard_map/ppermute | solution.py:43
  141.3 2.3 %collective-permute-start.16 = (bf16[2048,1024]{1,0:T(8,128)(2,1)}, bf16[2048,1024]{1,0:T(8,128)(2,1)}, u32[]{:S(2)}, u32[]{:S(2)}) collective-permute-start(bf16[2048,1024]{1,0:T(8,128)(2,1)} %get-tuple-element.69.refs_1_), channel_id=1, source_target_pairs={{0,16},{16,0},{1,17},{17,1},{2,18},{18,2},{3,19},{19,3},{4,20},{20... | collective-permute-start | bytes 12582920 | tf_op jit(solution)/shard_map/ppermute | solution.py:43
  145.3 4.4 %all-to-all-start.4 = ((f32[8,24,256]{2,1,0:T(8,128)}), f32[8,24,256]{2,1,0:T(8,128)S(1)}, u32[]{:S(2)}, u32[]{:S(2)}) async-start(f32[8,24,256]{2,1,0:T(8,128)} %get-tuple-element.67), calls=%async_computation.4 | async-start | bytes 393216 | tf_op jit(solution)/shard_map/all_to_all | solution.py:423
  153.2 7.5 %context_grad.1.refs_1_ = bf16[256,2048]{1,0:T(8,128)(2,1)} custom-call(s32[1,2,2]{2,1,0:T(2,128)S(1)} %copy-done.12, s32[1,2]{1,0:T(1,128)S(1)} %copy-done.14, s32[1,4]{1,0:T(1,128)S(1)} %copy-done.16, bf16[8,256,256]{2,1,0:T(8,128)(2,1)S(1)} %get-tuple-element.68.refs_0_, bf16[2048,1024]{1,0:T(8,128)(2,1)} %get-tuple-element.69.refs_1_, ...), custom_call_target="tpu_custom_call" | custom-call | flops 1 | bytes 1 | tf_op jit(solution)/shard_map/context_grad/pallas_call | solution.py:94
  (79 shorter events, 34.5 us)
Async XLA Ops:
  7.2 89.6 %all-gather.2.cloned.1.call-start = ((), (), s32[]{:S(2)}) async-start(), calls=%async_computation.5 | async-start | bytes 4456448 | tf_op jit(solution)/shard_map/all_gather | solution.py:346
  10.8 24.0 %all-to-all-start = ((bf16[8,304,256]{2,1,0:T(8,128)(2,1)}), bf16[8,304,256]{2,1,0:T(8,128)(2,1)S(1)}, u32[]{:S(2)}, u32[]{:S(2)}) async-start(bf16[8,304,256]{2,1,0:T(8,128)(2,1)} %get-tuple-element.41), calls=%async_computation | async-start | bytes 2490368 | tf_op jit(solution)/shard_map/all_to_all | solution.py:347
  17.5 39.8 %collective-permute-start.2 = (bf16[256,2048]{1,0:T(8,128)(2,1)}, bf16[256,2048]{1,0:T(8,128)(2,1)}, u32[]{:S(2)}, u32[]{:S(2)}) collective-permute-start(bf16[256,2048]{1,0:T(8,128)(2,1)} %bitcast.3.refs_1_), channel_id=1, source_target_pairs={{0,32},{32,64},{64,96},{96,0},{1,33},{33,65},{65,97},{97,1},{2,34}... | collective-permute-start | bytes 3145736 | tf_op jit(solution)/shard_map/ppermute | solution.py:43
  18.9 38.4 %collective-permute-start.3 = (bf16[256,2048]{1,0:T(8,128)(2,1)}, bf16[256,2048]{1,0:T(8,128)(2,1)}, u32[]{:S(2)}, u32[]{:S(2)}) collective-permute-start(bf16[256,2048]{1,0:T(8,128)(2,1)} %bitcast.3.refs_1_), channel_id=1, source_target_pairs={{0,96},{32,0},{64,32},{96,64},{1,97},{33,1},{65,33},{97,65},{2,98}... | collective-permute-start | bytes 3145736 | tf_op jit(solution)/shard_map/ppermute | solution.py:43
  35.4 12.9 %collective-permute-start = (bf16[8,32,256]{2,1,0:T(8,128)(2,1)S(1)}, bf16[8,32,256]{2,1,0:T(8,128)(2,1)S(1)}, u32[]{:S(2)}, u32[]{:S(2)}) collective-permute-start(bf16[8,32,256]{2,1,0:T(8,128)(2,1)S(1)} %unpack.1), channel_id=1, source_target_pairs={{0,128},{128,0},{1,129},{129,1},{2,130},{130,2},{3,131},{131,3},{4... | collective-permute-start | bytes 393224 | tf_op jit(solution)/shard_map/ppermute | solution.py:43
  50.4 6.8 %collective-permute-start.1 = (f32[2,2,2,128]{3,2,1,0:T(2,128)S(1)}, f32[2,2,2,128]{3,2,1,0:T(2,128)S(1)}, u32[]{:S(2)}, u32[]{:S(2)}) collective-permute-start(f32[2,2,2,128]{3,2,1,0:T(2,128)S(1)} %get-tuple-element.45.refs_3_), channel_id=1, source_target_pairs={{0,128},{128,0},{1,129},{129,1},{2,130},{130,2},{3,131},{131,3},{4... | collective-permute-start | bytes 12296 | tf_op jit(solution)/shard_map/ppermute | solution.py:43
  53.2 18.9 %collective-permute-start.4 = (bf16[256,2048]{1,0:T(8,128)(2,1)}, bf16[256,2048]{1,0:T(8,128)(2,1)}, u32[]{:S(2)}, u32[]{:S(2)}) collective-permute-start(bf16[256,2048]{1,0:T(8,128)(2,1)} %bitcast.3.refs_1_), channel_id=1, source_target_pairs={{0,16},{16,0},{1,17},{17,1},{2,18},{18,2},{3,19},{19,3},{4,20},{20... | collective-permute-start | bytes 3145736 | tf_op jit(solution)/shard_map/ppermute | solution.py:43
  60.1 12.0 %collective-permute-start.5 = (bf16[256,2048]{1,0:T(8,128)(2,1)}, bf16[256,2048]{1,0:T(8,128)(2,1)}, u32[]{:S(2)}, u32[]{:S(2)}) collective-permute-start(bf16[256,2048]{1,0:T(8,128)(2,1)} %get-tuple-element.47.refs_2_.refs_3_), channel_id=1, source_target_pairs={{0,16},{16,0},{1,17},{17,1},{2,18},{18,2},{3,19},{19,3},{4,20},{20... | collective-permute-start | bytes 3145736 | tf_op jit(solution)/shard_map/ppermute | solution.py:43
  61.8 10.3 %collective-permute-start.6 = (bf16[256,2048]{1,0:T(8,128)(2,1)}, bf16[256,2048]{1,0:T(8,128)(2,1)}, u32[]{:S(2)}, u32[]{:S(2)}) collective-permute-start(bf16[256,2048]{1,0:T(8,128)(2,1)} %get-tuple-element.48.refs_3_.refs_5_), channel_id=1, source_target_pairs={{0,16},{16,0},{1,17},{17,1},{2,18},{18,2},{3,19},{19,3},{4,20},{20... | collective-permute-start | bytes 3145736 | tf_op jit(solution)/shard_map/ppermute | solution.py:43
  61.9 17.0 %collective-permute-start.7 = (bf16[128,2048]{1,0:T(8,128)(2,1)}, bf16[128,2048]{1,0:T(8,128)(2,1)}, u32[]{:S(2)}, u32[]{:S(2)}) collective-permute-start(bf16[128,2048]{1,0:T(8,128)(2,1)} %get-tuple-element.51), channel_id=1, source_target_pairs={{0,32},{32,64},{64,96},{96,0},{1,33},{33,65},{65,97},{97,1},{2,34}... | collective-permute-start | bytes 1572872 | tf_op jit(solution)/shard_map/ppermute | solution.py:43
  61.9 17.0 %collective-permute-start.8 = (bf16[128,2048]{1,0:T(8,128)(2,1)}, bf16[128,2048]{1,0:T(8,128)(2,1)}, u32[]{:S(2)}, u32[]{:S(2)}) collective-permute-start(bf16[128,2048]{1,0:T(8,128)(2,1)} %get-tuple-element.52), channel_id=1, source_target_pairs={{0,96},{32,0},{64,32},{96,64},{1,97},{33,1},{65,33},{97,65},{2,98}... | collective-permute-start | bytes 1572872 | tf_op jit(solution)/shard_map/ppermute | solution.py:43
  67.5 19.8 %all-to-all-start.1 = ((bf16[8,256,256]{2,1,0:T(8,128)(2,1)}), bf16[8,256,256]{2,1,0:T(8,128)(2,1)S(1)}, u32[]{:S(2)}, u32[]{:S(2)}) async-start(bf16[8,256,256]{2,1,0:T(8,128)(2,1)} %copy-done.2), calls=%async_computation.1 | async-start | bytes 2097152 | tf_op jit(solution)/shard_map/all_to_all | solution.py:384
  80.1 7.3 %collective-permute-start.9 = (bf16[128,2048]{1,0:T(8,128)(2,1)}, bf16[128,2048]{1,0:T(8,128)(2,1)}, u32[]{:S(2)}, u32[]{:S(2)}) collective-permute-start(bf16[128,2048]{1,0:T(8,128)(2,1)} %get-tuple-element.53.refs_2_.refs_7_), channel_id=1, source_target_pairs={{0,16},{16,0},{1,17},{17,1},{2,18},{18,2},{3,19},{19,3},{4,20},{20... | collective-permute-start | bytes 1572872 | tf_op jit(solution)/shard_map/ppermute | solution.py:43
  81.3 6.1 %collective-permute-start.10 = (bf16[128,2048]{1,0:T(8,128)(2,1)}, bf16[128,2048]{1,0:T(8,128)(2,1)}, u32[]{:S(2)}, u32[]{:S(2)}) collective-permute-start(bf16[128,2048]{1,0:T(8,128)(2,1)} %get-tuple-element.54.refs_3_.refs_8_), channel_id=1, source_target_pairs={{0,16},{16,0},{1,17},{17,1},{2,18},{18,2},{3,19},{19,3},{4,20},{20... | collective-permute-start | bytes 1572872 | tf_op jit(solution)/shard_map/ppermute | solution.py:43
  91.9 24.2 %all-to-all-start.2 = ((bf16[4,8,64,256]{3,2,1,0:T(8,128)(2,1)}), bf16[4,8,64,256]{3,2,1,0:T(8,128)(2,1)}, u32[]{:S(2)}, u32[]{:S(2)}) async-start(bf16[4,8,64,256]{3,2,1,0:T(8,128)(2,1)} %copy-done.8), calls=%async_computation.2 | async-start | bytes 2097152 | tf_op jit(solution)/shard_map/all_to_all | solution.py:396
  106.6 4.6 %collective-permute-start.11 = (f32[2,2,128]{2,1,0:T(2,128)S(1)}, f32[2,2,128]{2,1,0:T(2,128)S(1)}, u32[]{:S(2)}, u32[]{:S(2)}) collective-permute-start(f32[2,2,128]{2,1,0:T(2,128)S(1)} %get-tuple-element.59.refs_4_), channel_id=1, source_target_pairs={{0,128},{128,0},{1,129},{129,1},{2,130},{130,2},{3,131},{131,3},{4... | collective-permute-start | bytes 6152 | tf_op jit(solution)/shard_map/ppermute | solution.py:43
  118.8 20.2 %all-to-all-start.3 = ((bf16[8,64,256]{2,1,0:T(8,128)(2,1)}), bf16[8,64,256]{2,1,0:T(8,128)(2,1)S(1)}, u32[]{:S(2)}, u32[]{:S(2)}) async-start(bf16[8,64,256]{2,1,0:T(8,128)(2,1)} %get-tuple-element.61), calls=%async_computation.3 | async-start | bytes 524288 | tf_op jit(solution)/shard_map/all_to_all | solution.py:411
  124.8 9.9 %collective-permute-start.13 = (bf16[2,256,256]{2,1,0:T(8,128)(2,1)}, bf16[2,256,256]{2,1,0:T(8,128)(2,1)S(1)}, u32[]{:S(2)}, u32[]{:S(2)}) collective-permute-start(bf16[2,256,256]{2,1,0:T(8,128)(2,1)} %get-tuple-element.64), channel_id=1, source_target_pairs={{0,32},{32,64},{64,96},{96,0},{1,33},{33,65},{65,97},{97,1},{2,34}... | collective-permute-start | bytes 786440 | tf_op jit(solution)/shard_map/ppermute | solution.py:43
  125.4 9.7 %collective-permute-start.14 = (bf16[2,256,256]{2,1,0:T(8,128)(2,1)}, bf16[2,256,256]{2,1,0:T(8,128)(2,1)S(1)}, u32[]{:S(2)}, u32[]{:S(2)}) collective-permute-start(bf16[2,256,256]{2,1,0:T(8,128)(2,1)} %get-tuple-element.65), channel_id=1, source_target_pairs={{0,64},{32,96},{64,0},{96,32},{1,65},{33,97},{65,1},{97,33},{2,66}... | collective-permute-start | bytes 786440 | tf_op jit(solution)/shard_map/ppermute | solution.py:43
  127.0 12.0 %collective-permute-start.15 = (bf16[2,256,256]{2,1,0:T(8,128)(2,1)}, bf16[2,256,256]{2,1,0:T(8,128)(2,1)S(1)}, u32[]{:S(2)}, u32[]{:S(2)}) collective-permute-start(bf16[2,256,256]{2,1,0:T(8,128)(2,1)} %get-tuple-element.66), channel_id=1, source_target_pairs={{0,96},{32,0},{64,32},{96,64},{1,97},{33,1},{65,33},{97,65},{2,98}... | collective-permute-start | bytes 786440 | tf_op jit(solution)/shard_map/ppermute | solution.py:43
  127.9 4.6 %collective-permute-start.12 = (bf16[8,16,256]{2,1,0:T(8,128)(2,1)S(1)}, bf16[8,16,256]{2,1,0:T(8,128)(2,1)S(1)}, u32[]{:S(2)}, u32[]{:S(2)}) collective-permute-start(bf16[8,16,256]{2,1,0:T(8,128)(2,1)S(1)} %get-tuple-element.63), channel_id=1, source_target_pairs={{0,128},{128,0},{1,129},{129,1},{2,130},{130,2},{3,131},{131,3},{4... | collective-permute-start | bytes 196616 | tf_op jit(solution)/shard_map/ppermute | solution.py:43
  141.3 11.8 %collective-permute-start.16 = (bf16[2048,1024]{1,0:T(8,128)(2,1)}, bf16[2048,1024]{1,0:T(8,128)(2,1)}, u32[]{:S(2)}, u32[]{:S(2)}) collective-permute-start(bf16[2048,1024]{1,0:T(8,128)(2,1)} %get-tuple-element.69.refs_1_), channel_id=1, source_target_pairs={{0,16},{16,0},{1,17},{17,1},{2,18},{18,2},{3,19},{19,3},{4,20},{20... | collective-permute-start | bytes 12582920 | tf_op jit(solution)/shard_map/ppermute | solution.py:43
  145.2 6.2 %collective-permute-start.17 = (bf16[4,256,256]{2,1,0:T(8,128)(2,1)}, bf16[4,256,256]{2,1,0:T(8,128)(2,1)S(1)}, u32[]{:S(2)}, u32[]{:S(2)}) collective-permute-start(bf16[4,256,256]{2,1,0:T(8,128)(2,1)} %get-tuple-element.75), channel_id=1, source_target_pairs={{0,16},{16,0},{1,17},{17,1},{2,18},{18,2},{3,19},{19,3},{4,20},{20... | collective-permute-start | bytes 1572872 | tf_op jit(solution)/shard_map/ppermute | solution.py:43
  145.3 15.4 %all-to-all-start.4 = ((f32[8,24,256]{2,1,0:T(8,128)}), f32[8,24,256]{2,1,0:T(8,128)S(1)}, u32[]{:S(2)}, u32[]{:S(2)}) async-start(f32[8,24,256]{2,1,0:T(8,128)} %get-tuple-element.67), calls=%async_computation.4 | async-start | bytes 393216 | tf_op jit(solution)/shard_map/all_to_all | solution.py:423
  (19 other events, 235.6 us)
Sparse Core Ops, SparseCore 0:
  10.9 71.9 all-gather.1

commit v5 on v4

--- a/solution.py
+++ b/solution.py
@@ -388,18 +388,18 @@
     _, c_2a, c_2b = run(after_kernel, "after", [((8, 128), F32)], [mark], 1, 1, ties=c_own[3:])
     c_own[3:] = [c_2a, c_2b]
     c_oth = c_oth + [shift(c_2a, "k", 1), shift(c_2b, "k", 1)]
-    pieces, home = run(
+    (pieces,) = run(
         late_kernel, "block_late", [((4, 8, 64, BLOCK), BF)], [acc, vg] + c_own[3:] + c_oth[3:], 540, 4,
-        ties=[home],
     )
 
     got = lax.all_to_all(pieces, ("yh", "yl"), 0, 0)
     pairs = [c for both in zip(c_own[:3], c_oth[:3]) for c in both]
-    prods, cross = run(
+    prods, cross, home = run(
         prods_kernel, "prods", [(unit, F32), ((2, 2, QC), F32)],
         [w_own] + pairs + c_own[3:] + c_oth[3:] + [qg, p, fac], 2300, 10, [((WIDTH, BLOCK), BF)],
         stack=tuple(range(1, 11)),
         picks={0: (lambda info, r: r.at[:, pl.ds(pl.multiple_of(info.x * 256, 256), 256)], (WIDTH, BLOCK))},
+        ties=[home],
     )
     g_0, g_1, g_2, g_3, q_own, q_far = run(
         grads_kernel, "grads", [((2, TOK, BLOCK), BF)] * 4 + [((8, 16, BLOCK), BF)] * 2,

time: 171 us -> 171 us (level)
  local copies, waits for them, and re-layouts: 5.94 us -> 10 us
  waiting for transfers between devices: 43 us -> 39.8 us
    all_to_all x1, waiting for transfers between devices: 5.8 us -> 0.01 us  [on_device(): home = lax.all_to_all(vg, ring, 0, 0)]
    unnamed x38 -> x50, local copies, waits for them, and re-layouts: 5.94 us -> 10 us
    ppermute x18, waiting for transfers between devices: 22.6 us -> 25.2 us  [shift(): return lax.ppermute(a, axis, [(i, (i + by) % n) for i in range(n)])]
  transfers between devices with their start and end apart: 24 -> 24, of which waited for: 9 -> 9; matrix products, arithmetic and copies ran while one was open for 0% -> 0% of each run, Pallas kernels for 25% -> 24%
where the time goes in v5:
time: 171 us; the launch traced here: 170 us
  starting transfers between devices  55.4 us (32%)
  Pallas kernels  50.6 us (30%)
  waiting for transfers between devices  39.8 us (23%)
  between operations  14.4 us (8%)
  local copies, waits for them, and re-layouts  10 us (6%)
    pallas_call x15, Pallas kernels, call(): pl.pallas_call(body, in_specs=[SMEM] * 3 + [anywhere] * (n_in + n_tie), o...  48.3 us
    ppermute x18, starting transfers between devices, shift(): return lax.ppermute(a, axis, [(i, (i + by) % n) for i in range(n)])  29.6 us
    ppermute x18, waiting for transfers between devices, shift(): return lax.ppermute(a, axis, [(i, (i + by) % n) for i in range(n)])  25.2 us
    all_to_all x1, waiting for transfers between devices, on_device(): pay = lax.all_to_all(pay, ring, 0, 0)  14.6 us
    unnamed x50, local copies, waits for them, and re-layouts  10 us
    all_to_all x1, starting transfers between devices, on_device(): pay = lax.all_to_all(pay, ring, 0, 0)  6.72 us
    all_to_all x1, starting transfers between devices, on_device(): z_out = lax.all_to_all(z_in, 'z', 0, 0)  5.62 us
    all_to_all x1, starting transfers between devices, on_device(): got = lax.all_to_all(pieces, ('yh', 'yl'), 0, 0)  5 us
  transfers between devices with their start and end apart: 24, of which 9 were waited for; matrix products, arithmetic and copies ran while one was open for 0% of the time, Pallas kernels for 24%

profile of v5, /device:TPU:1, one launch (start us, length us, event | category | flops | bytes accessed | tf_op | source)
XLA Modules:
  0.0 170.2 jit_solution(12626616585336406007)
XLA Ops:
  7.2 3.5 %pack.1 = (bf16[8,304,256]{2,1,0:T(8,128)(2,1)}, bf16[128,1024]{1,0:T(8,128)(2,1)}) custom-call(s32[1,2,2]{2,1,0:T(2,128)} %plan.29, s32[1,2]{1,0:T(1,128)} %lengths.29, s32[1,4]{1,0:T(1,128)} %blocks.29, bf16[256,2048]{1,0:T(8,128)(2,1)} %bitcast.9, bf16[16,2048]{1,0:T(8,128)(2,1)} %bitcast.10, bf16[16,2048]{1,0:T(8,128)(2,1)} %bitcast.11, ...), custom_call_target="tpu_custom_call" | custom-call | flops 1 | bytes 1 | tf_op jit(solution)/shard_map/pack/pallas_call | solution.py:94
  10.8 6.7 %all-to-all-start = ((bf16[8,304,256]{2,1,0:T(8,128)(2,1)}), bf16[8,304,256]{2,1,0:T(8,128)(2,1)S(1)}, u32[]{:S(2)}, u32[]{:S(2)}) async-start(bf16[8,304,256]{2,1,0:T(8,128)(2,1)} %get-tuple-element.40), calls=%async_computation | async-start | bytes 2490368 | tf_op jit(solution)/shard_map/all_to_all | solution.py:347
  20.2 14.6 %all-to-all-done.refs_0_.refs_6_ = bf16[8,304,256]{2,1,0:T(8,128)(2,1)S(1)} async-done(((bf16[8,304,256]{2,1,0:T(8,128)(2,1)}), bf16[8,304,256]{2,1,0:T(8,128)(2,1)S(1)}, u32[]{:S(2)}, u32[]{:S(2)}) %all-to-all-start) | async-done | bytes 1245216 | tf_op jit(solution)/shard_map/all_to_all | solution.py:347
  37.4 10.8 %collective-permute-done.refs_1_ = bf16[8,32,256]{2,1,0:T(8,128)(2,1)S(1)} collective-permute-done((bf16[8,32,256]{2,1,0:T(8,128)(2,1)S(1)}, bf16[8,32,256]{2,1,0:T(8,128)(2,1)S(1)}, u32[]{:S(2)}, u32[]{:S(2)}) %collective-permute-start) | collective-permute-done | bytes 131104 | tf_op jit(solution)/shard_map/ppermute | solution.py:43
  50.4 2.8 %collective-permute-start.1 = (f32[2,2,2,128]{3,2,1,0:T(2,128)S(1)}, f32[2,2,2,128]{3,2,1,0:T(2,128)S(1)}, u32[]{:S(2)}, u32[]{:S(2)}) collective-permute-start(f32[2,2,2,128]{3,2,1,0:T(2,128)S(1)} %get-tuple-element.44.refs_3_), channel_id=1, source_target_pairs={{0,128},{128,0},{1,129},{129,1},{2,130},{130,2},{3,131},{131,3},{4... | collective-permute-start | bytes 12296 | tf_op jit(solution)/shard_map/ppermute | solution.py:43
  53.2 4.0 %collective-permute-start.4 = (bf16[256,2048]{1,0:T(8,128)(2,1)}, bf16[256,2048]{1,0:T(8,128)(2,1)}, u32[]{:S(2)}, u32[]{:S(2)}) collective-permute-start(bf16[256,2048]{1,0:T(8,128)(2,1)} %bitcast.3.refs_1_), channel_id=1, source_target_pairs={{0,16},{16,0},{1,17},{17,1},{2,18},{18,2},{3,19},{19,3},{4,20},{20... | collective-permute-start | bytes 3145736 | tf_op jit(solution)/shard_map/ppermute | solution.py:43
  57.8 2.2 %halves.1 = (bf16[128,2048]{1,0:T(8,128)(2,1)}, bf16[128,2048]{1,0:T(8,128)(2,1)}, bf16[256,2048]{1,0:T(8,128)(2,1)}, bf16[256,2048]{1,0:T(8,128)(2,1)}) custom-call(f32[2,2,2,128]{3,2,1,0:T(2,128)} %copy-done.21, bf16[256,2048]{1,0:T(8,128)(2,1)} %collective-permute-done.2.m1, ...), custom_call_target="tpu_custom_call", output_to_operand_aliasing={{2}: (1, {}), {3}: (2, {})} | custom-call | flops 1 | bytes 1 | tf_op jit(solution)/shard_map/halves/pallas_call | solution.py:366
  61.9 2.7 %collective-permute-start.8 = (bf16[128,2048]{1,0:T(8,128)(2,1)}, bf16[128,2048]{1,0:T(8,128)(2,1)}, u32[]{:S(2)}, u32[]{:S(2)}) collective-permute-start(bf16[128,2048]{1,0:T(8,128)(2,1)} %get-tuple-element.51), channel_id=1, source_target_pairs={{0,96},{32,0},{64,32},{96,64},{1,97},{33,1},{65,33},{97,65},{2,98}... | collective-permute-start | bytes 1572872 | tf_op jit(solution)/shard_map/ppermute | solution.py:43
  67.5 4.6 %all-to-all-start.2 = ((bf16[8,256,256]{2,1,0:T(8,128)(2,1)}), bf16[8,256,256]{2,1,0:T(8,128)(2,1)S(1)}, u32[]{:S(2)}, u32[]{:S(2)}) async-start(bf16[8,256,256]{2,1,0:T(8,128)(2,1)} %copy-done.2), calls=%async_computation.2 | async-start | bytes 2097152 | tf_op jit(solution)/shard_map/all_to_all | solution.py:384
  72.1 6.8 %block_early.1 = (f32[2048,256]{1,0:T(8,128)}, f32[8,128]{1,0:T(8,128)S(1)}) custom-call(s32[1,2,2]{2,1,0:T(2,128)S(1)} %copy-done.15, s32[1,2]{1,0:T(1,128)S(1)} %copy-done.17, s32[1,4]{1,0:T(1,128)S(1)} %copy-done.19, bf16[8,256,256]{2,1,0:T(8,128)(2,1)S(1)} %copy-done.3, bf16[256,2048]{1,0:T(8,128)(2,1)} %bitcast.3.refs_1_, ...), custom_call_target="tpu_custom_call" | custom-call | flops 1 | bytes 1 | tf_op jit(solution)/shard_map/block_early/pallas_call | solution.py:94
  83.8 3.3 %block_late.1 = bf16[4,8,64,256]{3,2,1,0:T(8,128)(2,1)S(1)} custom-call(s32[1,2,2]{2,1,0:T(2,128)S(1)} %copy-done.15, s32[1,2]{1,0:T(1,128)S(1)} %copy-done.17, s32[1,4]{1,0:T(1,128)S(1)} %copy-done.19, f32[2048,256]{1,0:T(8,128)} %get-tuple-element.48.refs_0_, bf16[8,256,256]{2,1,0:T(8,128)(2,1)S(1)} %copy-done.3, ...), custom_call_target="tpu_custom_call" | custom-call | flops 1 | bytes 1 | tf_op jit(solution)/shard_map/block_late/pallas_call | solution.py:94
  89.7 5.0 %all-to-all-start.1 = ((bf16[4,8,64,256]{3,2,1,0:T(8,128)(2,1)}), bf16[4,8,64,256]{3,2,1,0:T(8,128)(2,1)}, u32[]{:S(2)}, u32[]{:S(2)}) async-start(bf16[4,8,64,256]{3,2,1,0:T(8,128)(2,1)} %copy-done.5), calls=%async_computation.1 | async-start | bytes 2097152 | tf_op jit(solution)/shard_map/all_to_all | solution.py:395
  95.8 9.6 %prods.1 = (f32[8,256,256]{2,1,0:T(8,128)}, f32[2,2,128]{2,1,0:T(2,128)S(1)}, bf16[8,256,256]{2,1,0:T(8,128)(2,1)S(1)}) custom-call(s32[1,2,2]{2,1,0:T(2,128)S(1)} %copy-done.15, s32[1,2]{1,0:T(1,128)S(1)} %copy-done.17, s32[1,4]{1,0:T(1,128)S(1)} %copy-done.19, ...), custom_call_target="tpu_custom_call", output_to_operand_aliasing={{2}: (17, {})} | custom-call | flops 1 | bytes 1 | tf_op jit(solution)/shard_map/prods/pallas_call | solution.py:94
  105.3 3.1 %collective-permute-start.11 = (f32[2,2,128]{2,1,0:T(2,128)S(1)}, f32[2,2,128]{2,1,0:T(2,128)S(1)}, u32[]{:S(2)}, u32[]{:S(2)}) collective-permute-start(f32[2,2,128]{2,1,0:T(2,128)S(1)} %get-tuple-element.57.refs_4_), channel_id=1, source_target_pairs={{0,128},{128,0},{1,129},{129,1},{2,130},{130,2},{3,131},{131,3},{4... | collective-permute-start | bytes 6152 | tf_op jit(solution)/shard_map/ppermute | solution.py:43
  109.9 3.5 %grads.1 = (bf16[2,256,256]{2,1,0:T(8,128)(2,1)S(1)}, bf16[2,256,256]{2,1,0:T(8,128)(2,1)S(1)}, bf16[2,256,256]{2,1,0:T(8,128)(2,1)S(1)}, bf16[2,256,256]{2,1,0:...) custom-call(s32[1,2,2]{2,1,0:T(2,128)S(1)} %copy-done.15, s32[1,2]{1,0:T(1,128)S(1)} %copy-done.17, ...), custom_call_target="tpu_custom_call" | custom-call | flops 1 | bytes 1 | tf_op jit(solution)/shard_map/grads/pallas_call | solution.py:94
  115.5 2.8 %sum_y.1 = (bf16[8,64,256]{2,1,0:T(8,128)(2,1)}, bf16[8,16,256]{2,1,0:T(8,128)(2,1)}) custom-call(s32[1,2,2]{2,1,0:T(2,128)} %plan.29, s32[1,2]{1,0:T(1,128)} %lengths.29, s32[1,4]{1,0:T(1,128)} %blocks.29, bf16[4,8,64,256]{3,2,1,0:T(8,128)(2,1)} %all-to-all-done.1.refs_0_, bf16[8,16,256]{2,1,0:T(8,128)(2,1)} %copy-done.13), custom_call_target="tpu_custom_call", output_to_operand_aliasing={{1}: (4, {})} | custom-call | flops 1 | bytes 1 | tf_op jit(solution)/shard_map/sum_y/pallas_call | solution.py:94
  118.3 5.6 %all-to-all-start.3 = ((bf16[8,64,256]{2,1,0:T(8,128)(2,1)}), bf16[8,64,256]{2,1,0:T(8,128)(2,1)S(1)}, u32[]{:S(2)}, u32[]{:S(2)}) async-start(bf16[8,64,256]{2,1,0:T(8,128)(2,1)} %get-tuple-element.59), calls=%async_computation.3 | async-start | bytes 524288 | tf_op jit(solution)/shard_map/all_to_all | solution.py:411
  124.5 3.5 %collective-permute-start.14 = (bf16[2,256,256]{2,1,0:T(8,128)(2,1)}, bf16[2,256,256]{2,1,0:T(8,128)(2,1)S(1)}, u32[]{:S(2)}, u32[]{:S(2)}) collective-permute-start(bf16[2,256,256]{2,1,0:T(8,128)(2,1)} %copy-done.23), channel_id=1, source_target_pairs={{0,64},{32,96},{64,0},{96,32},{1,65},{33,97},{65,1},{97,33},{2,66}... | collective-permute-start | bytes 786440 | tf_op jit(solution)/shard_map/ppermute | solution.py:43
  128.1 2.4 %collective-permute-start.12 = (bf16[8,16,256]{2,1,0:T(8,128)(2,1)S(1)}, bf16[8,16,256]{2,1,0:T(8,128)(2,1)S(1)}, u32[]{:S(2)}, u32[]{:S(2)}) collective-permute-start(bf16[8,16,256]{2,1,0:T(8,128)(2,1)S(1)} %get-tuple-element.61), channel_id=1, source_target_pairs={{0,128},{128,0},{1,129},{129,1},{2,130},{130,2},{3,131},{131,3},{4... | collective-permute-start | bytes 196616 | tf_op jit(solution)/shard_map/ppermute | solution.py:43
  130.6 2.2 %collective-permute-done.12.refs_2_ = bf16[8,16,256]{2,1,0:T(8,128)(2,1)S(1)} collective-permute-done((bf16[8,16,256]{2,1,0:T(8,128)(2,1)S(1)}, bf16[8,16,256]{2,1,0:T(8,128)(2,1)S(1)}, u32[]{:S(2)}, u32[]{:S(2)}) %collective-permute-start.12) | collective-permute-done | bytes 65568 | tf_op jit(solution)/shard_map/ppermute | solution.py:43
  132.8 6.0 %collective-permute-done.14.refs_5_ = bf16[2,256,256]{2,1,0:T(8,128)(2,1)S(1)} collective-permute-done((bf16[2,256,256]{2,1,0:T(8,128)(2,1)}, bf16[2,256,256]{2,1,0:T(8,128)(2,1)S(1)}, u32[]{:S(2)}, u32[]{:S(2)}) %collective-permute-start.14) | collective-permute-done | bytes 262176 | tf_op jit(solution)/shard_map/ppermute | solution.py:43
  145.3 3.9 %all-to-all-start.4 = ((f32[8,24,256]{2,1,0:T(8,128)}), f32[8,24,256]{2,1,0:T(8,128)S(1)}, u32[]{:S(2)}, u32[]{:S(2)}) async-start(f32[8,24,256]{2,1,0:T(8,128)} %get-tuple-element.65), calls=%async_computation.4 | async-start | bytes 393216 | tf_op jit(solution)/shard_map/all_to_all | solution.py:423
  149.2 2.2 %collective-permute-done.17.refs_1_ = bf16[4,256,256]{2,1,0:T(8,128)(2,1)S(1)} collective-permute-done((bf16[4,256,256]{2,1,0:T(8,128)(2,1)}, bf16[4,256,256]{2,1,0:T(8,128)(2,1)S(1)}, u32[]{:S(2)}, u32[]{:S(2)}) %collective-permute-start.17) | collective-permute-done | bytes 524320 | tf_op jit(solution)/shard_map/ppermute | solution.py:43
  153.2 7.5 %context_grad.1.refs_1_ = bf16[256,2048]{1,0:T(8,128)(2,1)} custom-call(s32[1,2,2]{2,1,0:T(2,128)S(1)} %copy-done.16, s32[1,2]{1,0:T(1,128)S(1)} %copy-done.18, s32[1,4]{1,0:T(1,128)S(1)} %copy-done.20, bf16[8,256,256]{2,1,0:T(8,128)(2,1)S(1)} %get-tuple-element.66.refs_0_, bf16[2048,1024]{1,0:T(8,128)(2,1)} %get-tuple-element.67.refs_1_, ...), custom_call_target="tpu_custom_call" | custom-call | flops 1 | bytes 1 | tf_op jit(solution)/shard_map/context_grad/pallas_call | solution.py:94
  (91 shorter events, 36.7 us)
Async XLA Ops:
  7.2 87.5 %all-gather.2.cloned.1.call-start = ((), (), s32[]{:S(2)}) async-start(), calls=%async_computation.5 | async-start | bytes 4456448 | tf_op jit(solution)/shard_map/all_gather | solution.py:346
  10.8 24.0 %all-to-all-start = ((bf16[8,304,256]{2,1,0:T(8,128)(2,1)}), bf16[8,304,256]{2,1,0:T(8,128)(2,1)S(1)}, u32[]{:S(2)}, u32[]{:S(2)}) async-start(bf16[8,304,256]{2,1,0:T(8,128)(2,1)} %get-tuple-element.40), calls=%async_computation | async-start | bytes 2490368 | tf_op jit(solution)/shard_map/all_to_all | solution.py:347
  17.5 39.8 %collective-permute-start.2 = (bf16[256,2048]{1,0:T(8,128)(2,1)}, bf16[256,2048]{1,0:T(8,128)(2,1)}, u32[]{:S(2)}, u32[]{:S(2)}) collective-permute-start(bf16[256,2048]{1,0:T(8,128)(2,1)} %bitcast.3.refs_1_), channel_id=1, source_target_pairs={{0,32},{32,64},{64,96},{96,0},{1,33},{33,65},{65,97},{97,1},{2,34}... | collective-permute-start | bytes 3145736 | tf_op jit(solution)/shard_map/ppermute | solution.py:43
  18.9 38.4 %collective-permute-start.3 = (bf16[256,2048]{1,0:T(8,128)(2,1)}, bf16[256,2048]{1,0:T(8,128)(2,1)}, u32[]{:S(2)}, u32[]{:S(2)}) collective-permute-start(bf16[256,2048]{1,0:T(8,128)(2,1)} %bitcast.3.refs_1_), channel_id=1, source_target_pairs={{0,96},{32,0},{64,32},{96,64},{1,97},{33,1},{65,33},{97,65},{2,98}... | collective-permute-start | bytes 3145736 | tf_op jit(solution)/shard_map/ppermute | solution.py:43
  35.4 12.9 %collective-permute-start = (bf16[8,32,256]{2,1,0:T(8,128)(2,1)S(1)}, bf16[8,32,256]{2,1,0:T(8,128)(2,1)S(1)}, u32[]{:S(2)}, u32[]{:S(2)}) collective-permute-start(bf16[8,32,256]{2,1,0:T(8,128)(2,1)S(1)} %unpack.1), channel_id=1, source_target_pairs={{0,128},{128,0},{1,129},{129,1},{2,130},{130,2},{3,131},{131,3},{4... | collective-permute-start | bytes 393224 | tf_op jit(solution)/shard_map/ppermute | solution.py:43
  50.4 6.8 %collective-permute-start.1 = (f32[2,2,2,128]{3,2,1,0:T(2,128)S(1)}, f32[2,2,2,128]{3,2,1,0:T(2,128)S(1)}, u32[]{:S(2)}, u32[]{:S(2)}) collective-permute-start(f32[2,2,2,128]{3,2,1,0:T(2,128)S(1)} %get-tuple-element.44.refs_3_), channel_id=1, source_target_pairs={{0,128},{128,0},{1,129},{129,1},{2,130},{130,2},{3,131},{131,3},{4... | collective-permute-start | bytes 12296 | tf_op jit(solution)/shard_map/ppermute | solution.py:43
  53.2 18.9 %collective-permute-start.4 = (bf16[256,2048]{1,0:T(8,128)(2,1)}, bf16[256,2048]{1,0:T(8,128)(2,1)}, u32[]{:S(2)}, u32[]{:S(2)}) collective-permute-start(bf16[256,2048]{1,0:T(8,128)(2,1)} %bitcast.3.refs_1_), channel_id=1, source_target_pairs={{0,16},{16,0},{1,17},{17,1},{2,18},{18,2},{3,19},{19,3},{4,20},{20... | collective-permute-start | bytes 3145736 | tf_op jit(solution)/shard_map/ppermute | solution.py:43
  60.1 12.0 %collective-permute-start.5 = (bf16[256,2048]{1,0:T(8,128)(2,1)}, bf16[256,2048]{1,0:T(8,128)(2,1)}, u32[]{:S(2)}, u32[]{:S(2)}) collective-permute-start(bf16[256,2048]{1,0:T(8,128)(2,1)} %get-tuple-element.46.refs_2_.refs_3_), channel_id=1, source_target_pairs={{0,16},{16,0},{1,17},{17,1},{2,18},{18,2},{3,19},{19,3},{4,20},{20... | collective-permute-start | bytes 3145736 | tf_op jit(solution)/shard_map/ppermute | solution.py:43
  61.8 10.3 %collective-permute-start.6 = (bf16[256,2048]{1,0:T(8,128)(2,1)}, bf16[256,2048]{1,0:T(8,128)(2,1)}, u32[]{:S(2)}, u32[]{:S(2)}) collective-permute-start(bf16[256,2048]{1,0:T(8,128)(2,1)} %get-tuple-element.47.refs_3_.refs_5_), channel_id=1, source_target_pairs={{0,16},{16,0},{1,17},{17,1},{2,18},{18,2},{3,19},{19,3},{4,20},{20... | collective-permute-start | bytes 3145736 | tf_op jit(solution)/shard_map/ppermute | solution.py:43
  61.9 17.0 %collective-permute-start.7 = (bf16[128,2048]{1,0:T(8,128)(2,1)}, bf16[128,2048]{1,0:T(8,128)(2,1)}, u32[]{:S(2)}, u32[]{:S(2)}) collective-permute-start(bf16[128,2048]{1,0:T(8,128)(2,1)} %get-tuple-element.50), channel_id=1, source_target_pairs={{0,32},{32,64},{64,96},{96,0},{1,33},{33,65},{65,97},{97,1},{2,34}... | collective-permute-start | bytes 1572872 | tf_op jit(solution)/shard_map/ppermute | solution.py:43
  61.9 17.0 %collective-permute-start.8 = (bf16[128,2048]{1,0:T(8,128)(2,1)}, bf16[128,2048]{1,0:T(8,128)(2,1)}, u32[]{:S(2)}, u32[]{:S(2)}) collective-permute-start(bf16[128,2048]{1,0:T(8,128)(2,1)} %get-tuple-element.51), channel_id=1, source_target_pairs={{0,96},{32,0},{64,32},{96,64},{1,97},{33,1},{65,33},{97,65},{2,98}... | collective-permute-start | bytes 1572872 | tf_op jit(solution)/shard_map/ppermute | solution.py:43
  67.5 22.2 %all-to-all-start.2 = ((bf16[8,256,256]{2,1,0:T(8,128)(2,1)}), bf16[8,256,256]{2,1,0:T(8,128)(2,1)S(1)}, u32[]{:S(2)}, u32[]{:S(2)}) async-start(bf16[8,256,256]{2,1,0:T(8,128)(2,1)} %copy-done.2), calls=%async_computation.2 | async-start | bytes 2097152 | tf_op jit(solution)/shard_map/all_to_all | solution.py:384
  80.1 2.9 %collective-permute-start.9 = (bf16[128,2048]{1,0:T(8,128)(2,1)}, bf16[128,2048]{1,0:T(8,128)(2,1)S(1)}, u32[]{:S(2)}, u32[]{:S(2)}) collective-permute-start(bf16[128,2048]{1,0:T(8,128)(2,1)} %get-tuple-element.52.refs_2_.refs_7_), channel_id=1, source_target_pairs={{0,16},{16,0},{1,17},{17,1},{2,18},{18,2},{3,19},{19,3},{4,20},{20... | collective-permute-start | bytes 1572872 | tf_op jit(solution)/shard_map/ppermute | solution.py:43
  81.3 2.5 %collective-permute-start.10 = (bf16[128,2048]{1,0:T(8,128)(2,1)}, bf16[128,2048]{1,0:T(8,128)(2,1)S(1)}, u32[]{:S(2)}, u32[]{:S(2)}) collective-permute-start(bf16[128,2048]{1,0:T(8,128)(2,1)} %get-tuple-element.53.refs_3_.refs_8_), channel_id=1, source_target_pairs={{0,16},{16,0},{1,17},{17,1},{2,18},{18,2},{3,19},{19,3},{4,20},{20... | collective-permute-start | bytes 1572872 | tf_op jit(solution)/shard_map/ppermute | solution.py:43
  89.7 25.8 %all-to-all-start.1 = ((bf16[4,8,64,256]{3,2,1,0:T(8,128)(2,1)}), bf16[4,8,64,256]{3,2,1,0:T(8,128)(2,1)}, u32[]{:S(2)}, u32[]{:S(2)}) async-start(bf16[4,8,64,256]{3,2,1,0:T(8,128)(2,1)} %copy-done.5), calls=%async_computation.1 | async-start | bytes 2097152 | tf_op jit(solution)/shard_map/all_to_all | solution.py:395
  105.3 4.6 %collective-permute-start.11 = (f32[2,2,128]{2,1,0:T(2,128)S(1)}, f32[2,2,128]{2,1,0:T(2,128)S(1)}, u32[]{:S(2)}, u32[]{:S(2)}) collective-permute-start(f32[2,2,128]{2,1,0:T(2,128)S(1)} %get-tuple-element.57.refs_4_), channel_id=1, source_target_pairs={{0,128},{128,0},{1,129},{129,1},{2,130},{130,2},{3,131},{131,3},{4... | collective-permute-start | bytes 6152 | tf_op jit(solution)/shard_map/ppermute | solution.py:43
  118.3 20.9 %all-to-all-start.3 = ((bf16[8,64,256]{2,1,0:T(8,128)(2,1)}), bf16[8,64,256]{2,1,0:T(8,128)(2,1)S(1)}, u32[]{:S(2)}, u32[]{:S(2)}) async-start(bf16[8,64,256]{2,1,0:T(8,128)(2,1)} %get-tuple-element.59), calls=%async_computation.3 | async-start | bytes 524288 | tf_op jit(solution)/shard_map/all_to_all | solution.py:411
  123.9 8.9 %collective-permute-start.13 = (bf16[2,256,256]{2,1,0:T(8,128)(2,1)}, bf16[2,256,256]{2,1,0:T(8,128)(2,1)S(1)}, u32[]{:S(2)}, u32[]{:S(2)}) collective-permute-start(bf16[2,256,256]{2,1,0:T(8,128)(2,1)} %copy-done.24), channel_id=1, source_target_pairs={{0,32},{32,64},{64,96},{96,0},{1,33},{33,65},{65,97},{97,1},{2,34}... | collective-permute-start | bytes 786440 | tf_op jit(solution)/shard_map/ppermute | solution.py:43
  124.5 14.2 %collective-permute-start.14 = (bf16[2,256,256]{2,1,0:T(8,128)(2,1)}, bf16[2,256,256]{2,1,0:T(8,128)(2,1)S(1)}, u32[]{:S(2)}, u32[]{:S(2)}) collective-permute-start(bf16[2,256,256]{2,1,0:T(8,128)(2,1)} %copy-done.23), channel_id=1, source_target_pairs={{0,64},{32,96},{64,0},{96,32},{1,65},{33,97},{65,1},{97,33},{2,66}... | collective-permute-start | bytes 786440 | tf_op jit(solution)/shard_map/ppermute | solution.py:43
  128.1 11.1 %collective-permute-start.15 = (bf16[2,256,256]{2,1,0:T(8,128)(2,1)S(1)}, bf16[2,256,256]{2,1,0:T(8,128)(2,1)S(1)}, u32[]{:S(2)}, u32[]{:S(2)}) collective-permute-start(bf16[2,256,256]{2,1,0:T(8,128)(2,1)S(1)} %get-tuple-element.64), channel_id=1, source_target_pairs={{0,96},{32,0},{64,32},{96,64},{1,97},{33,1},{65,33},{97,65},{2,98}... | collective-permute-start | bytes 786440 | tf_op jit(solution)/shard_map/ppermute | solution.py:43
  128.1 4.6 %collective-permute-start.12 = (bf16[8,16,256]{2,1,0:T(8,128)(2,1)S(1)}, bf16[8,16,256]{2,1,0:T(8,128)(2,1)S(1)}, u32[]{:S(2)}, u32[]{:S(2)}) collective-permute-start(bf16[8,16,256]{2,1,0:T(8,128)(2,1)S(1)} %get-tuple-element.61), channel_id=1, source_target_pairs={{0,128},{128,0},{1,129},{129,1},{2,130},{130,2},{3,131},{131,3},{4... | collective-permute-start | bytes 196616 | tf_op jit(solution)/shard_map/ppermute | solution.py:43
  141.5 11.6 %collective-permute-start.16 = (bf16[2048,1024]{1,0:T(8,128)(2,1)}, bf16[2048,1024]{1,0:T(8,128)(2,1)}, u32[]{:S(2)}, u32[]{:S(2)}) collective-permute-start(bf16[2048,1024]{1,0:T(8,128)(2,1)} %get-tuple-element.67.refs_1_), channel_id=1, source_target_pairs={{0,16},{16,0},{1,17},{17,1},{2,18},{18,2},{3,19},{19,3},{4,20},{20... | collective-permute-start | bytes 12582920 | tf_op jit(solution)/shard_map/ppermute | solution.py:43
  145.2 6.2 %collective-permute-start.17 = (bf16[4,256,256]{2,1,0:T(8,128)(2,1)}, bf16[4,256,256]{2,1,0:T(8,128)(2,1)S(1)}, u32[]{:S(2)}, u32[]{:S(2)}) collective-permute-start(bf16[4,256,256]{2,1,0:T(8,128)(2,1)} %get-tuple-element.73), channel_id=1, source_target_pairs={{0,16},{16,0},{1,17},{17,1},{2,18},{18,2},{3,19},{19,3},{4,20},{20... | collective-permute-start | bytes 1572872 | tf_op jit(solution)/shard_map/ppermute | solution.py:43
  145.3 15.4 %all-to-all-start.4 = ((f32[8,24,256]{2,1,0:T(8,128)}), f32[8,24,256]{2,1,0:T(8,128)S(1)}, u32[]{:S(2)}, u32[]{:S(2)}) async-start(f32[8,24,256]{2,1,0:T(8,128)} %get-tuple-element.65), calls=%async_computation.4 | async-start | bytes 393216 | tf_op jit(solution)/shard_map/all_to_all | solution.py:423
  (25 other events, 248.8 us)
Sparse Core Ops, SparseCore 0:
  10.9 71.9 all-gather.1

commit v6 on v4

--- a/solution.py
+++ b/solution.py
@@ -160,7 +160,7 @@
             masked = jnp.where(visible, dot(own[n, 0:256, hs], qg_ref[0, e, :, hs], 1, 1) * SCALE, NEG)
             top = jnp.max(masked, axis=0, keepdims=True)
             p = jnp.where(visible, jnp.exp(masked - top), 0.0)
-            p_ref[n, :, hs] = p
+            p_ref[n, :, hs] = p.astype(BF)
             top_rows.append(top)
             sum_rows.append(jnp.sum(p, axis=0, keepdims=True))
         tops.append(jnp.concatenate(top_rows, axis=0))
@@ -179,7 +179,7 @@
         ex_ref[1, e] = total
 
 
-def probs_kernel(info, qg_ref, p_ref, top_ref, x0, x1, vg_ref, fac_ref):
+def probs_kernel(info, qg_ref, p_ref, top_ref, x0, x1, vg_ref, u0, u1, u2, u3, fac_ref):
     tops, invs = [], []
     for e in range(2):
         top = jnp.maximum(x0[0, e], x1[0, e])
@@ -193,8 +193,11 @@
         fac_ref[n] = factor
         for hh in range(2):
             hs = slice(hh * HD, (hh + 1) * HD)
-            pr = (p_ref[n, :, hs] * factor[hh : hh + 1, :]).astype(BF)
+            pr = (p_ref[n, :, hs].astype(F32) * factor[hh : hh + 1, :]).astype(BF)
             vg_ref[n, :, hs] = dot(pr, qg_ref[1, e, :, hs], 1, 0).astype(BF)
+    for step, u in enumerate((u0, u1, u2, u3)):
+        for k in range(2):
+            u[k] = vg_ref[lax.rem(info.x + step, 4) * 2 + k]
 
 
 def ring_index(info, step, other):
@@ -252,7 +255,7 @@
             hs = slice(hh * HD, (hh + 1) * HD)
             prod = dot(v[:, hs], qg_ref[1, e, :, hs], 1, 1)
             prod_ref[n, :, hs] = prod
-            pr = p_ref[n, :, hs] * fac_ref[n, hh : hh + 1, :]
+            pr = p_ref[n, :, hs].astype(F32) * fac_ref[n, hh : hh + 1, :]
             rows.append(jnp.sum(pr * prod, axis=0, keepdims=True))
         part = jnp.concatenate(rows, axis=0)
         cross[0] = cross[0] + jnp.where(one, 0.0, part)
@@ -271,7 +274,7 @@
         delta = jnp.where(one, deltas[1], deltas[0])
         for hh in range(2):
             hs = slice(hh * HD, (hh + 1) * HD)
-            pr = p_ref[n, :, hs] * fac_ref[n, hh : hh + 1, :]
+            pr = p_ref[n, :, hs].astype(F32) * fac_ref[n, hh : hh + 1, :]
             ds = (pr * (prod_ref[n, :, hs] - delta[hh : hh + 1, :])).astype(BF)
             (g0, g1, g2, g3)[step][k, :, hs] = (SCALE * dot(ds, qg_ref[0, e, :, hs], 1, 0)).astype(BF)
             qp_buf[e, :, hs] += dot(ds, own[n, 0:256, hs], 0, 0)
@@ -279,10 +282,10 @@
         out[...] = (SCALE * qp_buf[e]).astype(BF).reshape(8, 16, BLOCK)
 
 
-def turn_kernel(info, g0, g1, g2, g3, keep_ref, send_ref):
-    for step, g in enumerate((g0, g1, g2, g3)):
-        keep_ref[step] = g[info.k]
-        send_ref[step] = g[1 - info.k]
+def turn_kernel(info, g0, g1, g2, g3, u0, u1, u2, u3, keep_ref, send_ref):
+    for n, part in enumerate((g0, g1, g2, g3, u0, u1, u2, u3)):
+        keep_ref[n] = part[info.k]
+        send_ref[n] = part[1 - info.k]
 
 
 def key_kernel(info, keep, got, out_ref):
@@ -312,9 +315,9 @@
     out_ref[...] = a[...]
 
 
-def context_kernel(info, home, w_own, w_oth, out_ref):
+def context_kernel(info, keep, got, w_own, w_oth, out_ref):
     left = [
-        jnp.concatenate([home[b * 2 + k] for b in range(4)], axis=1) for k in (info.k, 1 - info.k)
+        jnp.concatenate([part[lax.rem(info.x + 4 - b, 4)] for b in range(4)], axis=1) for part in (keep, got)
     ]
     for t in range(4):
         rows = slice(t * 512, (t + 1) * 512)
@@ -356,7 +359,7 @@
     unit = (8, TOK, BLOCK)
     p, tops, ex, qg = run(
         scores_kernel, "scores",
-        [(unit, F32), ((8, 2, QC), F32), ((2, 2, 2, QC), F32), ((2, 2, QC, BLOCK), BF)],
+        [(unit, BF), ((8, 2, QC), F32), ((2, 2, 2, QC), F32), ((2, 2, QC, BLOCK), BF)],
         [pay, far], 134, 4,
     )
     ex_far = shift(ex, "yh", 1)
@@ -377,20 +380,19 @@
     c_own = [context, c_m1, c_p1, shift(m1_top, "x", 1), shift(p1_bot, "x", -1)]
     c_oth = [shift(c, "k", 1) for c in c_own[:3]]
 
-    vg, fac = run(
-        probs_kernel, "probs", [(unit, BF), ((8, 2, QC), F32)],
+    vg, u_0, u_1, u_2, u_3, fac = run(
+        probs_kernel, "probs", [(unit, BF)] + [((2, TOK, BLOCK), BF)] * 4 + [((8, 2, QC), F32)],
         [qg, p, tops, ex, ex_far], 134, 4,
     )
-    home = lax.all_to_all(vg, ring, 0, 0)
     acc, mark = run(
         early_kernel, "block_early", [((WIDTH, BLOCK), F32), ((8, 128), F32)], [vg] + c_own[:3] + c_oth[:3], 1600, 8,
     )
     _, c_2a, c_2b = run(after_kernel, "after", [((8, 128), F32)], [mark], 1, 1, ties=c_own[3:])
     c_own[3:] = [c_2a, c_2b]
     c_oth = c_oth + [shift(c_2a, "k", 1), shift(c_2b, "k", 1)]
-    pieces, home = run(
+    pieces, u_1, u_2, u_3 = run(
         late_kernel, "block_late", [((4, 8, 64, BLOCK), BF)], [acc, vg] + c_own[3:] + c_oth[3:], 540, 4,
-        ties=[home],
+        ties=[u_1, u_2, u_3],
     )
 
     got = lax.all_to_all(pieces, ("yh", "yl"), 0, 0)
@@ -405,8 +407,9 @@
         grads_kernel, "grads", [((2, TOK, BLOCK), BF)] * 4 + [((8, 16, BLOCK), BF)] * 2,
         [qg, p, fac, prods, cross, shift(cross, "yh", 1), pay], 270, 6, [((2, QC, BLOCK), F32)],
     )
-    z_in, q_own = run(
-        sum_y_kernel, "sum_y", [((8, 64, BLOCK), BF)], [got], 1, 2, ties=[q_own], megabytes=60,
+    u_far = [shift(u_1, "x", 1), shift(u_2, "x", 2), shift(u_3, "x", -1)]
+    z_in, q_own, *u_far = run(
+        sum_y_kernel, "sum_y", [((8, 64, BLOCK), BF)], [got], 1, 2, ties=[q_own, *u_far], megabytes=60,
     )
     z_out = lax.all_to_all(z_in, "z", 0, 0)
     g_far = [shift(g_1, "x", 1), shift(g_2, "x", 2), shift(g_3, "x", -1)]
@@ -415,14 +418,18 @@
         ties=[w_own, *g_far],
     )
     keep, send = run(
-        turn_kernel, "turn", [((4, TOK, BLOCK), BF)] * 2,
-        [g_0, *g_far], 1, 2,
-    )
-    (key_grad,) = run(key_kernel, "key_home", [((TOK, WIDTH), BF)], [keep, shift(send, "k", 1)], 1, 2)
+        turn_kernel, "turn", [((8, TOK, BLOCK), BF)] * 2,
+        [g_0, *g_far, u_0, *u_far], 1, 2,
+    )
+    got = shift(send, "k", 1)
+    picks = {i: (lambda info, r: r.at[pl.ds(0, 4)], (4, TOK, BLOCK)) for i in range(2)}
+    (key_grad,) = run(key_kernel, "key_home", [((TOK, WIDTH), BF)], [keep, got], 1, 2, picks=picks)
 
     joined = lax.all_to_all(joined, ring, 0, 0)
+    picks = {i: (lambda info, r: r.at[pl.ds(4, 4)], (4, TOK, BLOCK)) for i in range(2)}
     (context_grad,) = run(
-        context_kernel, "context_grad", [((TOK, WIDTH), BF)], [home, w_own, shift(w_own, "k", 1)], 2200, 10,
+        context_kernel, "context_grad", [((TOK, WIDTH), BF)], [keep, got, w_own, shift(w_own, "k", 1)], 2200, 10,
+        picks=picks,
     )
     weight_grad, query_grad = run(
         finish_kernel, "finish", [((8, WIDTH), F32), ((16, WIDTH), BF)], [joined, context_grad, key_grad], 1, 1,

time: 171 us -> 173 us (1.012)
  local copies, waits for them, and re-layouts: 5.94 us -> 16 us
  waiting for transfers between devices: 43 us -> 37.1 us
  Pallas kernels: 51.7 us -> 48.7 us
    unnamed x38 -> x64, local copies, waits for them, and re-layouts: 5.94 us -> 16 us
    all_to_all x1 -> x0, waiting for transfers between devices: 5.8 us -> none  [on_device(): home = lax.all_to_all(vg, ring, 0, 0)]
    ppermute x18 -> x21, starting transfers between devices: 28.6 us -> 33.5 us  [shift(): return lax.ppermute(a, axis, [(i, (i + by) % n) for i in range(n)])]
    all_to_all x1 -> x0, starting transfers between devices: 4.56 us -> none  [on_device(): home = lax.all_to_all(vg, ring, 0, 0)]
    pallas_call x15, Pallas kernels: 49.5 us -> 46.5 us  [call(): pl.pallas_call(body, in_specs=[SMEM] * 3 + [anywhere] * (n_in + n_tie), o...]
    ppermute x18 -> x21, waiting for transfers between devices: 22.6 us -> 22.5 us  [shift(): return lax.ppermute(a, axis, [(i, (i + by) % n) for i in range(n)])]
  transfers between devices with their start and end apart: 24 -> 26, of which waited for: 9 -> 10; matrix products, arithmetic and copies ran while one was open for 0% -> 0% of each run, Pallas kernels for 25% -> 23%
where the time goes in v6:
time: 173 us; the launch traced here: 172 us
  starting transfers between devices  56.2 us (32%)
  Pallas kernels  48.7 us (28%)
  waiting for transfers between devices  37.1 us (21%)
  local copies, waits for them, and re-layouts  16 us (9%)
  between operations  14.4 us (8%)
    pallas_call x15, Pallas kernels, call(): pl.pallas_call(body, in_specs=[SMEM] * 3 + [anywhere] * (n_in + n_tie), o...  46.5 us
    ppermute x21, starting transfers between devices, shift(): return lax.ppermute(a, axis, [(i, (i + by) % n) for i in range(n)])  33.5 us
    ppermute x21, waiting for transfers between devices, shift(): return lax.ppermute(a, axis, [(i, (i + by) % n) for i in range(n)])  22.5 us
    unnamed x64, local copies, waits for them, and re-layouts  16 us
    all_to_all x1, waiting for transfers between devices, on_device(): pay = lax.all_to_all(pay, ring, 0, 0)  14.6 us
    all_to_all x1, starting transfers between devices, on_device(): pay = lax.all_to_all(pay, ring, 0, 0)  6.72 us
    all_to_all x1, starting transfers between devices, on_device(): z_out = lax.all_to_all(z_in, 'z', 0, 0)  6.42 us
    all_to_all x1, starting transfers between devices, on_device(): got = lax.all_to_all(pieces, ('yh', 'yl'), 0, 0)  5.06 us
  transfers between devices with their start and end apart: 26, of which 10 were waited for; matrix products, arithmetic and copies ran while one was open for 0% of the time, Pallas kernels for 23%

profile of v6, /device:TPU:1, one launch (start us, length us, event | category | flops | bytes accessed | tf_op | source)
XLA Modules:
  0.0 172.4 jit_solution(8602907033103213090)
XLA Ops:
  7.2 3.5 %pack.1 = (bf16[8,304,256]{2,1,0:T(8,128)(2,1)}, bf16[128,1024]{1,0:T(8,128)(2,1)}) custom-call(s32[1,2,2]{2,1,0:T(2,128)} %plan.29, s32[1,2]{1,0:T(1,128)} %lengths.29, s32[1,4]{1,0:T(1,128)} %blocks.29, bf16[256,2048]{1,0:T(8,128)(2,1)} %bitcast.9, bf16[16,2048]{1,0:T(8,128)(2,1)} %bitcast.10, bf16[16,2048]{1,0:T(8,128)(2,1)} %bitcast.11, ...), custom_call_target="tpu_custom_call" | custom-call | flops 1 | bytes 1 | tf_op jit(solution)/shard_map/pack/pallas_call | solution.py:94
  10.8 6.7 %all-to-all-start = ((bf16[8,304,256]{2,1,0:T(8,128)(2,1)}), bf16[8,304,256]{2,1,0:T(8,128)(2,1)S(1)}, u32[]{:S(2)}, u32[]{:S(2)}) async-start(bf16[8,304,256]{2,1,0:T(8,128)(2,1)} %get-tuple-element.50), calls=%async_computation | async-start | bytes 2490368 | tf_op jit(solution)/shard_map/all_to_all | solution.py:350
  20.2 14.6 %all-to-all-done.refs_0_.refs_6_ = bf16[8,304,256]{2,1,0:T(8,128)(2,1)S(1)} async-done(((bf16[8,304,256]{2,1,0:T(8,128)(2,1)}), bf16[8,304,256]{2,1,0:T(8,128)(2,1)S(1)}, u32[]{:S(2)}, u32[]{:S(2)}) %all-to-all-start) | async-done | bytes 1245216 | tf_op jit(solution)/shard_map/all_to_all | solution.py:350
  37.4 10.8 %collective-permute-done.refs_1_ = bf16[8,32,256]{2,1,0:T(8,128)(2,1)S(1)} collective-permute-done((bf16[8,32,256]{2,1,0:T(8,128)(2,1)S(1)}, bf16[8,32,256]{2,1,0:T(8,128)(2,1)S(1)}, u32[]{:S(2)}, u32[]{:S(2)}) %collective-permute-start) | collective-permute-done | bytes 131104 | tf_op jit(solution)/shard_map/ppermute | solution.py:43
  50.5 2.8 %collective-permute-start.1 = (f32[2,2,2,128]{3,2,1,0:T(2,128)S(1)}, f32[2,2,2,128]{3,2,1,0:T(2,128)S(1)}, u32[]{:S(2)}, u32[]{:S(2)}) collective-permute-start(f32[2,2,2,128]{3,2,1,0:T(2,128)S(1)} %get-tuple-element.54.refs_3_), channel_id=1, source_target_pairs={{0,128},{128,0},{1,129},{129,1},{2,130},{130,2},{3,131},{131,3},{4... | collective-permute-start | bytes 12296 | tf_op jit(solution)/shard_map/ppermute | solution.py:43
  53.3 4.0 %collective-permute-start.4 = (bf16[256,2048]{1,0:T(8,128)(2,1)}, bf16[256,2048]{1,0:T(8,128)(2,1)}, u32[]{:S(2)}, u32[]{:S(2)}) collective-permute-start(bf16[256,2048]{1,0:T(8,128)(2,1)} %bitcast.3.refs_1_), channel_id=1, source_target_pairs={{0,16},{16,0},{1,17},{17,1},{2,18},{18,2},{3,19},{19,3},{4,20},{20... | collective-permute-start | bytes 3145736 | tf_op jit(solution)/shard_map/ppermute | solution.py:43
  58.9 2.2 %halves.1 = (bf16[128,2048]{1,0:T(8,128)(2,1)}, bf16[128,2048]{1,0:T(8,128)(2,1)}, bf16[256,2048]{1,0:T(8,128)(2,1)}, bf16[256,2048]{1,0:T(8,128)(2,1)}) custom-call(f32[2,2,2,128]{3,2,1,0:T(2,128)} %copy-done.28, bf16[256,2048]{1,0:T(8,128)(2,1)} %copy-done.2, bf16[256,2048]{1,0:T(8,128)(2,1)} %collective-permute-done.3.p1), custom_call_target="tpu_custom_call", output_to_operand_aliasing={{2}: (1, {}), {3}: (2, {})} | custom-call | flops 1 | bytes 1 | tf_op jit(solution)/shard_map/halves/pallas_call | solution.py:369
  62.0 2.7 %collective-permute-start.8 = (bf16[128,2048]{1,0:T(8,128)(2,1)}, bf16[128,2048]{1,0:T(8,128)(2,1)S(1)}, u32[]{:S(2)}, u32[]{:S(2)}) collective-permute-start(bf16[128,2048]{1,0:T(8,128)(2,1)} %get-tuple-element.61), channel_id=1, source_target_pairs={{0,96},{32,0},{64,32},{96,64},{1,97},{33,1},{65,33},{97,65},{2,98}... | collective-permute-start | bytes 1572872 | tf_op jit(solution)/shard_map/ppermute | solution.py:43
  70.0 6.4 %block_early.1 = (f32[2048,256]{1,0:T(8,128)}, f32[8,128]{1,0:T(8,128)S(1)}) custom-call(s32[1,2,2]{2,1,0:T(2,128)S(1)} %copy-done.22, s32[1,2]{1,0:T(1,128)S(1)} %copy-done.24, s32[1,4]{1,0:T(1,128)S(1)} %copy-done.26, bf16[8,256,256]{2,1,0:T(8,128)(2,1)S(1)} %get-tuple-element.55.refs_0_.refs_1_, bf16[256,2048]{1,0:T(8,128)(2,1)} %bitcast.3.refs_1_, ...), custom_call_target="tpu_custom_call" | custom-call | flops 1 | bytes 1 | tf_op jit(solution)/shard_map/block_early/pallas_call | solution.py:94
  81.3 3.1 %block_late.1 = (bf16[4,8,64,256]{3,2,1,0:T(8,128)(2,1)S(1)}, bf16[2,256,256]{2,1,0:T(8,128)(2,1)S(1)}, bf16[2,256,256]{2,1,0:T(8,128)(2,1)S(1)}, bf16[2,256,256]{2,1,0:T(8,128)(2,1)S(1)}) custom-call(s32[1,2,2]{2,1,0:T(2,128)S(1)} %copy-done.22, s32[1,2]{1,0:T(1,128)S(1)} %copy-done.24, ...), custom_call_target="tpu_custom_call", output_to_operand_aliasing={{1}: (9, {}), {2}: (10, {}), {3}: (11, {})} | custom-call | flops 1 | bytes 1 | tf_op jit(solution)/shard_map/block_late/pallas_call | solution.py:94
  87.5 5.1 %all-to-all-start.1 = ((bf16[4,8,64,256]{3,2,1,0:T(8,128)(2,1)}), bf16[4,8,64,256]{3,2,1,0:T(8,128)(2,1)}, u32[]{:S(2)}, u32[]{:S(2)}) async-start(bf16[4,8,64,256]{3,2,1,0:T(8,128)(2,1)} %copy-done.14), calls=%async_computation.1 | async-start | bytes 2097152 | tf_op jit(solution)/shard_map/all_to_all | solution.py:398
  92.6 3.9 %collective-permute-start.13 = (bf16[2,256,256]{2,1,0:T(8,128)(2,1)}, bf16[2,256,256]{2,1,0:T(8,128)(2,1)}, u32[]{:S(2)}, u32[]{:S(2)}) collective-permute-start(bf16[2,256,256]{2,1,0:T(8,128)(2,1)} %copy-done.20), channel_id=1, source_target_pairs={{0,64},{32,96},{64,0},{96,32},{1,65},{33,97},{65,1},{97,33},{2,66}... | collective-permute-start | bytes 786440 | tf_op jit(solution)/shard_map/ppermute | solution.py:43
  99.5 8.9 %prods.1 = (f32[8,256,256]{2,1,0:T(8,128)}, f32[2,2,128]{2,1,0:T(2,128)S(1)}) custom-call(s32[1,2,2]{2,1,0:T(2,128)S(1)} %copy-done.22, s32[1,2]{1,0:T(1,128)S(1)} %copy-done.24, s32[1,4]{1,0:T(1,128)S(1)} %copy-done.26, bf16[2048,1024]{1,0:T(8,128)(2,1)} %all-gather.2.cloned.1.call-done.refs_0_.refs_3_, bf16[256,2048]{1,0:T(8,128)(2,1)} %bitcast.3.refs_1_, ...), custom_call_target="tpu_custom_call" | custom-call | flops 1 | bytes 1 | tf_op jit(solution)/shard_map/prods/pallas_call | solution.py:94
  108.4 3.1 %collective-permute-start.11 = (f32[2,2,128]{2,1,0:T(2,128)S(1)}, f32[2,2,128]{2,1,0:T(2,128)S(1)}, u32[]{:S(2)}, u32[]{:S(2)}) collective-permute-start(f32[2,2,128]{2,1,0:T(2,128)S(1)} %get-tuple-element.71.refs_4_), channel_id=1, source_target_pairs={{0,128},{128,0},{1,129},{129,1},{2,130},{130,2},{3,131},{131,3},{4... | collective-permute-start | bytes 6152 | tf_op jit(solution)/shard_map/ppermute | solution.py:43
  114.1 2.3 %grads.1 = (bf16[2,256,256]{2,1,0:T(8,128)(2,1)S(1)}, bf16[2,256,256]{2,1,0:T(8,128)(2,1)S(1)}, bf16[2,256,256]{2,1,0:T(8,128)(2,1)S(1)}, bf16[2,256,256]{2,1,0:...) custom-call(s32[1,2,2]{2,1,0:T(2,128)S(1)} %copy-done.22, s32[1,2]{1,0:T(1,128)S(1)} %copy-done.24, ...), custom_call_target="tpu_custom_call" | custom-call | flops 1 | bytes 1 | tf_op jit(solution)/shard_map/grads/pallas_call | solution.py:94
  117.1 2.8 %sum_y.1 = (bf16[8,64,256]{2,1,0:T(8,128)(2,1)}, bf16[8,16,256]{2,1,0:T(8,128)(2,1)}, bf16[2,256,256]{2,1,0:T(8,128)(2,1)}, bf16[2,256,256]{2,1,0:T(8,128)(2,1)}, bf16[2,256,256]{2,1,0:T(8,128)(2,1)}) custom-call(s32[1,2,2]{2,1,0:T(2,128)} %plan.29, s32[1,2]{1,0:T(1,128)} %lengths.29, ...), custom_call_target="tpu_custom_call", output_to_operand_aliasing={{1}: (4, {}), {2}: (5, {}), {3}: (6, {}), {4}: (7, {})} | custom-call | flops 1 | bytes 1 | tf_op jit(solution)/shard_map/sum_y/pallas_call | solution.py:94
  119.9 6.4 %all-to-all-start.2 = ((bf16[8,64,256]{2,1,0:T(8,128)(2,1)}), bf16[8,64,256]{2,1,0:T(8,128)(2,1)S(1)}, u32[]{:S(2)}, u32[]{:S(2)}) async-start(bf16[8,64,256]{2,1,0:T(8,128)(2,1)} %get-tuple-element.76), calls=%async_computation.2 | async-start | bytes 524288 | tf_op jit(solution)/shard_map/all_to_all | solution.py:414
  127.8 2.5 %collective-permute-start.18 = (bf16[2,256,256]{2,1,0:T(8,128)(2,1)S(1)}, bf16[2,256,256]{2,1,0:T(8,128)(2,1)S(1)}, u32[]{:S(2)}, u32[]{:S(2)}) collective-permute-start(bf16[2,256,256]{2,1,0:T(8,128)(2,1)S(1)} %get-tuple-element.81), channel_id=1, source_target_pairs={{0,96},{32,0},{64,32},{96,64},{1,97},{33,1},{65,33},{97,65},{2,98}... | collective-permute-start | bytes 786440 | tf_op jit(solution)/shard_map/ppermute | solution.py:43
  130.3 2.9 %collective-permute-start.15 = (bf16[8,16,256]{2,1,0:T(8,128)(2,1)S(1)}, bf16[8,16,256]{2,1,0:T(8,128)(2,1)S(1)}, u32[]{:S(2)}, u32[]{:S(2)}) collective-permute-start(bf16[8,16,256]{2,1,0:T(8,128)(2,1)S(1)} %get-tuple-element.78), channel_id=1, source_target_pairs={{0,128},{128,0},{1,129},{129,1},{2,130},{130,2},{3,131},{131,3},{4... | collective-permute-start | bytes 196616 | tf_op jit(solution)/shard_map/ppermute | solution.py:43
  135.0 2.6 %collective-permute-done.17.refs_5_ = bf16[2,256,256]{2,1,0:T(8,128)(2,1)S(1)} collective-permute-done((bf16[2,256,256]{2,1,0:T(8,128)(2,1)S(1)}, bf16[2,256,256]{2,1,0:T(8,128)(2,1)S(1)}, u32[]{:S(2)}, u32[]{:S(2)}) %collective-permute-start.17) | collective-permute-done | bytes 262176 | tf_op jit(solution)/shard_map/ppermute | solution.py:43
  137.6 2.3 %collective-permute-done.18.refs_6_ = bf16[2,256,256]{2,1,0:T(8,128)(2,1)S(1)} collective-permute-done((bf16[2,256,256]{2,1,0:T(8,128)(2,1)S(1)}, bf16[2,256,256]{2,1,0:T(8,128)(2,1)S(1)}, u32[]{:S(2)}, u32[]{:S(2)}) %collective-permute-start.18) | collective-permute-done | bytes 262176 | tf_op jit(solution)/shard_map/ppermute | solution.py:43
  142.3 2.9 %collective-permute-start.20 = (bf16[2048,1024]{1,0:T(8,128)(2,1)}, bf16[2048,1024]{1,0:T(8,128)(2,1)}, u32[]{:S(2)}, u32[]{:S(2)}) collective-permute-start(bf16[2048,1024]{1,0:T(8,128)(2,1)} %get-tuple-element.93.refs_2_), channel_id=1, source_target_pairs={{0,16},{16,0},{1,17},{17,1},{2,18},{18,2},{3,19},{19,3},{4,20},{20... | collective-permute-start | bytes 12582920 | tf_op jit(solution)/shard_map/ppermute | solution.py:43
  147.2 4.4 %all-to-all-start.3 = ((f32[8,24,256]{2,1,0:T(8,128)}), f32[8,24,256]{2,1,0:T(8,128)S(1)}, u32[]{:S(2)}, u32[]{:S(2)}) async-start(f32[8,24,256]{2,1,0:T(8,128)} %get-tuple-element.82), calls=%async_computation.3 | async-start | bytes 393216 | tf_op jit(solution)/shard_map/all_to_all | solution.py:428
  155.3 7.5 %context_grad.1.refs_1_ = bf16[256,2048]{1,0:T(8,128)(2,1)} custom-call(s32[1,2,2]{2,1,0:T(2,128)S(1)} %copy-done.23, s32[1,2]{1,0:T(1,128)S(1)} %copy-done.25, s32[1,4]{1,0:T(1,128)S(1)} %copy-done.27, bf16[8,256,256]{2,1,0:T(8,128)(2,1)S(1)} %get-tuple-element.91.refs_0_, bf16[8,256,256]{2,1,0:T(8,128)(2,1)S(1)} %collective-permute-done.19.refs_1_, ...), custom_call_target="tpu_custom_call" | custom-call | flops 1 | bytes 1 | tf_op jit(solution)/shard_map/context_grad/pallas_call | solution.py:94
  (109 shorter events, 43.6 us)
Async XLA Ops:
  7.2 89.3 %all-gather.2.cloned.1.call-start = ((), (), s32[]{:S(2)}) async-start(), calls=%async_computation.4 | async-start | bytes 4456448 | tf_op jit(solution)/shard_map/all_gather | solution.py:349
  10.8 24.0 %all-to-all-start = ((bf16[8,304,256]{2,1,0:T(8,128)(2,1)}), bf16[8,304,256]{2,1,0:T(8,128)(2,1)S(1)}, u32[]{:S(2)}, u32[]{:S(2)}) async-start(bf16[8,304,256]{2,1,0:T(8,128)(2,1)} %get-tuple-element.50), calls=%async_computation | async-start | bytes 2490368 | tf_op jit(solution)/shard_map/all_to_all | solution.py:350
  17.5 39.8 %collective-permute-start.2 = (bf16[256,2048]{1,0:T(8,128)(2,1)}, bf16[256,2048]{1,0:T(8,128)(2,1)S(1)}, u32[]{:S(2)}, u32[]{:S(2)}) collective-permute-start(bf16[256,2048]{1,0:T(8,128)(2,1)} %bitcast.3.refs_1_), channel_id=1, source_target_pairs={{0,32},{32,64},{64,96},{96,0},{1,33},{33,65},{65,97},{97,1},{2,34}... | collective-permute-start | bytes 3145736 | tf_op jit(solution)/shard_map/ppermute | solution.py:43
  18.9 38.5 %collective-permute-start.3 = (bf16[256,2048]{1,0:T(8,128)(2,1)}, bf16[256,2048]{1,0:T(8,128)(2,1)}, u32[]{:S(2)}, u32[]{:S(2)}) collective-permute-start(bf16[256,2048]{1,0:T(8,128)(2,1)} %bitcast.3.refs_1_), channel_id=1, source_target_pairs={{0,96},{32,0},{64,32},{96,64},{1,97},{33,1},{65,33},{97,65},{2,98}... | collective-permute-start | bytes 3145736 | tf_op jit(solution)/shard_map/ppermute | solution.py:43
  35.4 12.9 %collective-permute-start = (bf16[8,32,256]{2,1,0:T(8,128)(2,1)S(1)}, bf16[8,32,256]{2,1,0:T(8,128)(2,1)S(1)}, u32[]{:S(2)}, u32[]{:S(2)}) collective-permute-start(bf16[8,32,256]{2,1,0:T(8,128)(2,1)S(1)} %unpack.1), channel_id=1, source_target_pairs={{0,128},{128,0},{1,129},{129,1},{2,130},{130,2},{3,131},{131,3},{4... | collective-permute-start | bytes 393224 | tf_op jit(solution)/shard_map/ppermute | solution.py:43
  50.5 6.8 %collective-permute-start.1 = (f32[2,2,2,128]{3,2,1,0:T(2,128)S(1)}, f32[2,2,2,128]{3,2,1,0:T(2,128)S(1)}, u32[]{:S(2)}, u32[]{:S(2)}) collective-permute-start(f32[2,2,2,128]{3,2,1,0:T(2,128)S(1)} %get-tuple-element.54.refs_3_), channel_id=1, source_target_pairs={{0,128},{128,0},{1,129},{129,1},{2,130},{130,2},{3,131},{131,3},{4... | collective-permute-start | bytes 12296 | tf_op jit(solution)/shard_map/ppermute | solution.py:43
  53.3 14.1 %collective-permute-start.4 = (bf16[256,2048]{1,0:T(8,128)(2,1)}, bf16[256,2048]{1,0:T(8,128)(2,1)}, u32[]{:S(2)}, u32[]{:S(2)}) collective-permute-start(bf16[256,2048]{1,0:T(8,128)(2,1)} %bitcast.3.refs_1_), channel_id=1, source_target_pairs={{0,16},{16,0},{1,17},{17,1},{2,18},{18,2},{3,19},{19,3},{4,20},{20... | collective-permute-start | bytes 3145736 | tf_op jit(solution)/shard_map/ppermute | solution.py:43
  61.1 6.2 %collective-permute-start.5 = (bf16[256,2048]{1,0:T(8,128)(2,1)}, bf16[256,2048]{1,0:T(8,128)(2,1)S(1)}, u32[]{:S(2)}, u32[]{:S(2)}) collective-permute-start(bf16[256,2048]{1,0:T(8,128)(2,1)} %get-tuple-element.56.refs_2_.refs_3_), channel_id=1, source_target_pairs={{0,16},{16,0},{1,17},{17,1},{2,18},{18,2},{3,19},{19,3},{4,20},{20... | collective-permute-start | bytes 3145736 | tf_op jit(solution)/shard_map/ppermute | solution.py:43
  61.8 5.6 %collective-permute-start.6 = (bf16[256,2048]{1,0:T(8,128)(2,1)}, bf16[256,2048]{1,0:T(8,128)(2,1)S(1)}, u32[]{:S(2)}, u32[]{:S(2)}) collective-permute-start(bf16[256,2048]{1,0:T(8,128)(2,1)} %get-tuple-element.57.refs_3_.refs_5_), channel_id=1, source_target_pairs={{0,16},{16,0},{1,17},{17,1},{2,18},{18,2},{3,19},{19,3},{4,20},{20... | collective-permute-start | bytes 3145736 | tf_op jit(solution)/shard_map/ppermute | solution.py:43
  61.9 14.5 %collective-permute-start.7 = (bf16[128,2048]{1,0:T(8,128)(2,1)}, bf16[128,2048]{1,0:T(8,128)(2,1)S(1)}, u32[]{:S(2)}, u32[]{:S(2)}) collective-permute-start(bf16[128,2048]{1,0:T(8,128)(2,1)} %get-tuple-element.60), channel_id=1, source_target_pairs={{0,32},{32,64},{64,96},{96,0},{1,33},{33,65},{65,97},{97,1},{2,34}... | collective-permute-start | bytes 1572872 | tf_op jit(solution)/shard_map/ppermute | solution.py:43
  62.0 14.5 %collective-permute-start.8 = (bf16[128,2048]{1,0:T(8,128)(2,1)}, bf16[128,2048]{1,0:T(8,128)(2,1)S(1)}, u32[]{:S(2)}, u32[]{:S(2)}) collective-permute-start(bf16[128,2048]{1,0:T(8,128)(2,1)} %get-tuple-element.61), channel_id=1, source_target_pairs={{0,96},{32,0},{64,32},{96,64},{1,97},{33,1},{65,33},{97,65},{2,98}... | collective-permute-start | bytes 1572872 | tf_op jit(solution)/shard_map/ppermute | solution.py:43
  87.5 29.6 %all-to-all-start.1 = ((bf16[4,8,64,256]{3,2,1,0:T(8,128)(2,1)}), bf16[4,8,64,256]{3,2,1,0:T(8,128)(2,1)}, u32[]{:S(2)}, u32[]{:S(2)}) async-start(bf16[4,8,64,256]{3,2,1,0:T(8,128)(2,1)} %copy-done.14), calls=%async_computation.1 | async-start | bytes 2097152 | tf_op jit(solution)/shard_map/all_to_all | solution.py:398
  92.6 24.5 %collective-permute-start.12 = (bf16[2,256,256]{2,1,0:T(8,128)(2,1)}, bf16[2,256,256]{2,1,0:T(8,128)(2,1)}, u32[]{:S(2)}, u32[]{:S(2)}) collective-permute-start(bf16[2,256,256]{2,1,0:T(8,128)(2,1)} %copy-done.19), channel_id=1, source_target_pairs={{0,32},{32,64},{64,96},{96,0},{1,33},{33,65},{65,97},{97,1},{2,34}... | collective-permute-start | bytes 786440 | tf_op jit(solution)/shard_map/ppermute | solution.py:43
  92.6 24.5 %collective-permute-start.13 = (bf16[2,256,256]{2,1,0:T(8,128)(2,1)}, bf16[2,256,256]{2,1,0:T(8,128)(2,1)}, u32[]{:S(2)}, u32[]{:S(2)}) collective-permute-start(bf16[2,256,256]{2,1,0:T(8,128)(2,1)} %copy-done.20), channel_id=1, source_target_pairs={{0,64},{32,96},{64,0},{96,32},{1,65},{33,97},{65,1},{97,33},{2,66}... | collective-permute-start | bytes 786440 | tf_op jit(solution)/shard_map/ppermute | solution.py:43
  96.4 20.7 %collective-permute-start.14 = (bf16[2,256,256]{2,1,0:T(8,128)(2,1)}, bf16[2,256,256]{2,1,0:T(8,128)(2,1)}, u32[]{:S(2)}, u32[]{:S(2)}) collective-permute-start(bf16[2,256,256]{2,1,0:T(8,128)(2,1)} %copy-done.21), channel_id=1, source_target_pairs={{0,96},{32,0},{64,32},{96,64},{1,97},{33,1},{65,33},{97,65},{2,98}... | collective-permute-start | bytes 786440 | tf_op jit(solution)/shard_map/ppermute | solution.py:43
  108.4 4.1 %collective-permute-start.11 = (f32[2,2,128]{2,1,0:T(2,128)S(1)}, f32[2,2,128]{2,1,0:T(2,128)S(1)}, u32[]{:S(2)}, u32[]{:S(2)}) collective-permute-start(f32[2,2,128]{2,1,0:T(2,128)S(1)} %get-tuple-element.71.refs_4_), channel_id=1, source_target_pairs={{0,128},{128,0},{1,129},{129,1},{2,130},{130,2},{3,131},{131,3},{4... | collective-permute-start | bytes 6152 | tf_op jit(solution)/shard_map/ppermute | solution.py:43
  119.9 20.0 %all-to-all-start.2 = ((bf16[8,64,256]{2,1,0:T(8,128)(2,1)}), bf16[8,64,256]{2,1,0:T(8,128)(2,1)S(1)}, u32[]{:S(2)}, u32[]{:S(2)}) async-start(bf16[8,64,256]{2,1,0:T(8,128)(2,1)} %get-tuple-element.76), calls=%async_computation.2 | async-start | bytes 524288 | tf_op jit(solution)/shard_map/all_to_all | solution.py:414
  126.3 8.7 %collective-permute-start.16 = (bf16[2,256,256]{2,1,0:T(8,128)(2,1)S(1)}, bf16[2,256,256]{2,1,0:T(8,128)(2,1)S(1)}, u32[]{:S(2)}, u32[]{:S(2)}) collective-permute-start(bf16[2,256,256]{2,1,0:T(8,128)(2,1)S(1)} %get-tuple-element.79), channel_id=1, source_target_pairs={{0,32},{32,64},{64,96},{96,0},{1,33},{33,65},{65,97},{97,1},{2,34}... | collective-permute-start | bytes 786440 | tf_op jit(solution)/shard_map/ppermute | solution.py:43
  127.8 9.8 %collective-permute-start.17 = (bf16[2,256,256]{2,1,0:T(8,128)(2,1)S(1)}, bf16[2,256,256]{2,1,0:T(8,128)(2,1)S(1)}, u32[]{:S(2)}, u32[]{:S(2)}) collective-permute-start(bf16[2,256,256]{2,1,0:T(8,128)(2,1)S(1)} %get-tuple-element.80), channel_id=1, source_target_pairs={{0,64},{32,96},{64,0},{96,32},{1,65},{33,97},{65,1},{97,33},{2,66}... | collective-permute-start | bytes 786440 | tf_op jit(solution)/shard_map/ppermute | solution.py:43
  127.8 12.1 %collective-permute-start.18 = (bf16[2,256,256]{2,1,0:T(8,128)(2,1)S(1)}, bf16[2,256,256]{2,1,0:T(8,128)(2,1)S(1)}, u32[]{:S(2)}, u32[]{:S(2)}) collective-permute-start(bf16[2,256,256]{2,1,0:T(8,128)(2,1)S(1)} %get-tuple-element.81), channel_id=1, source_target_pairs={{0,96},{32,0},{64,32},{96,64},{1,97},{33,1},{65,33},{97,65},{2,98}... | collective-permute-start | bytes 786440 | tf_op jit(solution)/shard_map/ppermute | solution.py:43
  130.3 4.7 %collective-permute-start.15 = (bf16[8,16,256]{2,1,0:T(8,128)(2,1)S(1)}, bf16[8,16,256]{2,1,0:T(8,128)(2,1)S(1)}, u32[]{:S(2)}, u32[]{:S(2)}) collective-permute-start(bf16[8,16,256]{2,1,0:T(8,128)(2,1)S(1)} %get-tuple-element.78), channel_id=1, source_target_pairs={{0,128},{128,0},{1,129},{129,1},{2,130},{130,2},{3,131},{131,3},{4... | collective-permute-start | bytes 196616 | tf_op jit(solution)/shard_map/ppermute | solution.py:43
  142.3 13.0 %collective-permute-start.20 = (bf16[2048,1024]{1,0:T(8,128)(2,1)}, bf16[2048,1024]{1,0:T(8,128)(2,1)}, u32[]{:S(2)}, u32[]{:S(2)}) collective-permute-start(bf16[2048,1024]{1,0:T(8,128)(2,1)} %get-tuple-element.93.refs_2_), channel_id=1, source_target_pairs={{0,16},{16,0},{1,17},{17,1},{2,18},{18,2},{3,19},{19,3},{4,20},{20... | collective-permute-start | bytes 12582920 | tf_op jit(solution)/shard_map/ppermute | solution.py:43
  147.1 6.4 %collective-permute-start.19 = (bf16[8,256,256]{2,1,0:T(8,128)(2,1)S(1)}, bf16[8,256,256]{2,1,0:T(8,128)(2,1)S(1)}, u32[]{:S(2)}, u32[]{:S(2)}) collective-permute-start(bf16[8,256,256]{2,1,0:T(8,128)(2,1)S(1)} %get-tuple-element.92), channel_id=1, source_target_pairs={{0,16},{16,0},{1,17},{17,1},{2,18},{18,2},{3,19},{19,3},{4,20},{20... | collective-permute-start | bytes 3145736 | tf_op jit(solution)/shard_map/ppermute | solution.py:43
  147.2 15.6 %all-to-all-start.3 = ((f32[8,24,256]{2,1,0:T(8,128)}), f32[8,24,256]{2,1,0:T(8,128)S(1)}, u32[]{:S(2)}, u32[]{:S(2)}) async-start(f32[8,24,256]{2,1,0:T(8,128)} %get-tuple-element.82), calls=%async_computation.3 | async-start | bytes 393216 | tf_op jit(solution)/shard_map/all_to_all | solution.py:428
  (34 other events, 249.0 us)
Sparse Core Ops, SparseCore 0:
  10.9 71.9 all-gather.1

commit v7 on v5

--- a/solution.py
+++ b/solution.py
@@ -160,7 +160,7 @@
             masked = jnp.where(visible, dot(own[n, 0:256, hs], qg_ref[0, e, :, hs], 1, 1) * SCALE, NEG)
             top = jnp.max(masked, axis=0, keepdims=True)
             p = jnp.where(visible, jnp.exp(masked - top), 0.0)
-            p_ref[n, :, hs] = p
+            p_ref[n, :, hs] = p.astype(BF)
             top_rows.append(top)
             sum_rows.append(jnp.sum(p, axis=0, keepdims=True))
         tops.append(jnp.concatenate(top_rows, axis=0))
@@ -193,7 +193,7 @@
         fac_ref[n] = factor
         for hh in range(2):
             hs = slice(hh * HD, (hh + 1) * HD)
-            pr = (p_ref[n, :, hs] * factor[hh : hh + 1, :]).astype(BF)
+            pr = (p_ref[n, :, hs].astype(F32) * factor[hh : hh + 1, :]).astype(BF)
             vg_ref[n, :, hs] = dot(pr, qg_ref[1, e, :, hs], 1, 0).astype(BF)
 
 
@@ -252,7 +252,7 @@
             hs = slice(hh * HD, (hh + 1) * HD)
             prod = dot(v[:, hs], qg_ref[1, e, :, hs], 1, 1)
             prod_ref[n, :, hs] = prod
-            pr = p_ref[n, :, hs] * fac_ref[n, hh : hh + 1, :]
+            pr = p_ref[n, :, hs].astype(F32) * fac_ref[n, hh : hh + 1, :]
             rows.append(jnp.sum(pr * prod, axis=0, keepdims=True))
         part = jnp.concatenate(rows, axis=0)
         cross[0] = cross[0] + jnp.where(one, 0.0, part)
@@ -271,7 +271,7 @@
         delta = jnp.where(one, deltas[1], deltas[0])
         for hh in range(2):
             hs = slice(hh * HD, (hh + 1) * HD)
-            pr = p_ref[n, :, hs] * fac_ref[n, hh : hh + 1, :]
+            pr = p_ref[n, :, hs].astype(F32) * fac_ref[n, hh : hh + 1, :]
             ds = (pr * (prod_ref[n, :, hs] - delta[hh : hh + 1, :])).astype(BF)
             (g0, g1, g2, g3)[step][k, :, hs] = (SCALE * dot(ds, qg_ref[0, e, :, hs], 1, 0)).astype(BF)
             qp_buf[e, :, hs] += dot(ds, own[n, 0:256, hs], 0, 0)
@@ -356,7 +356,7 @@
     unit = (8, TOK, BLOCK)
     p, tops, ex, qg = run(
         scores_kernel, "scores",
-        [(unit, F32), ((8, 2, QC), F32), ((2, 2, 2, QC), F32), ((2, 2, QC, BLOCK), BF)],
+        [(unit, BF), ((8, 2, QC), F32), ((2, 2, 2, QC), F32), ((2, 2, QC, BLOCK), BF)],
         [pay, far], 134, 4,
     )
     ex_far = shift(ex, "yh", 1)

time: 171 us -> 170 us (level)
    unnamed x50 -> x44, local copies, waits for them, and re-layouts: 10 us -> 9.44 us
where the time goes in v7:
time: 170 us; the launch traced here: 169 us
  starting transfers between devices  56 us (33%)
  Pallas kernels  49.7 us (29%)
  waiting for transfers between devices  39.6 us (23%)
  between operations  14.4 us (8%)
  local copies, waits for them, and re-layouts  9.44 us (6%)
    pallas_call x15, Pallas kernels, call(): pl.pallas_call(body, in_specs=[SMEM] * 3 + [anywhere] * (n_in + n_tie), o...  47.4 us
    ppermute x18, starting transfers between devices, shift(): return lax.ppermute(a, axis, [(i, (i + by) % n) for i in range(n)])  28.3 us
    ppermute x18, waiting for transfers between devices, shift(): return lax.ppermute(a, axis, [(i, (i + by) % n) for i in range(n)])  25 us
    all_to_all x1, waiting for transfers between devices, on_device(): pay = lax.all_to_all(pay, ring, 0, 0)  14.6 us
    unnamed x44, local copies, waits for them, and re-layouts  9.44 us
    all_to_all x1, starting transfers between devices, on_device(): pay = lax.all_to_all(pay, ring, 0, 0)  6.72 us
    all_to_all x1, starting transfers between devices, on_device(): z_out = lax.all_to_all(z_in, 'z', 0, 0)  6.31 us
    all_to_all x1, starting transfers between devices, on_device(): got = lax.all_to_all(pieces, ('yh', 'yl'), 0, 0)  5.1 us
  transfers between devices with their start and end apart: 24, of which 9 were waited for; matrix products, arithmetic and copies ran while one was open for 0% of the time, Pallas kernels for 24%

profile of v7, /device:TPU:1, one launch (start us, length us, event | category | flops | bytes accessed | tf_op | source)
XLA Modules:
  0.0 169.1 jit_solution(18007615701150978923)
XLA Ops:
  7.2 3.5 %pack.1 = (bf16[8,304,256]{2,1,0:T(8,128)(2,1)}, bf16[128,1024]{1,0:T(8,128)(2,1)}) custom-call(s32[1,2,2]{2,1,0:T(2,128)} %plan.29, s32[1,2]{1,0:T(1,128)} %lengths.29, s32[1,4]{1,0:T(1,128)} %blocks.29, bf16[256,2048]{1,0:T(8,128)(2,1)} %bitcast.9, bf16[16,2048]{1,0:T(8,128)(2,1)} %bitcast.10, bf16[16,2048]{1,0:T(8,128)(2,1)} %bitcast.11, ...), custom_call_target="tpu_custom_call" | custom-call | flops 1 | bytes 1 | tf_op jit(solution)/shard_map/pack/pallas_call | solution.py:94
  10.7 6.7 %all-to-all-start = ((bf16[8,304,256]{2,1,0:T(8,128)(2,1)}), bf16[8,304,256]{2,1,0:T(8,128)(2,1)S(1)}, u32[]{:S(2)}, u32[]{:S(2)}) async-start(bf16[8,304,256]{2,1,0:T(8,128)(2,1)} %get-tuple-element.40), calls=%async_computation | async-start | bytes 2490368 | tf_op jit(solution)/shard_map/all_to_all | solution.py:347
  20.1 14.6 %all-to-all-done.refs_0_.refs_6_ = bf16[8,304,256]{2,1,0:T(8,128)(2,1)S(1)} async-done(((bf16[8,304,256]{2,1,0:T(8,128)(2,1)}), bf16[8,304,256]{2,1,0:T(8,128)(2,1)S(1)}, u32[]{:S(2)}, u32[]{:S(2)}) %all-to-all-start) | async-done | bytes 1245216 | tf_op jit(solution)/shard_map/all_to_all | solution.py:347
  37.4 10.8 %collective-permute-done.refs_1_ = bf16[8,32,256]{2,1,0:T(8,128)(2,1)S(1)} collective-permute-done((bf16[8,32,256]{2,1,0:T(8,128)(2,1)S(1)}, bf16[8,32,256]{2,1,0:T(8,128)(2,1)S(1)}, u32[]{:S(2)}, u32[]{:S(2)}) %collective-permute-start) | collective-permute-done | bytes 131104 | tf_op jit(solution)/shard_map/ppermute | solution.py:43
  50.5 2.8 %collective-permute-start.1 = (f32[2,2,2,128]{3,2,1,0:T(2,128)S(1)}, f32[2,2,2,128]{3,2,1,0:T(2,128)S(1)}, u32[]{:S(2)}, u32[]{:S(2)}) collective-permute-start(f32[2,2,2,128]{3,2,1,0:T(2,128)S(1)} %get-tuple-element.44.refs_3_), channel_id=1, source_target_pairs={{0,128},{128,0},{1,129},{129,1},{2,130},{130,2},{3,131},{131,3},{4... | collective-permute-start | bytes 12296 | tf_op jit(solution)/shard_map/ppermute | solution.py:43
  53.3 4.0 %collective-permute-start.4 = (bf16[256,2048]{1,0:T(8,128)(2,1)}, bf16[256,2048]{1,0:T(8,128)(2,1)}, u32[]{:S(2)}, u32[]{:S(2)}) collective-permute-start(bf16[256,2048]{1,0:T(8,128)(2,1)} %bitcast.3.refs_1_), channel_id=1, source_target_pairs={{0,16},{16,0},{1,17},{17,1},{2,18},{18,2},{3,19},{19,3},{4,20},{20... | collective-permute-start | bytes 3145736 | tf_op jit(solution)/shard_map/ppermute | solution.py:43
  58.9 2.3 %halves.1 = (bf16[128,2048]{1,0:T(8,128)(2,1)}, bf16[128,2048]{1,0:T(8,128)(2,1)}, bf16[256,2048]{1,0:T(8,128)(2,1)}, bf16[256,2048]{1,0:T(8,128)(2,1)}) custom-call(f32[2,2,2,128]{3,2,1,0:T(2,128)} %copy-done.20, bf16[256,2048]{1,0:T(8,128)(2,1)} %copy-done.2, bf16[256,2048]{1,0:T(8,128)(2,1)} %collective-permute-done.3.p1), custom_call_target="tpu_custom_call", output_to_operand_aliasing={{2}: (1, {}), {3}: (2, {})} | custom-call | flops 1 | bytes 1 | tf_op jit(solution)/shard_map/halves/pallas_call | solution.py:366
  62.0 2.7 %collective-permute-start.8 = (bf16[128,2048]{1,0:T(8,128)(2,1)}, bf16[128,2048]{1,0:T(8,128)(2,1)}, u32[]{:S(2)}, u32[]{:S(2)}) collective-permute-start(bf16[128,2048]{1,0:T(8,128)(2,1)} %get-tuple-element.51), channel_id=1, source_target_pairs={{0,96},{32,0},{64,32},{96,64},{1,97},{33,1},{65,33},{97,65},{2,98}... | collective-permute-start | bytes 1572872 | tf_op jit(solution)/shard_map/ppermute | solution.py:43
  68.2 5.1 %all-to-all-start.2 = ((bf16[8,256,256]{2,1,0:T(8,128)(2,1)}), bf16[8,256,256]{2,1,0:T(8,128)(2,1)}, u32[]{:S(2)}, u32[]{:S(2)}) async-start(bf16[8,256,256]{2,1,0:T(8,128)(2,1)} %copy-done.4), calls=%async_computation.2 | async-start | bytes 2097152 | tf_op jit(solution)/shard_map/all_to_all | solution.py:384
  74.6 6.5 %block_early.1 = (f32[2048,256]{1,0:T(8,128)}, f32[8,128]{1,0:T(8,128)S(1)}) custom-call(s32[1,2,2]{2,1,0:T(2,128)S(1)} %copy-done.14, s32[1,2]{1,0:T(1,128)S(1)} %copy-done.16, s32[1,4]{1,0:T(1,128)S(1)} %copy-done.18, bf16[8,256,256]{2,1,0:T(8,128)(2,1)S(1)} %copy-done.5, bf16[256,2048]{1,0:T(8,128)(2,1)} %bitcast.3.refs_1_, ...), custom_call_target="tpu_custom_call" | custom-call | flops 1 | bytes 1 | tf_op jit(solution)/shard_map/block_early/pallas_call | solution.py:94
  85.3 4.4 %block_late.1 = bf16[4,8,64,256]{3,2,1,0:T(8,128)(2,1)} custom-call(s32[1,2,2]{2,1,0:T(2,128)S(1)} %copy-done.14, s32[1,2]{1,0:T(1,128)S(1)} %copy-done.16, s32[1,4]{1,0:T(1,128)S(1)} %copy-done.18, f32[2048,256]{1,0:T(8,128)} %get-tuple-element.48.refs_0_, bf16[8,256,256]{2,1,0:T(8,128)(2,1)S(1)} %copy-done.6, ...), custom_call_target="tpu_custom_call" | custom-call | flops 1 | bytes 1 | tf_op jit(solution)/shard_map/block_late/pallas_call | solution.py:94
  89.7 5.1 %all-to-all-start.1 = ((bf16[4,8,64,256]{3,2,1,0:T(8,128)(2,1)}), bf16[4,8,64,256]{3,2,1,0:T(8,128)(2,1)}, u32[]{:S(2)}, u32[]{:S(2)}) async-start(bf16[4,8,64,256]{3,2,1,0:T(8,128)(2,1)} %block_late.1), calls=%async_computation.1 | async-start | bytes 2097152 | tf_op jit(solution)/shard_map/all_to_all | solution.py:395
  94.8 9.5 %prods.1 = (f32[8,256,256]{2,1,0:T(8,128)}, f32[2,2,128]{2,1,0:T(2,128)S(1)}, bf16[8,256,256]{2,1,0:T(8,128)(2,1)}) custom-call(s32[1,2,2]{2,1,0:T(2,128)S(1)} %copy-done.14, s32[1,2]{1,0:T(1,128)S(1)} %copy-done.16, s32[1,4]{1,0:T(1,128)S(1)} %copy-done.18, ...), custom_call_target="tpu_custom_call", output_to_operand_aliasing={{2}: (17, {})} | custom-call | flops 1 | bytes 1 | tf_op jit(solution)/shard_map/prods/pallas_call | solution.py:94
  104.3 3.1 %collective-permute-start.11 = (f32[2,2,128]{2,1,0:T(2,128)S(1)}, f32[2,2,128]{2,1,0:T(2,128)S(1)}, u32[]{:S(2)}, u32[]{:S(2)}) collective-permute-start(f32[2,2,128]{2,1,0:T(2,128)S(1)} %get-tuple-element.57.refs_4_), channel_id=1, source_target_pairs={{0,128},{128,0},{1,129},{129,1},{2,130},{130,2},{3,131},{131,3},{4... | collective-permute-start | bytes 6152 | tf_op jit(solution)/shard_map/ppermute | solution.py:43
  111.3 2.3 %grads.1 = (bf16[2,256,256]{2,1,0:T(8,128)(2,1)S(1)}, bf16[2,256,256]{2,1,0:T(8,128)(2,1)S(1)}, bf16[2,256,256]{2,1,0:T(8,128)(2,1)S(1)}, bf16[2,256,256]{2,1,0:...) custom-call(s32[1,2,2]{2,1,0:T(2,128)S(1)} %copy-done.14, s32[1,2]{1,0:T(1,128)S(1)} %copy-done.16, ...), custom_call_target="tpu_custom_call" | custom-call | flops 1 | bytes 1 | tf_op jit(solution)/shard_map/grads/pallas_call | solution.py:94
  114.3 2.8 %sum_y.1 = (bf16[8,64,256]{2,1,0:T(8,128)(2,1)}, bf16[8,16,256]{2,1,0:T(8,128)(2,1)}) custom-call(s32[1,2,2]{2,1,0:T(2,128)} %plan.29, s32[1,2]{1,0:T(1,128)} %lengths.29, s32[1,4]{1,0:T(1,128)} %blocks.29, bf16[4,8,64,256]{3,2,1,0:T(8,128)(2,1)} %all-to-all-done.1.refs_0_, bf16[8,16,256]{2,1,0:T(8,128)(2,1)} %copy-done.12), custom_call_target="tpu_custom_call", output_to_operand_aliasing={{1}: (4, {})} | custom-call | flops 1 | bytes 1 | tf_op jit(solution)/shard_map/sum_y/pallas_call | solution.py:94
  117.0 6.3 %all-to-all-start.3 = ((bf16[8,64,256]{2,1,0:T(8,128)(2,1)}), bf16[8,64,256]{2,1,0:T(8,128)(2,1)S(1)}, u32[]{:S(2)}, u32[]{:S(2)}) async-start(bf16[8,64,256]{2,1,0:T(8,128)(2,1)} %get-tuple-element.59), calls=%async_computation.3 | async-start | bytes 524288 | tf_op jit(solution)/shard_map/all_to_all | solution.py:411
  124.6 2.4 %collective-permute-start.14 = (bf16[2,256,256]{2,1,0:T(8,128)(2,1)S(1)}, bf16[2,256,256]{2,1,0:T(8,128)(2,1)S(1)}, u32[]{:S(2)}, u32[]{:S(2)}) collective-permute-start(bf16[2,256,256]{2,1,0:T(8,128)(2,1)S(1)} %get-tuple-element.63), channel_id=1, source_target_pairs={{0,64},{32,96},{64,0},{96,32},{1,65},{33,97},{65,1},{97,33},{2,66}... | collective-permute-start | bytes 786440 | tf_op jit(solution)/shard_map/ppermute | solution.py:43
  130.1 2.7 %collective-permute-done.12.refs_2_ = bf16[8,16,256]{2,1,0:T(8,128)(2,1)S(1)} collective-permute-done((bf16[8,16,256]{2,1,0:T(8,128)(2,1)S(1)}, bf16[8,16,256]{2,1,0:T(8,128)(2,1)S(1)}, u32[]{:S(2)}, u32[]{:S(2)}) %collective-permute-start.12) | collective-permute-done | bytes 65568 | tf_op jit(solution)/shard_map/ppermute | solution.py:43
  132.8 4.5 %collective-permute-done.14.refs_5_ = bf16[2,256,256]{2,1,0:T(8,128)(2,1)S(1)} collective-permute-done((bf16[2,256,256]{2,1,0:T(8,128)(2,1)S(1)}, bf16[2,256,256]{2,1,0:T(8,128)(2,1)S(1)}, u32[]{:S(2)}, u32[]{:S(2)}) %collective-permute-start.14) | collective-permute-done | bytes 262176 | tf_op jit(solution)/shard_map/ppermute | solution.py:43
  139.7 2.7 %collective-permute-start.16 = (bf16[2048,1024]{1,0:T(8,128)(2,1)}, bf16[2048,1024]{1,0:T(8,128)(2,1)}, u32[]{:S(2)}, u32[]{:S(2)}) collective-permute-start(bf16[2048,1024]{1,0:T(8,128)(2,1)} %get-tuple-element.67.refs_1_), channel_id=1, source_target_pairs={{0,16},{16,0},{1,17},{17,1},{2,18},{18,2},{3,19},{19,3},{4,20},{20... | collective-permute-start | bytes 12582920 | tf_op jit(solution)/shard_map/ppermute | solution.py:43
  143.3 4.4 %all-to-all-start.4 = ((f32[8,24,256]{2,1,0:T(8,128)}), f32[8,24,256]{2,1,0:T(8,128)S(1)}, u32[]{:S(2)}, u32[]{:S(2)}) async-start(f32[8,24,256]{2,1,0:T(8,128)} %get-tuple-element.65), calls=%async_computation.4 | async-start | bytes 393216 | tf_op jit(solution)/shard_map/all_to_all | solution.py:423
  147.7 2.3 %collective-permute-done.17.refs_1_ = bf16[4,256,256]{2,1,0:T(8,128)(2,1)S(1)} collective-permute-done((bf16[4,256,256]{2,1,0:T(8,128)(2,1)S(1)}, bf16[4,256,256]{2,1,0:T(8,128)(2,1)S(1)}, u32[]{:S(2)}, u32[]{:S(2)}) %collective-permute-start.17) | collective-permute-done | bytes 524320 | tf_op jit(solution)/shard_map/ppermute | solution.py:43
  151.8 7.7 %context_grad.1.refs_1_ = bf16[256,2048]{1,0:T(8,128)(2,1)} custom-call(s32[1,2,2]{2,1,0:T(2,128)S(1)} %copy-done.15, s32[1,2]{1,0:T(1,128)S(1)} %copy-done.17, s32[1,4]{1,0:T(1,128)S(1)} %copy-done.19, bf16[8,256,256]{2,1,0:T(8,128)(2,1)} %get-tuple-element.66.refs_0_, bf16[2048,1024]{1,0:T(8,128)(2,1)} %get-tuple-element.67.refs_1_, ...), custom_call_target="tpu_custom_call" | custom-call | flops 1 | bytes 1 | tf_op jit(solution)/shard_map/context_grad/pallas_call | solution.py:94
  (85 shorter events, 35.6 us)
Async XLA Ops:
  7.2 87.6 %all-gather.2.cloned.1.call-start = ((), (), s32[]{:S(2)}) async-start(), calls=%async_computation.5 | async-start | bytes 4456448 | tf_op jit(solution)/shard_map/all_gather | solution.py:346
  10.7 24.0 %all-to-all-start = ((bf16[8,304,256]{2,1,0:T(8,128)(2,1)}), bf16[8,304,256]{2,1,0:T(8,128)(2,1)S(1)}, u32[]{:S(2)}, u32[]{:S(2)}) async-start(bf16[8,304,256]{2,1,0:T(8,128)(2,1)} %get-tuple-element.40), calls=%async_computation | async-start | bytes 2490368 | tf_op jit(solution)/shard_map/all_to_all | solution.py:347
  17.5 39.9 %collective-permute-start.2 = (bf16[256,2048]{1,0:T(8,128)(2,1)}, bf16[256,2048]{1,0:T(8,128)(2,1)S(1)}, u32[]{:S(2)}, u32[]{:S(2)}) collective-permute-start(bf16[256,2048]{1,0:T(8,128)(2,1)} %bitcast.3.refs_1_), channel_id=1, source_target_pairs={{0,32},{32,64},{64,96},{96,0},{1,33},{33,65},{65,97},{97,1},{2,34}... | collective-permute-start | bytes 3145736 | tf_op jit(solution)/shard_map/ppermute | solution.py:43
  18.9 38.5 %collective-permute-start.3 = (bf16[256,2048]{1,0:T(8,128)(2,1)}, bf16[256,2048]{1,0:T(8,128)(2,1)}, u32[]{:S(2)}, u32[]{:S(2)}) collective-permute-start(bf16[256,2048]{1,0:T(8,128)(2,1)} %bitcast.3.refs_1_), channel_id=1, source_target_pairs={{0,96},{32,0},{64,32},{96,64},{1,97},{33,1},{65,33},{97,65},{2,98}... | collective-permute-start | bytes 3145736 | tf_op jit(solution)/shard_map/ppermute | solution.py:43
  35.4 12.9 %collective-permute-start = (bf16[8,32,256]{2,1,0:T(8,128)(2,1)S(1)}, bf16[8,32,256]{2,1,0:T(8,128)(2,1)S(1)}, u32[]{:S(2)}, u32[]{:S(2)}) collective-permute-start(bf16[8,32,256]{2,1,0:T(8,128)(2,1)S(1)} %unpack.1), channel_id=1, source_target_pairs={{0,128},{128,0},{1,129},{129,1},{2,130},{130,2},{3,131},{131,3},{4... | collective-permute-start | bytes 393224 | tf_op jit(solution)/shard_map/ppermute | solution.py:43
  50.5 6.8 %collective-permute-start.1 = (f32[2,2,2,128]{3,2,1,0:T(2,128)S(1)}, f32[2,2,2,128]{3,2,1,0:T(2,128)S(1)}, u32[]{:S(2)}, u32[]{:S(2)}) collective-permute-start(f32[2,2,2,128]{3,2,1,0:T(2,128)S(1)} %get-tuple-element.44.refs_3_), channel_id=1, source_target_pairs={{0,128},{128,0},{1,129},{129,1},{2,130},{130,2},{3,131},{131,3},{4... | collective-permute-start | bytes 12296 | tf_op jit(solution)/shard_map/ppermute | solution.py:43
  53.3 20.1 %collective-permute-start.4 = (bf16[256,2048]{1,0:T(8,128)(2,1)}, bf16[256,2048]{1,0:T(8,128)(2,1)}, u32[]{:S(2)}, u32[]{:S(2)}) collective-permute-start(bf16[256,2048]{1,0:T(8,128)(2,1)} %bitcast.3.refs_1_), channel_id=1, source_target_pairs={{0,16},{16,0},{1,17},{17,1},{2,18},{18,2},{3,19},{19,3},{4,20},{20... | collective-permute-start | bytes 3145736 | tf_op jit(solution)/shard_map/ppermute | solution.py:43
  61.2 12.2 %collective-permute-start.5 = (bf16[256,2048]{1,0:T(8,128)(2,1)}, bf16[256,2048]{1,0:T(8,128)(2,1)}, u32[]{:S(2)}, u32[]{:S(2)}) collective-permute-start(bf16[256,2048]{1,0:T(8,128)(2,1)} %get-tuple-element.46.refs_2_.refs_3_), channel_id=1, source_target_pairs={{0,16},{16,0},{1,17},{17,1},{2,18},{18,2},{3,19},{19,3},{4,20},{20... | collective-permute-start | bytes 3145736 | tf_op jit(solution)/shard_map/ppermute | solution.py:43
  61.9 11.5 %collective-permute-start.6 = (bf16[256,2048]{1,0:T(8,128)(2,1)}, bf16[256,2048]{1,0:T(8,128)(2,1)}, u32[]{:S(2)}, u32[]{:S(2)}) collective-permute-start(bf16[256,2048]{1,0:T(8,128)(2,1)} %get-tuple-element.47.refs_3_.refs_5_), channel_id=1, source_target_pairs={{0,16},{16,0},{1,17},{17,1},{2,18},{18,2},{3,19},{19,3},{4,20},{20... | collective-permute-start | bytes 3145736 | tf_op jit(solution)/shard_map/ppermute | solution.py:43
  62.0 19.1 %collective-permute-start.7 = (bf16[128,2048]{1,0:T(8,128)(2,1)}, bf16[128,2048]{1,0:T(8,128)(2,1)}, u32[]{:S(2)}, u32[]{:S(2)}) collective-permute-start(bf16[128,2048]{1,0:T(8,128)(2,1)} %get-tuple-element.50), channel_id=1, source_target_pairs={{0,32},{32,64},{64,96},{96,0},{1,33},{33,65},{65,97},{97,1},{2,34}... | collective-permute-start | bytes 1572872 | tf_op jit(solution)/shard_map/ppermute | solution.py:43
  62.0 19.1 %collective-permute-start.8 = (bf16[128,2048]{1,0:T(8,128)(2,1)}, bf16[128,2048]{1,0:T(8,128)(2,1)}, u32[]{:S(2)}, u32[]{:S(2)}) collective-permute-start(bf16[128,2048]{1,0:T(8,128)(2,1)} %get-tuple-element.51), channel_id=1, source_target_pairs={{0,96},{32,0},{64,32},{96,64},{1,97},{33,1},{65,33},{97,65},{2,98}... | collective-permute-start | bytes 1572872 | tf_op jit(solution)/shard_map/ppermute | solution.py:43
  68.2 21.5 %all-to-all-start.2 = ((bf16[8,256,256]{2,1,0:T(8,128)(2,1)}), bf16[8,256,256]{2,1,0:T(8,128)(2,1)}, u32[]{:S(2)}, u32[]{:S(2)}) async-start(bf16[8,256,256]{2,1,0:T(8,128)(2,1)} %copy-done.4), calls=%async_computation.2 | async-start | bytes 2097152 | tf_op jit(solution)/shard_map/all_to_all | solution.py:384
  82.3 2.2 %collective-permute-start.9 = (bf16[128,2048]{1,0:T(8,128)(2,1)}, bf16[128,2048]{1,0:T(8,128)(2,1)S(1)}, u32[]{:S(2)}, u32[]{:S(2)}) collective-permute-start(bf16[128,2048]{1,0:T(8,128)(2,1)} %get-tuple-element.52.refs_2_.refs_7_), channel_id=1, source_target_pairs={{0,16},{16,0},{1,17},{17,1},{2,18},{18,2},{3,19},{19,3},{4,20},{20... | collective-permute-start | bytes 1572872 | tf_op jit(solution)/shard_map/ppermute | solution.py:43
  82.6 2.7 %collective-permute-start.10 = (bf16[128,2048]{1,0:T(8,128)(2,1)}, bf16[128,2048]{1,0:T(8,128)(2,1)S(1)}, u32[]{:S(2)}, u32[]{:S(2)}) collective-permute-start(bf16[128,2048]{1,0:T(8,128)(2,1)} %get-tuple-element.53.refs_3_.refs_8_), channel_id=1, source_target_pairs={{0,16},{16,0},{1,17},{17,1},{2,18},{18,2},{3,19},{19,3},{4,20},{20... | collective-permute-start | bytes 1572872 | tf_op jit(solution)/shard_map/ppermute | solution.py:43
  89.7 24.6 %all-to-all-start.1 = ((bf16[4,8,64,256]{3,2,1,0:T(8,128)(2,1)}), bf16[4,8,64,256]{3,2,1,0:T(8,128)(2,1)}, u32[]{:S(2)}, u32[]{:S(2)}) async-start(bf16[4,8,64,256]{3,2,1,0:T(8,128)(2,1)} %block_late.1), calls=%async_computation.1 | async-start | bytes 2097152 | tf_op jit(solution)/shard_map/all_to_all | solution.py:395
  104.3 5.4 %collective-permute-start.11 = (f32[2,2,128]{2,1,0:T(2,128)S(1)}, f32[2,2,128]{2,1,0:T(2,128)S(1)}, u32[]{:S(2)}, u32[]{:S(2)}) collective-permute-start(f32[2,2,128]{2,1,0:T(2,128)S(1)} %get-tuple-element.57.refs_4_), channel_id=1, source_target_pairs={{0,128},{128,0},{1,129},{129,1},{2,130},{130,2},{3,131},{131,3},{4... | collective-permute-start | bytes 6152 | tf_op jit(solution)/shard_map/ppermute | solution.py:43
  117.0 20.3 %all-to-all-start.3 = ((bf16[8,64,256]{2,1,0:T(8,128)(2,1)}), bf16[8,64,256]{2,1,0:T(8,128)(2,1)S(1)}, u32[]{:S(2)}, u32[]{:S(2)}) async-start(bf16[8,64,256]{2,1,0:T(8,128)(2,1)} %get-tuple-element.59), calls=%async_computation.3 | async-start | bytes 524288 | tf_op jit(solution)/shard_map/all_to_all | solution.py:411
  123.3 9.4 %collective-permute-start.13 = (bf16[2,256,256]{2,1,0:T(8,128)(2,1)S(1)}, bf16[2,256,256]{2,1,0:T(8,128)(2,1)S(1)}, u32[]{:S(2)}, u32[]{:S(2)}) collective-permute-start(bf16[2,256,256]{2,1,0:T(8,128)(2,1)S(1)} %get-tuple-element.62), channel_id=1, source_target_pairs={{0,32},{32,64},{64,96},{96,0},{1,33},{33,65},{65,97},{97,1},{2,34}... | collective-permute-start | bytes 786440 | tf_op jit(solution)/shard_map/ppermute | solution.py:43
  124.6 12.6 %collective-permute-start.14 = (bf16[2,256,256]{2,1,0:T(8,128)(2,1)S(1)}, bf16[2,256,256]{2,1,0:T(8,128)(2,1)S(1)}, u32[]{:S(2)}, u32[]{:S(2)}) collective-permute-start(bf16[2,256,256]{2,1,0:T(8,128)(2,1)S(1)} %get-tuple-element.63), channel_id=1, source_target_pairs={{0,64},{32,96},{64,0},{96,32},{1,65},{33,97},{65,1},{97,33},{2,66}... | collective-permute-start | bytes 786440 | tf_op jit(solution)/shard_map/ppermute | solution.py:43
  127.0 10.3 %collective-permute-start.15 = (bf16[2,256,256]{2,1,0:T(8,128)(2,1)S(1)}, bf16[2,256,256]{2,1,0:T(8,128)(2,1)S(1)}, u32[]{:S(2)}, u32[]{:S(2)}) collective-permute-start(bf16[2,256,256]{2,1,0:T(8,128)(2,1)S(1)} %get-tuple-element.64), channel_id=1, source_target_pairs={{0,96},{32,0},{64,32},{96,64},{1,97},{33,1},{65,33},{97,65},{2,98}... | collective-permute-start | bytes 786440 | tf_op jit(solution)/shard_map/ppermute | solution.py:43
  128.2 4.6 %collective-permute-start.12 = (bf16[8,16,256]{2,1,0:T(8,128)(2,1)S(1)}, bf16[8,16,256]{2,1,0:T(8,128)(2,1)S(1)}, u32[]{:S(2)}, u32[]{:S(2)}) collective-permute-start(bf16[8,16,256]{2,1,0:T(8,128)(2,1)S(1)} %get-tuple-element.61), channel_id=1, source_target_pairs={{0,128},{128,0},{1,129},{129,1},{2,130},{130,2},{3,131},{131,3},{4... | collective-permute-start | bytes 196616 | tf_op jit(solution)/shard_map/ppermute | solution.py:43
  139.7 12.1 %collective-permute-start.16 = (bf16[2048,1024]{1,0:T(8,128)(2,1)}, bf16[2048,1024]{1,0:T(8,128)(2,1)}, u32[]{:S(2)}, u32[]{:S(2)}) collective-permute-start(bf16[2048,1024]{1,0:T(8,128)(2,1)} %get-tuple-element.67.refs_1_), channel_id=1, source_target_pairs={{0,16},{16,0},{1,17},{17,1},{2,18},{18,2},{3,19},{19,3},{4,20},{20... | collective-permute-start | bytes 12582920 | tf_op jit(solution)/shard_map/ppermute | solution.py:43
  143.2 6.8 %collective-permute-start.17 = (bf16[4,256,256]{2,1,0:T(8,128)(2,1)S(1)}, bf16[4,256,256]{2,1,0:T(8,128)(2,1)S(1)}, u32[]{:S(2)}, u32[]{:S(2)}) collective-permute-start(bf16[4,256,256]{2,1,0:T(8,128)(2,1)S(1)} %get-tuple-element.73), channel_id=1, source_target_pairs={{0,16},{16,0},{1,17},{17,1},{2,18},{18,2},{3,19},{19,3},{4,20},{20... | collective-permute-start | bytes 1572872 | tf_op jit(solution)/shard_map/ppermute | solution.py:43
  143.3 16.2 %all-to-all-start.4 = ((f32[8,24,256]{2,1,0:T(8,128)}), f32[8,24,256]{2,1,0:T(8,128)S(1)}, u32[]{:S(2)}, u32[]{:S(2)}) async-start(f32[8,24,256]{2,1,0:T(8,128)} %get-tuple-element.65), calls=%async_computation.4 | async-start | bytes 393216 | tf_op jit(solution)/shard_map/all_to_all | solution.py:423
  (22 other events, 238.4 us)
Sparse Core Ops, SparseCore 0:
  10.9 71.9 all-gather.1

commit v8 on v7

--- a/solution.py
+++ b/solution.py
@@ -292,7 +292,7 @@
             out_ref[:, pl.ds(pl.multiple_of(at, BLOCK), BLOCK)] = part[step]
 
 
-def join_kernel(info, got_ref, q0, q1, out_ref):
+def join_kernel(info, got_ref, q0, q1, after, out_ref):
     total = jnp.zeros((64, BLOCK), F32)
     for n in range(8):
         total = total + got_ref[n].astype(F32)
@@ -301,7 +301,7 @@
         out_ref[j, 8:24, :] = q0[j].astype(F32) + q1[j].astype(F32)
 
 
-def finish_kernel(info, got_ref, after, after_too, w_ref, q_ref):
+def finish_kernel(info, got_ref, after, w_ref, q_ref):
     for j in range(8):
         cols = slice(j * BLOCK, (j + 1) * BLOCK)
         w_ref[:, cols] = got_ref[j, 0:8, :]
@@ -405,14 +405,17 @@
         grads_kernel, "grads", [((2, TOK, BLOCK), BF)] * 4 + [((8, 16, BLOCK), BF)] * 2,
         [qg, p, fac, prods, cross, shift(cross, "yh", 1), pay], 270, 6, [((2, QC, BLOCK), F32)],
     )
-    z_in, q_own = run(
-        sum_y_kernel, "sum_y", [((8, 64, BLOCK), BF)], [got], 1, 2, ties=[q_own], megabytes=60,
+    z_in, q_own, w_own = run(
+        sum_y_kernel, "sum_y", [((8, 64, BLOCK), BF)], [got], 1, 2, ties=[q_own, w_own], megabytes=60,
     )
     z_out = lax.all_to_all(z_in, "z", 0, 0)
     g_far = [shift(g_1, "x", 1), shift(g_2, "x", 2), shift(g_3, "x", -1)]
-    joined, w_own, *g_far = run(
-        join_kernel, "join", [((8, 24, BLOCK), F32)], [z_out, q_own, shift(q_far, "yh", 1)], 1, 1,
-        ties=[w_own, *g_far],
+    (context_grad,) = run(
+        context_kernel, "context_grad", [((TOK, WIDTH), BF)], [home, w_own, shift(w_own, "k", 1)], 2200, 10,
+    )
+    joined, *g_far = run(
+        join_kernel, "join", [((8, 24, BLOCK), F32)], [z_out, q_own, shift(q_far, "yh", 1), context_grad], 1, 1,
+        ties=g_far, picks={3: (lambda info, r: r.at[pl.ds(0, 16), pl.ds(0, 128)], (16, 128))},
     )
     keep, send = run(
         turn_kernel, "turn", [((4, TOK, BLOCK), BF)] * 2,
@@ -421,12 +424,9 @@
     (key_grad,) = run(key_kernel, "key_home", [((TOK, WIDTH), BF)], [keep, shift(send, "k", 1)], 1, 2)
 
     joined = lax.all_to_all(joined, ring, 0, 0)
-    (context_grad,) = run(
-        context_kernel, "context_grad", [((TOK, WIDTH), BF)], [home, w_own, shift(w_own, "k", 1)], 2200, 10,
-    )
     weight_grad, query_grad = run(
-        finish_kernel, "finish", [((8, WIDTH), F32), ((16, WIDTH), BF)], [joined, context_grad, key_grad], 1, 1,
-        picks={i: (lambda info, r: r.at[pl.ds(0, 16), pl.ds(0, 128)], (16, 128)) for i in (1, 2)},
+        finish_kernel, "finish", [((8, WIDTH), F32), ((16, WIDTH), BF)], [joined, key_grad], 1, 1,
+        picks={1: (lambda info, r: r.at[pl.ds(0, 16), pl.ds(0, 128)], (16, 128))},
     )
     return (query_grad[None], key_grad[None], context_grad[None], weight_grad)
 

time: 170 us -> 166 us (0.976)
  waiting for transfers between devices: 39.6 us -> 34.2 us
  local copies, waits for them, and re-layouts: 9.44 us -> 12 us
    ppermute x18, waiting for transfers between devices: 25 us -> 15.5 us  [shift(): return lax.ppermute(a, axis, [(i, (i + by) % n) for i in range(n)])]
    all_to_all x1, waiting for transfers between devices: 0.01 us -> 4.09 us  [on_device(): joined = lax.all_to_all(joined, ring, 0, 0)]
    unnamed x44 -> x46, local copies, waits for them, and re-layouts: 9.44 us -> 12 us
  transfers between devices with their start and end apart: 24 -> 24, of which waited for: 9 -> 6; matrix products, arithmetic and copies ran while one was open for 0% -> 0% of each run, Pallas kernels for 24% -> 23%
where the time goes in v8:
time: 166 us; the launch traced here: 165 us
  starting transfers between devices  55.7 us (34%)
  Pallas kernels  48.4 us (29%)
  waiting for transfers between devices  34.2 us (21%)
  between operations  14.4 us (9%)
  local copies, waits for them, and re-layouts  12 us (7%)
    pallas_call x15, Pallas kernels, call(): pl.pallas_call(body, in_specs=[SMEM] * 3 + [anywhere] * (n_in + n_tie), o...  46.1 us
    ppermute x18, starting transfers between devices, shift(): return lax.ppermute(a, axis, [(i, (i + by) % n) for i in range(n)])  29.1 us
    ppermute x18, waiting for transfers between devices, shift(): return lax.ppermute(a, axis, [(i, (i + by) % n) for i in range(n)])  15.5 us
    all_to_all x1, waiting for transfers between devices, on_device(): pay = lax.all_to_all(pay, ring, 0, 0)  14.6 us
    unnamed x46, local copies, waits for them, and re-layouts  12 us
    all_to_all x1, starting transfers between devices, on_device(): pay = lax.all_to_all(pay, ring, 0, 0)  6.72 us
    all_to_all x1, starting transfers between devices, on_device(): z_out = lax.all_to_all(z_in, 'z', 0, 0)  6.31 us
    all_to_all x1, starting transfers between devices, on_device(): got = lax.all_to_all(pieces, ('yh', 'yl'), 0, 0)  5.11 us
  transfers between devices with their start and end apart: 24, of which 6 were waited for; matrix products, arithmetic and copies ran while one was open for 0% of the time, Pallas kernels for 23%

profile of v8, /device:TPU:1, one launch (start us, length us, event | category | flops | bytes accessed | tf_op | source)
XLA Modules:
  0.0 164.7 jit_solution(4476498360773091188)
XLA Ops:
  7.2 3.5 %pack.1 = (bf16[8,304,256]{2,1,0:T(8,128)(2,1)}, bf16[128,1024]{1,0:T(8,128)(2,1)}) custom-call(s32[1,2,2]{2,1,0:T(2,128)} %plan.29, s32[1,2]{1,0:T(1,128)} %lengths.29, s32[1,4]{1,0:T(1,128)} %blocks.29, bf16[256,2048]{1,0:T(8,128)(2,1)} %bitcast.9, bf16[16,2048]{1,0:T(8,128)(2,1)} %bitcast.10, bf16[16,2048]{1,0:T(8,128)(2,1)} %bitcast.11, ...), custom_call_target="tpu_custom_call" | custom-call | flops 1 | bytes 1 | tf_op jit(solution)/shard_map/pack/pallas_call | solution.py:94
  10.8 6.7 %all-to-all-start = ((bf16[8,304,256]{2,1,0:T(8,128)(2,1)}), bf16[8,304,256]{2,1,0:T(8,128)(2,1)S(1)}, u32[]{:S(2)}, u32[]{:S(2)}) async-start(bf16[8,304,256]{2,1,0:T(8,128)(2,1)} %get-tuple-element.40), calls=%async_computation | async-start | bytes 2490368 | tf_op jit(solution)/shard_map/all_to_all | solution.py:347
  20.1 14.6 %all-to-all-done.refs_0_.refs_6_ = bf16[8,304,256]{2,1,0:T(8,128)(2,1)S(1)} async-done(((bf16[8,304,256]{2,1,0:T(8,128)(2,1)}), bf16[8,304,256]{2,1,0:T(8,128)(2,1)S(1)}, u32[]{:S(2)}, u32[]{:S(2)}) %all-to-all-start) | async-done | bytes 1245216 | tf_op jit(solution)/shard_map/all_to_all | solution.py:347
  37.4 10.8 %collective-permute-done.refs_1_ = bf16[8,32,256]{2,1,0:T(8,128)(2,1)S(1)} collective-permute-done((bf16[8,32,256]{2,1,0:T(8,128)(2,1)S(1)}, bf16[8,32,256]{2,1,0:T(8,128)(2,1)S(1)}, u32[]{:S(2)}, u32[]{:S(2)}) %collective-permute-start) | collective-permute-done | bytes 131104 | tf_op jit(solution)/shard_map/ppermute | solution.py:43
  48.2 2.2 %scores.1 = (bf16[8,256,256]{2,1,0:T(8,128)(2,1)S(1)}, f32[8,2,128]{2,1,0:T(2,128)S(1)}, f32[2,2,2,128]{3,2,1,0:T(2,128)S(1)}, bf16[2,2,128,256]{3,2,1,0:T(8,128)(2,1)S(1)}) custom-call(s32[1,2,2]{2,1,0:T(2,128)S(1)} %copy-done.15, s32[1,2]{1,0:T(1,128)S(1)} %copy-done.17, s32[1,4]{1,0:T(1,128)S(1)} %copy-done.19, ...), custom_call_target="tpu_custom_call" | custom-call | flops 1 | bytes 1 | tf_op jit(solution)/shard_map/scores/pallas_call | solution.py:94
  50.5 2.8 %collective-permute-start.1 = (f32[2,2,2,128]{3,2,1,0:T(2,128)S(1)}, f32[2,2,2,128]{3,2,1,0:T(2,128)S(1)}, u32[]{:S(2)}, u32[]{:S(2)}) collective-permute-start(f32[2,2,2,128]{3,2,1,0:T(2,128)S(1)} %get-tuple-element.44.refs_3_), channel_id=1, source_target_pairs={{0,128},{128,0},{1,129},{129,1},{2,130},{130,2},{3,131},{131,3},{4... | collective-permute-start | bytes 12296 | tf_op jit(solution)/shard_map/ppermute | solution.py:43
  53.3 4.0 %collective-permute-start.4 = (bf16[256,2048]{1,0:T(8,128)(2,1)}, bf16[256,2048]{1,0:T(8,128)(2,1)}, u32[]{:S(2)}, u32[]{:S(2)}) collective-permute-start(bf16[256,2048]{1,0:T(8,128)(2,1)} %bitcast.3.refs_1_), channel_id=1, source_target_pairs={{0,16},{16,0},{1,17},{17,1},{2,18},{18,2},{3,19},{19,3},{4,20},{20... | collective-permute-start | bytes 3145736 | tf_op jit(solution)/shard_map/ppermute | solution.py:43
  58.9 2.3 %halves.1 = (bf16[128,2048]{1,0:T(8,128)(2,1)}, bf16[128,2048]{1,0:T(8,128)(2,1)}, bf16[256,2048]{1,0:T(8,128)(2,1)}, bf16[256,2048]{1,0:T(8,128)(2,1)}) custom-call(f32[2,2,2,128]{3,2,1,0:T(2,128)} %copy-done.21, bf16[256,2048]{1,0:T(8,128)(2,1)} %copy-done.3, bf16[256,2048]{1,0:T(8,128)(2,1)} %collective-permute-done.3.p1), custom_call_target="tpu_custom_call", output_to_operand_aliasing={{2}: (1, {}), {3}: (2, {})} | custom-call | flops 1 | bytes 1 | tf_op jit(solution)/shard_map/halves/pallas_call | solution.py:366
  62.0 2.7 %collective-permute-start.8 = (bf16[128,2048]{1,0:T(8,128)(2,1)}, bf16[128,2048]{1,0:T(8,128)(2,1)}, u32[]{:S(2)}, u32[]{:S(2)}) collective-permute-start(bf16[128,2048]{1,0:T(8,128)(2,1)} %get-tuple-element.51), channel_id=1, source_target_pairs={{0,96},{32,0},{64,32},{96,64},{1,97},{33,1},{65,33},{97,65},{2,98}... | collective-permute-start | bytes 1572872 | tf_op jit(solution)/shard_map/ppermute | solution.py:43
  68.2 5.1 %all-to-all-start.2 = ((bf16[8,256,256]{2,1,0:T(8,128)(2,1)}), bf16[8,256,256]{2,1,0:T(8,128)(2,1)}, u32[]{:S(2)}, u32[]{:S(2)}) async-start(bf16[8,256,256]{2,1,0:T(8,128)(2,1)} %copy-done.5), calls=%async_computation.2 | async-start | bytes 2097152 | tf_op jit(solution)/shard_map/all_to_all | solution.py:384
  74.6 6.4 %block_early.1 = (f32[2048,256]{1,0:T(8,128)}, f32[8,128]{1,0:T(8,128)S(1)}) custom-call(s32[1,2,2]{2,1,0:T(2,128)S(1)} %copy-done.15, s32[1,2]{1,0:T(1,128)S(1)} %copy-done.17, s32[1,4]{1,0:T(1,128)S(1)} %copy-done.19, bf16[8,256,256]{2,1,0:T(8,128)(2,1)S(1)} %copy-done.6, bf16[256,2048]{1,0:T(8,128)(2,1)} %bitcast.3.refs_1_, ...), custom_call_target="tpu_custom_call" | custom-call | flops 1 | bytes 1 | tf_op jit(solution)/shard_map/block_early/pallas_call | solution.py:94
  85.1 4.3 %block_late.1 = bf16[4,8,64,256]{3,2,1,0:T(8,128)(2,1)} custom-call(s32[1,2,2]{2,1,0:T(2,128)S(1)} %copy-done.15, s32[1,2]{1,0:T(1,128)S(1)} %copy-done.17, s32[1,4]{1,0:T(1,128)S(1)} %copy-done.19, f32[2048,256]{1,0:T(8,128)} %get-tuple-element.48.refs_0_, bf16[8,256,256]{2,1,0:T(8,128)(2,1)S(1)} %copy-done.7, ...), custom_call_target="tpu_custom_call" | custom-call | flops 1 | bytes 1 | tf_op jit(solution)/shard_map/block_late/pallas_call | solution.py:94
  89.4 5.1 %all-to-all-start.1 = ((bf16[4,8,64,256]{3,2,1,0:T(8,128)(2,1)}), bf16[4,8,64,256]{3,2,1,0:T(8,128)(2,1)}, u32[]{:S(2)}, u32[]{:S(2)}) async-start(bf16[4,8,64,256]{3,2,1,0:T(8,128)(2,1)} %block_late.1), calls=%async_computation.1 | async-start | bytes 2097152 | tf_op jit(solution)/shard_map/all_to_all | solution.py:395
  94.6 9.5 %prods.1 = (f32[8,256,256]{2,1,0:T(8,128)}, f32[2,2,128]{2,1,0:T(2,128)S(1)}, bf16[8,256,256]{2,1,0:T(8,128)(2,1)}) custom-call(s32[1,2,2]{2,1,0:T(2,128)S(1)} %copy-done.15, s32[1,2]{1,0:T(1,128)S(1)} %copy-done.17, s32[1,4]{1,0:T(1,128)S(1)} %copy-done.19, ...), custom_call_target="tpu_custom_call", output_to_operand_aliasing={{2}: (17, {})} | custom-call | flops 1 | bytes 1 | tf_op jit(solution)/shard_map/prods/pallas_call | solution.py:94
  104.1 3.1 %collective-permute-start.11 = (f32[2,2,128]{2,1,0:T(2,128)S(1)}, f32[2,2,128]{2,1,0:T(2,128)S(1)}, u32[]{:S(2)}, u32[]{:S(2)}) collective-permute-start(f32[2,2,128]{2,1,0:T(2,128)S(1)} %get-tuple-element.57.refs_4_), channel_id=1, source_target_pairs={{0,128},{128,0},{1,129},{129,1},{2,130},{130,2},{3,131},{131,3},{4... | collective-permute-start | bytes 6152 | tf_op jit(solution)/shard_map/ppermute | solution.py:43
  107.2 2.3 %collective-permute-done.11.refs_5_ = f32[2,2,128]{2,1,0:T(2,128)S(1)} collective-permute-done((f32[2,2,128]{2,1,0:T(2,128)S(1)}, f32[2,2,128]{2,1,0:T(2,128)S(1)}, u32[]{:S(2)}, u32[]{:S(2)}) %collective-permute-start.11) | collective-permute-done | bytes 2080 | tf_op jit(solution)/shard_map/ppermute | solution.py:43
  111.1 2.3 %grads.1 = (bf16[2,256,256]{2,1,0:T(8,128)(2,1)S(1)}, bf16[2,256,256]{2,1,0:T(8,128)(2,1)S(1)}, bf16[2,256,256]{2,1,0:T(8,128)(2,1)S(1)}, bf16[2,256,256]{2,1,0:...) custom-call(s32[1,2,2]{2,1,0:T(2,128)S(1)} %copy-done.15, s32[1,2]{1,0:T(1,128)S(1)} %copy-done.17, ...), custom_call_target="tpu_custom_call" | custom-call | flops 1 | bytes 1 | tf_op jit(solution)/shard_map/grads/pallas_call | solution.py:94
  114.0 2.9 %sum_y.1 = (bf16[8,64,256]{2,1,0:T(8,128)(2,1)}, bf16[8,16,256]{2,1,0:T(8,128)(2,1)}, bf16[2048,1024]{1,0:T(8,128)(2,1)}) custom-call(s32[1,2,2]{2,1,0:T(2,128)} %plan.29, s32[1,2]{1,0:T(1,128)} %lengths.29, s32[1,4]{1,0:T(1,128)} %blocks.29, bf16[4,8,64,256]{3,2,1,0:T(8,128)(2,1)} %all-to-all-done.1.refs_0_, ...), custom_call_target="tpu_custom_call", output_to_operand_aliasing={{1}: (4, {}), {2}: (5, {})} | custom-call | flops 1 | bytes 1 | tf_op jit(solution)/shard_map/sum_y/pallas_call | solution.py:94
  118.3 6.3 %all-to-all-start.3 = ((bf16[8,64,256]{2,1,0:T(8,128)(2,1)}), bf16[8,64,256]{2,1,0:T(8,128)(2,1)S(1)}, u32[]{:S(2)}, u32[]{:S(2)}) async-start(bf16[8,64,256]{2,1,0:T(8,128)(2,1)} %get-tuple-element.59), calls=%async_computation.3 | async-start | bytes 524288 | tf_op jit(solution)/shard_map/all_to_all | solution.py:411
  126.0 2.4 %collective-permute-start.15 = (bf16[2,256,256]{2,1,0:T(8,128)(2,1)S(1)}, bf16[2,256,256]{2,1,0:T(8,128)(2,1)S(1)}, u32[]{:S(2)}, u32[]{:S(2)}) collective-permute-start(bf16[2,256,256]{2,1,0:T(8,128)(2,1)S(1)} %get-tuple-element.65), channel_id=1, source_target_pairs={{0,64},{32,96},{64,0},{96,32},{1,65},{33,97},{65,1},{97,33},{2,66}... | collective-permute-start | bytes 786440 | tf_op jit(solution)/shard_map/ppermute | solution.py:43
  129.6 2.4 %collective-permute-start.12 = (bf16[8,16,256]{2,1,0:T(8,128)(2,1)S(1)}, bf16[8,16,256]{2,1,0:T(8,128)(2,1)S(1)}, u32[]{:S(2)}, u32[]{:S(2)}) collective-permute-start(bf16[8,16,256]{2,1,0:T(8,128)(2,1)S(1)} %get-tuple-element.61), channel_id=1, source_target_pairs={{0,128},{128,0},{1,129},{129,1},{2,130},{130,2},{3,131},{131,3},{4... | collective-permute-start | bytes 196616 | tf_op jit(solution)/shard_map/ppermute | solution.py:43
  134.3 6.5 %context_grad.1.refs_3_ = bf16[256,2048]{1,0:T(8,128)(2,1)} custom-call(s32[1,2,2]{2,1,0:T(2,128)S(1)} %copy-done.16, s32[1,2]{1,0:T(1,128)S(1)} %copy-done.18, s32[1,4]{1,0:T(1,128)S(1)} %copy-done.20, bf16[8,256,256]{2,1,0:T(8,128)(2,1)} %get-tuple-element.62.refs_0_, bf16[2048,1024]{1,0:T(8,128)(2,1)S(1)} %copy-done, ...), custom_call_target="tpu_custom_call" | custom-call | flops 1 | bytes 1 | tf_op jit(solution)/shard_map/context_grad/pallas_call | solution.py:94
  145.9 3.3 %all-to-all-start.4 = ((f32[8,24,256]{2,1,0:T(8,128)}), f32[8,24,256]{2,1,0:T(8,128)S(1)}, u32[]{:S(2)}, u32[]{:S(2)}) async-start(f32[8,24,256]{2,1,0:T(8,128)} %get-tuple-element.67), calls=%async_computation.4 | async-start | bytes 393216 | tf_op jit(solution)/shard_map/all_to_all | solution.py:426
  151.0 4.1 %all-to-all-done.4.refs_0_ = f32[8,24,256]{2,1,0:T(8,128)S(1)} async-done(((f32[8,24,256]{2,1,0:T(8,128)}), f32[8,24,256]{2,1,0:T(8,128)S(1)}, u32[]{:S(2)}, u32[]{:S(2)}) %all-to-all-start.4) | async-done | bytes 196640 | tf_op jit(solution)/shard_map/all_to_all | solution.py:426
  (87 shorter events, 34.6 us)
Async XLA Ops:
  7.2 87.4 %all-gather.2.cloned.1.call-start = ((), (), s32[]{:S(2)}) async-start(), calls=%async_computation.5 | async-start | bytes 4456448 | tf_op jit(solution)/shard_map/all_gather | solution.py:346
  10.8 24.0 %all-to-all-start = ((bf16[8,304,256]{2,1,0:T(8,128)(2,1)}), bf16[8,304,256]{2,1,0:T(8,128)(2,1)S(1)}, u32[]{:S(2)}, u32[]{:S(2)}) async-start(bf16[8,304,256]{2,1,0:T(8,128)(2,1)} %get-tuple-element.40), calls=%async_computation | async-start | bytes 2490368 | tf_op jit(solution)/shard_map/all_to_all | solution.py:347
  17.5 39.8 %collective-permute-start.2 = (bf16[256,2048]{1,0:T(8,128)(2,1)}, bf16[256,2048]{1,0:T(8,128)(2,1)S(1)}, u32[]{:S(2)}, u32[]{:S(2)}) collective-permute-start(bf16[256,2048]{1,0:T(8,128)(2,1)} %bitcast.3.refs_1_), channel_id=1, source_target_pairs={{0,32},{32,64},{64,96},{96,0},{1,33},{33,65},{65,97},{97,1},{2,34}... | collective-permute-start | bytes 3145736 | tf_op jit(solution)/shard_map/ppermute | solution.py:43
  18.9 38.5 %collective-permute-start.3 = (bf16[256,2048]{1,0:T(8,128)(2,1)}, bf16[256,2048]{1,0:T(8,128)(2,1)}, u32[]{:S(2)}, u32[]{:S(2)}) collective-permute-start(bf16[256,2048]{1,0:T(8,128)(2,1)} %bitcast.3.refs_1_), channel_id=1, source_target_pairs={{0,96},{32,0},{64,32},{96,64},{1,97},{33,1},{65,33},{97,65},{2,98}... | collective-permute-start | bytes 3145736 | tf_op jit(solution)/shard_map/ppermute | solution.py:43
  35.4 12.9 %collective-permute-start = (bf16[8,32,256]{2,1,0:T(8,128)(2,1)S(1)}, bf16[8,32,256]{2,1,0:T(8,128)(2,1)S(1)}, u32[]{:S(2)}, u32[]{:S(2)}) collective-permute-start(bf16[8,32,256]{2,1,0:T(8,128)(2,1)S(1)} %unpack.1), channel_id=1, source_target_pairs={{0,128},{128,0},{1,129},{129,1},{2,130},{130,2},{3,131},{131,3},{4... | collective-permute-start | bytes 393224 | tf_op jit(solution)/shard_map/ppermute | solution.py:43
  50.5 6.8 %collective-permute-start.1 = (f32[2,2,2,128]{3,2,1,0:T(2,128)S(1)}, f32[2,2,2,128]{3,2,1,0:T(2,128)S(1)}, u32[]{:S(2)}, u32[]{:S(2)}) collective-permute-start(f32[2,2,2,128]{3,2,1,0:T(2,128)S(1)} %get-tuple-element.44.refs_3_), channel_id=1, source_target_pairs={{0,128},{128,0},{1,129},{129,1},{2,130},{130,2},{3,131},{131,3},{4... | collective-permute-start | bytes 12296 | tf_op jit(solution)/shard_map/ppermute | solution.py:43
  53.3 20.0 %collective-permute-start.4 = (bf16[256,2048]{1,0:T(8,128)(2,1)}, bf16[256,2048]{1,0:T(8,128)(2,1)}, u32[]{:S(2)}, u32[]{:S(2)}) collective-permute-start(bf16[256,2048]{1,0:T(8,128)(2,1)} %bitcast.3.refs_1_), channel_id=1, source_target_pairs={{0,16},{16,0},{1,17},{17,1},{2,18},{18,2},{3,19},{19,3},{4,20},{20... | collective-permute-start | bytes 3145736 | tf_op jit(solution)/shard_map/ppermute | solution.py:43
  61.2 12.1 %collective-permute-start.5 = (bf16[256,2048]{1,0:T(8,128)(2,1)}, bf16[256,2048]{1,0:T(8,128)(2,1)}, u32[]{:S(2)}, u32[]{:S(2)}) collective-permute-start(bf16[256,2048]{1,0:T(8,128)(2,1)} %get-tuple-element.46.refs_2_.refs_3_), channel_id=1, source_target_pairs={{0,16},{16,0},{1,17},{17,1},{2,18},{18,2},{3,19},{19,3},{4,20},{20... | collective-permute-start | bytes 3145736 | tf_op jit(solution)/shard_map/ppermute | solution.py:43
  61.9 11.4 %collective-permute-start.6 = (bf16[256,2048]{1,0:T(8,128)(2,1)}, bf16[256,2048]{1,0:T(8,128)(2,1)}, u32[]{:S(2)}, u32[]{:S(2)}) collective-permute-start(bf16[256,2048]{1,0:T(8,128)(2,1)} %get-tuple-element.47.refs_3_.refs_5_), channel_id=1, source_target_pairs={{0,16},{16,0},{1,17},{17,1},{2,18},{18,2},{3,19},{19,3},{4,20},{20... | collective-permute-start | bytes 3145736 | tf_op jit(solution)/shard_map/ppermute | solution.py:43
  62.0 19.0 %collective-permute-start.7 = (bf16[128,2048]{1,0:T(8,128)(2,1)}, bf16[128,2048]{1,0:T(8,128)(2,1)}, u32[]{:S(2)}, u32[]{:S(2)}) collective-permute-start(bf16[128,2048]{1,0:T(8,128)(2,1)} %get-tuple-element.50), channel_id=1, source_target_pairs={{0,32},{32,64},{64,96},{96,0},{1,33},{33,65},{65,97},{97,1},{2,34}... | collective-permute-start | bytes 1572872 | tf_op jit(solution)/shard_map/ppermute | solution.py:43
  62.0 19.0 %collective-permute-start.8 = (bf16[128,2048]{1,0:T(8,128)(2,1)}, bf16[128,2048]{1,0:T(8,128)(2,1)}, u32[]{:S(2)}, u32[]{:S(2)}) collective-permute-start(bf16[128,2048]{1,0:T(8,128)(2,1)} %get-tuple-element.51), channel_id=1, source_target_pairs={{0,96},{32,0},{64,32},{96,64},{1,97},{33,1},{65,33},{97,65},{2,98}... | collective-permute-start | bytes 1572872 | tf_op jit(solution)/shard_map/ppermute | solution.py:43
  68.2 21.2 %all-to-all-start.2 = ((bf16[8,256,256]{2,1,0:T(8,128)(2,1)}), bf16[8,256,256]{2,1,0:T(8,128)(2,1)}, u32[]{:S(2)}, u32[]{:S(2)}) async-start(bf16[8,256,256]{2,1,0:T(8,128)(2,1)} %copy-done.5), calls=%async_computation.2 | async-start | bytes 2097152 | tf_op jit(solution)/shard_map/all_to_all | solution.py:384
  82.2 2.2 %collective-permute-start.9 = (bf16[128,2048]{1,0:T(8,128)(2,1)}, bf16[128,2048]{1,0:T(8,128)(2,1)S(1)}, u32[]{:S(2)}, u32[]{:S(2)}) collective-permute-start(bf16[128,2048]{1,0:T(8,128)(2,1)} %get-tuple-element.52.refs_2_.refs_7_), channel_id=1, source_target_pairs={{0,16},{16,0},{1,17},{17,1},{2,18},{18,2},{3,19},{19,3},{4,20},{20... | collective-permute-start | bytes 1572872 | tf_op jit(solution)/shard_map/ppermute | solution.py:43
  82.4 2.7 %collective-permute-start.10 = (bf16[128,2048]{1,0:T(8,128)(2,1)}, bf16[128,2048]{1,0:T(8,128)(2,1)S(1)}, u32[]{:S(2)}, u32[]{:S(2)}) collective-permute-start(bf16[128,2048]{1,0:T(8,128)(2,1)} %get-tuple-element.53.refs_3_.refs_8_), channel_id=1, source_target_pairs={{0,16},{16,0},{1,17},{17,1},{2,18},{18,2},{3,19},{19,3},{4,20},{20... | collective-permute-start | bytes 1572872 | tf_op jit(solution)/shard_map/ppermute | solution.py:43
  89.4 24.6 %all-to-all-start.1 = ((bf16[4,8,64,256]{3,2,1,0:T(8,128)(2,1)}), bf16[4,8,64,256]{3,2,1,0:T(8,128)(2,1)}, u32[]{:S(2)}, u32[]{:S(2)}) async-start(bf16[4,8,64,256]{3,2,1,0:T(8,128)(2,1)} %block_late.1), calls=%async_computation.1 | async-start | bytes 2097152 | tf_op jit(solution)/shard_map/all_to_all | solution.py:395
  104.1 5.4 %collective-permute-start.11 = (f32[2,2,128]{2,1,0:T(2,128)S(1)}, f32[2,2,128]{2,1,0:T(2,128)S(1)}, u32[]{:S(2)}, u32[]{:S(2)}) collective-permute-start(f32[2,2,128]{2,1,0:T(2,128)S(1)} %get-tuple-element.57.refs_4_), channel_id=1, source_target_pairs={{0,128},{128,0},{1,129},{129,1},{2,130},{130,2},{3,131},{131,3},{4... | collective-permute-start | bytes 6152 | tf_op jit(solution)/shard_map/ppermute | solution.py:43
  116.9 15.1 %collective-permute-start.13 = (bf16[2048,1024]{1,0:T(8,128)(2,1)}, bf16[2048,1024]{1,0:T(8,128)(2,1)}, u32[]{:S(2)}, u32[]{:S(2)}) collective-permute-start(bf16[2048,1024]{1,0:T(8,128)(2,1)} %get-tuple-element.63.refs_1_), channel_id=1, source_target_pairs={{0,16},{16,0},{1,17},{17,1},{2,18},{18,2},{3,19},{19,3},{4,20},{20... | collective-permute-start | bytes 12582920 | tf_op jit(solution)/shard_map/ppermute | solution.py:43
  118.3 22.5 %all-to-all-start.3 = ((bf16[8,64,256]{2,1,0:T(8,128)(2,1)}), bf16[8,64,256]{2,1,0:T(8,128)(2,1)S(1)}, u32[]{:S(2)}, u32[]{:S(2)}) async-start(bf16[8,64,256]{2,1,0:T(8,128)(2,1)} %get-tuple-element.59), calls=%async_computation.3 | async-start | bytes 524288 | tf_op jit(solution)/shard_map/all_to_all | solution.py:411
  124.6 16.2 %collective-permute-start.14 = (bf16[2,256,256]{2,1,0:T(8,128)(2,1)S(1)}, bf16[2,256,256]{2,1,0:T(8,128)(2,1)S(1)}, u32[]{:S(2)}, u32[]{:S(2)}) collective-permute-start(bf16[2,256,256]{2,1,0:T(8,128)(2,1)S(1)} %get-tuple-element.64), channel_id=1, source_target_pairs={{0,32},{32,64},{64,96},{96,0},{1,33},{33,65},{65,97},{97,1},{2,34}... | collective-permute-start | bytes 786440 | tf_op jit(solution)/shard_map/ppermute | solution.py:43
  126.0 14.7 %collective-permute-start.15 = (bf16[2,256,256]{2,1,0:T(8,128)(2,1)S(1)}, bf16[2,256,256]{2,1,0:T(8,128)(2,1)S(1)}, u32[]{:S(2)}, u32[]{:S(2)}) collective-permute-start(bf16[2,256,256]{2,1,0:T(8,128)(2,1)S(1)} %get-tuple-element.65), channel_id=1, source_target_pairs={{0,64},{32,96},{64,0},{96,32},{1,65},{33,97},{65,1},{97,33},{2,66}... | collective-permute-start | bytes 786440 | tf_op jit(solution)/shard_map/ppermute | solution.py:43
  128.5 12.3 %collective-permute-start.16 = (bf16[2,256,256]{2,1,0:T(8,128)(2,1)S(1)}, bf16[2,256,256]{2,1,0:T(8,128)(2,1)S(1)}, u32[]{:S(2)}, u32[]{:S(2)}) collective-permute-start(bf16[2,256,256]{2,1,0:T(8,128)(2,1)S(1)} %get-tuple-element.66), channel_id=1, source_target_pairs={{0,96},{32,0},{64,32},{96,64},{1,97},{33,1},{65,33},{97,65},{2,98}... | collective-permute-start | bytes 786440 | tf_op jit(solution)/shard_map/ppermute | solution.py:43
  129.6 11.2 %collective-permute-start.12 = (bf16[8,16,256]{2,1,0:T(8,128)(2,1)S(1)}, bf16[8,16,256]{2,1,0:T(8,128)(2,1)S(1)}, u32[]{:S(2)}, u32[]{:S(2)}) collective-permute-start(bf16[8,16,256]{2,1,0:T(8,128)(2,1)S(1)} %get-tuple-element.61), channel_id=1, source_target_pairs={{0,128},{128,0},{1,129},{129,1},{2,130},{130,2},{3,131},{131,3},{4... | collective-permute-start | bytes 196616 | tf_op jit(solution)/shard_map/ppermute | solution.py:43
  144.4 4.9 %collective-permute-start.17 = (bf16[4,256,256]{2,1,0:T(8,128)(2,1)S(1)}, bf16[4,256,256]{2,1,0:T(8,128)(2,1)S(1)}, u32[]{:S(2)}, u32[]{:S(2)}) collective-permute-start(bf16[4,256,256]{2,1,0:T(8,128)(2,1)S(1)} %get-tuple-element.73), channel_id=1, source_target_pairs={{0,16},{16,0},{1,17},{17,1},{2,18},{18,2},{3,19},{19,3},{4,20},{20... | collective-permute-start | bytes 1572872 | tf_op jit(solution)/shard_map/ppermute | solution.py:43
  145.9 9.2 %all-to-all-start.4 = ((f32[8,24,256]{2,1,0:T(8,128)}), f32[8,24,256]{2,1,0:T(8,128)S(1)}, u32[]{:S(2)}, u32[]{:S(2)}) async-start(f32[8,24,256]{2,1,0:T(8,128)} %get-tuple-element.67), calls=%async_computation.4 | async-start | bytes 393216 | tf_op jit(solution)/shard_map/all_to_all | solution.py:426
  (23 other events, 215.8 us)
Sparse Core Ops, SparseCore 0:
  10.9 71.9 all-gather.1
